TPU v7x, 32 devices: a whole 2x2x4 slice. The times are simulated.
32 devices in a mesh: fsdp: 8 (over y, x, core), ctx: 4 (over z).
Axes of the slice: x: 2, y: 2, z: 4, core: 2. Of those that a mesh axis runs over, the one named last changes fastest.
Arguments:
- tokens_in: bfloat16 [8192, 1536], P(('fsdp', 'ctx')), may hold values from -6 to 6
- block_order: int32 [8, 4], P('fsdp'), may hold values from 0 to 3, each once within a row
- norm_attn: bfloat16 [1536], P('fsdp'), may hold values from 0.099609375 to 1.8984375
- w_qkv: bfloat16 [1536, 2048], P('fsdp'), may hold values from -0.15625 to 0.15625
- b_qkv: bfloat16 [2048], P('fsdp'), may hold values from -3 to 3
- w_out: bfloat16 [1536, 1536], P('fsdp'), may hold values from -0.625 to 0.625
- norm_mlp: bfloat16 [1536], P('fsdp'), may hold values from 0.099609375 to 1.8984375
- w_gate: bfloat16 [1536, 8960], P('fsdp'), may hold values from -0.15625 to 0.15625
- w_up: bfloat16 [1536, 8960], P('fsdp'), may hold values from -0.15625 to 0.15625
- w_down: bfloat16 [8960, 1536], P('fsdp'), may hold values from -0.0625 to 0.0625
- cotangent: bfloat16 [8192, 1536], P(('fsdp', 'ctx')), may hold values from -6 to 6
Outputs:
- out_tokens: bfloat16 [8192, 1536], P(('fsdp', 'ctx'))
- grad_tokens: bfloat16 [8192, 1536], P(('fsdp', 'ctx'))
- grad_norm_attn: float32 [1536], P('fsdp')
- grad_w_qkv: float32 [1536, 2048], P('fsdp')
- grad_b_qkv: float32 [2048], P('fsdp')
- grad_w_out: float32 [1536, 1536], P('fsdp')
- grad_norm_mlp: float32 [1536], P('fsdp')
- grad_w_gate: float32 [1536, 8960], P('fsdp')
- grad_w_up: float32 [1536, 8960], P('fsdp')
- grad_w_down: float32 [8960, 1536], P('fsdp')
Inputs may be any that keep to these rules, and one draw needn't show every extreme that they name: Each row holds every block number of its sequence once: ctx index c holds block block_order[s, c], tokens block_order[s, c] * 256 to that plus 256 - 1.
All inputs are finite; a program needn't handle non-finite values.
Results may differ from a plain program's by a relative error of at most 0.02.
Values may be sent and summed in bfloat16 or wider, within the bound.
No kernel may reach another device: no remote copies, remote signals or barrier semaphores. Data moves between devices by JAX's collectives and lax.ppermute only.
A program may use at most 704 MiB of HBM per device.

v0:
```python
import jax
import jax.numpy as jnp
from jax import lax
from jax.sharding import PartitionSpec as P

HEADS = 12
KV_HEADS = 2
HEAD = 128


norm_eps = 1e-06
rope_base = 1000000.0
masked_score = -1e30


def rotary(positions, width):
    half_width = width // 2
    frequency = rope_base ** (-(jnp.arange(half_width, dtype=jnp.float32) * 2.0) / width)
    angles = positions.astype(jnp.float32)[:, None] * frequency[None, :]
    angles = jnp.concatenate([angles, angles], 1)
    return (jnp.cos(angles)[:, None, :], jnp.sin(angles)[:, None, :])


def turned(tensor):
    half_width = tensor.shape[-1] // 2
    return jnp.concatenate([-tensor[..., half_width:], tensor[..., :half_width]], -1)


def turned_back(tensor):
    half_width = tensor.shape[-1] // 2
    return jnp.concatenate([tensor[..., half_width:], -tensor[..., :half_width]], -1)


def key_positions(orders, start_row, count, block_rows):
    row_ids = start_row + jnp.arange(count, dtype=jnp.int32)
    owner_dev = row_ids // block_rows
    device_ids = jnp.arange(orders.shape[0], dtype=jnp.int32)
    chosen = jnp.sum(jnp.where(owner_dev[:, None] == device_ids[None, :], orders[None, :], 0), 1)
    return chosen * block_rows + row_ids % block_rows


def contract_rows(left_side, right_side):
    return lax.dot_general(
        left_side, right_side, (((0,), (0,)), ((), ())), preferred_element_type=jnp.float32
    )


def contract_cols(left_side, right_side):
    return lax.dot_general(
        left_side, right_side, (((1,), (1,)), ((), ())), preferred_element_type=jnp.float32
    )


def summed_rows(term_rows, shard_count):
    return lax.psum_scatter(
        term_rows(jnp.int32(0), lax.axis_size("fsdp") * shard_count).astype(jnp.bfloat16),
        "fsdp",
        scatter_dimension=0,
        tiled=True,
    ).astype(jnp.float32)


def rows_of(left_side, right_side):

    def term_rows(start_row, count):
        return contract_rows(left_side, right_side)

    return term_rows


def local(
    tokens_in,
    block_order,
    norm_attn,
    w_qkv,
    b_qkv,
    w_out,
    norm_mlp,
    w_gate,
    w_up,
    w_down,
    cotangent,
):
    block_rows = tokens_in.shape[0]
    context_count = lax.axis_size("ctx")
    seq_length = block_rows * context_count
    orders = block_order[0]
    context_index = lax.axis_index("ctx")
    own_block = jnp.sum(
        jnp.where(jnp.arange(context_count, dtype=jnp.int32) == context_index, orders, 0)
    )
    query_pos = own_block * block_rows + jnp.arange(block_rows, dtype=jnp.int32)
    query_top = own_block * block_rows + block_rows - 1
    cosine, sine_part = rotary(query_pos, HEAD)
    group_size = HEADS // KV_HEADS
    q_width = HEADS * HEAD
    k_width = KV_HEADS * HEAD
    score_scale = HEAD ** (-0.5)
    source = tokens_in.astype(jnp.float32)
    qkv_all, out_all, bias_all, gain_attn, gain_mlp = (
        lax.all_gather(w_qkv, "fsdp", axis=0, tiled=True),
        lax.all_gather(w_out, "fsdp", axis=0, tiled=True),
        lax.all_gather(b_qkv, "fsdp", axis=0, tiled=True),
        lax.all_gather(norm_attn, "fsdp", axis=0, tiled=True),
        lax.all_gather(norm_mlp, "fsdp", axis=0, tiled=True),
    )
    gain_attn = gain_attn.astype(jnp.float32)
    gain_mlp = gain_mlp.astype(jnp.float32)
    scale_one = lax.rsqrt(jnp.mean(source * source, -1, keepdims=True) + norm_eps)
    normed = (source * scale_one * gain_attn).astype(jnp.bfloat16)
    projected = jnp.dot(normed, qkv_all, preferred_element_type=jnp.float32) + bias_all.astype(
        jnp.float32
    )
    query = projected[:, :q_width].reshape(block_rows, HEADS, HEAD)
    key_heads = projected[:, q_width : q_width + k_width].reshape(block_rows, KV_HEADS, HEAD)
    query = (
        (query * cosine + turned(query) * sine_part)
        .astype(jnp.bfloat16)
        .reshape(block_rows, KV_HEADS, group_size, HEAD)
    )
    key_heads = (
        (key_heads * cosine + turned(key_heads) * sine_part)
        .astype(jnp.bfloat16)
        .reshape(block_rows, k_width)
    )
    keys_values = jnp.concatenate(
        [key_heads, projected[:, q_width + k_width :].astype(jnp.bfloat16)], 1
    )

    def scores_of(key_rows, key_pos):
        raw_scores = (
            jnp.einsum("qhgd,khd->qhgk", query, key_rows, preferred_element_type=jnp.float32)
            * score_scale
        )
        visible = key_pos[None, None, None, :] <= query_pos[:, None, None, None]
        return (jnp.where(visible, raw_scores, masked_score), visible)

    start_state = (
        jnp.full((block_rows, KV_HEADS, group_size), masked_score, jnp.float32),
        jnp.zeros((block_rows, KV_HEADS, group_size), jnp.float32),
        jnp.zeros((block_rows, KV_HEADS, group_size, HEAD), jnp.float32),
    )
    carry_state = start_state
    shard_piece = lax.all_gather(keys_values, "ctx", axis=0, tiled=True)
    start_row = jnp.int32(0)
    count = shard_piece.shape[0]
    sub_rows = min(count, 512)
    for offset in range(0, count, sub_rows):
        subpiece = shard_piece[offset : offset + sub_rows]
        key_pos = key_positions(orders, start_row + offset, subpiece.shape[0], block_rows)

        def update(state_now):
            run_max, run_sum, accum = state_now
            key_rows = subpiece[:, :k_width].reshape(-1, KV_HEADS, HEAD)
            value_rows = subpiece[:, k_width:].reshape(-1, KV_HEADS, HEAD)
            scores, visible = scores_of(key_rows, key_pos)
            new_max = jnp.maximum(run_max, jnp.max(scores, -1))
            factor = jnp.exp(run_max - new_max)
            weights = jnp.where(visible, jnp.exp(scores - new_max[..., None]), 0.0)
            run_sum = run_sum * factor + jnp.sum(weights, -1)
            accum = accum * factor[..., None] + jnp.einsum(
                "qhgk,khd->qhgd",
                weights.astype(jnp.bfloat16),
                value_rows,
                preferred_element_type=jnp.float32,
            )
            return (new_max, run_sum, accum)

        carry_state = lax.cond(
            jnp.min(key_pos) <= query_top, update, lambda same_state: same_state, carry_state
        )
    run_max, run_sum, accum = carry_state
    log_total = run_max + jnp.log(run_sum)
    mixed_full = (accum / run_sum[..., None]).reshape(block_rows, q_width)
    mixed = mixed_full.astype(jnp.bfloat16)
    hidden = source + jnp.dot(mixed, out_all, preferred_element_type=jnp.float32)
    scale_two = lax.rsqrt(jnp.mean(hidden * hidden, -1, keepdims=True) + norm_eps)
    normed_two = (hidden * scale_two * gain_mlp).astype(jnp.bfloat16)
    pieces = (
        lax.all_gather(w_gate, "fsdp", axis=0, tiled=True),
        lax.all_gather(w_up, "fsdp", axis=0, tiled=True),
    )
    columns = normed_two
    gate_value = jnp.dot(columns, pieces[0], preferred_element_type=jnp.float32)
    up_value = jnp.dot(columns, pieces[1], preferred_element_type=jnp.float32)
    sigmoid_gate = jax.nn.sigmoid(gate_value)
    swished = gate_value * sigmoid_gate
    activation = (swished * up_value).astype(jnp.bfloat16)
    columns = activation
    mlp_out = jnp.dot(
        columns,
        lax.all_gather(w_down, "fsdp", axis=0, tiled=True),
        preferred_element_type=jnp.float32,
    )
    out_tokens = (hidden + mlp_out).astype(jnp.bfloat16)
    grad_out = cotangent.astype(jnp.float32)
    grad_act = contract_cols(cotangent, lax.all_gather(w_down, "fsdp", axis=0, tiled=True))
    slope = sigmoid_gate * (1.0 + gate_value * (1.0 - sigmoid_gate))
    grad_gate = (grad_act * up_value * slope).astype(jnp.bfloat16)
    grad_up = (grad_act * swished).astype(jnp.bfloat16)
    pieces = (
        lax.all_gather(w_gate, "fsdp", axis=0, tiled=True),
        lax.all_gather(w_up, "fsdp", axis=0, tiled=True),
    )
    part_grad = contract_cols(grad_gate, pieces[0]) + contract_cols(grad_up, pieces[1])
    scaled_two = part_grad * gain_mlp
    grad_hidden = (
        grad_out
        + scale_two * scaled_two
        - hidden * scale_two**3 * jnp.mean(hidden * scaled_two, -1, keepdims=True)
    )
    gain_mlp_local = jnp.sum(part_grad * hidden * scale_two, 0)
    grad_branch = grad_hidden.astype(jnp.bfloat16)
    grad_mixed = contract_cols(grad_branch, out_all).astype(jnp.bfloat16)
    grad_heads = grad_mixed.reshape(block_rows, KV_HEADS, group_size, HEAD)
    row_delta = jnp.sum(
        grad_heads.astype(jnp.float32) * mixed_full.reshape(block_rows, KV_HEADS, group_size, HEAD),
        -1,
    )
    start_back = (
        jnp.zeros((block_rows, KV_HEADS, group_size, HEAD), jnp.float32),
        jnp.zeros((seq_length, 2 * k_width), jnp.float32),
    )
    carry_state = start_back
    shard_piece = lax.all_gather(keys_values, "ctx", axis=0, tiled=True)
    start_row = jnp.int32(0)
    count = shard_piece.shape[0]
    sub_rows = min(count, 512)
    for offset in range(0, count, sub_rows):
        attend_subpiece = shard_piece[offset : offset + sub_rows]
        attend_key_pos = key_positions(
            orders, start_row + offset, attend_subpiece.shape[0], block_rows
        )
        row_first = start_row + offset

        def update(state_now):
            grad_query, kv_terms = state_now
            key_rows = attend_subpiece[:, :k_width].reshape(-1, KV_HEADS, HEAD)
            value_rows = attend_subpiece[:, k_width:].reshape(-1, KV_HEADS, HEAD)
            scores, visible = scores_of(key_rows, attend_key_pos)
            probability = jnp.where(visible, jnp.exp(scores - log_total[..., None]), 0.0)
            grad_probs = jnp.einsum(
                "qhgd,khd->qhgk", grad_heads, value_rows, preferred_element_type=jnp.float32
            )
            grad_scores = (probability * (grad_probs - row_delta[..., None]) * score_scale).astype(
                jnp.bfloat16
            )
            grad_query = grad_query + jnp.einsum(
                "qhgk,khd->qhgd", grad_scores, key_rows, preferred_element_type=jnp.float32
            )
            grad_keys = jnp.einsum(
                "qhgk,qhgd->khd", grad_scores, query, preferred_element_type=jnp.float32
            )
            grad_values = jnp.einsum(
                "qhgk,qhgd->khd",
                probability.astype(jnp.bfloat16),
                grad_heads,
                preferred_element_type=jnp.float32,
            )
            new_terms = jnp.concatenate(
                [grad_keys.reshape(-1, k_width), grad_values.reshape(-1, k_width)], 1
            )
            earlier = lax.dynamic_slice_in_dim(kv_terms, row_first, new_terms.shape[0], 0)
            kv_terms = lax.dynamic_update_slice_in_dim(kv_terms, earlier + new_terms, row_first, 0)
            return (grad_query, kv_terms)

        carry_state = lax.cond(
            jnp.min(attend_key_pos) <= query_top, update, lambda same_state: same_state, carry_state
        )
    grad_query, kv_terms = carry_state
    grad_kv = lax.psum_scatter(
        kv_terms.astype(jnp.bfloat16), "ctx", scatter_dimension=0, tiled=True
    ).astype(jnp.float32)
    grad_query = grad_query.reshape(block_rows, HEADS, HEAD)
    grad_query = grad_query * cosine + turned_back(grad_query * sine_part)
    grad_key = grad_kv[:, :k_width].reshape(block_rows, KV_HEADS, HEAD)
    grad_key = grad_key * cosine + turned_back(grad_key * sine_part)
    grad_projected = jnp.concatenate(
        [
            grad_query.reshape(block_rows, q_width),
            grad_key.reshape(block_rows, k_width),
            grad_kv[:, k_width:],
        ],
        1,
    ).astype(jnp.bfloat16)
    bias_local = jnp.sum(grad_projected.astype(jnp.float32), 0)
    grad_normed = contract_cols(grad_projected, qkv_all)
    scaled_one = grad_normed * gain_attn
    grad_tokens = (
        grad_hidden
        + scale_one * scaled_one
        - source * scale_one**3 * jnp.mean(source * scaled_one, -1, keepdims=True)
    ).astype(jnp.bfloat16)
    gain_attn_local = jnp.sum(grad_normed * source * scale_one, 0)

    def term_mlp(start_row, count):
        return jnp.stack(
            [contract_rows(normed_two, grad_gate), contract_rows(normed_two, grad_up)], 1
        )

    grad_qkv = summed_rows(rows_of(normed, grad_projected), w_qkv.shape[0])
    grad_outp = summed_rows(rows_of(mixed, grad_branch), w_out.shape[0])
    grad_mlp = summed_rows(term_mlp, w_gate.shape[0])
    grad_down = summed_rows(rows_of(activation, cotangent), w_down.shape[0])
    bias_part, gain_attn_part, gain_mlp_part = (
        lax.psum_scatter(bias_local, "fsdp", scatter_dimension=0, tiled=True),
        lax.psum_scatter(gain_attn_local, "fsdp", scatter_dimension=0, tiled=True),
        lax.psum_scatter(gain_mlp_local, "fsdp", scatter_dimension=0, tiled=True),
    )
    grad_qkv, grad_outp, grad_mlp, grad_down, bias_part, gain_attn_part, gain_mlp_part = (
        lax.psum(grad_qkv.astype(jnp.bfloat16), "ctx").astype(jnp.float32),
        lax.psum(grad_outp.astype(jnp.bfloat16), "ctx").astype(jnp.float32),
        lax.psum(grad_mlp.astype(jnp.bfloat16), "ctx").astype(jnp.float32),
        lax.psum(grad_down.astype(jnp.bfloat16), "ctx").astype(jnp.float32),
        lax.psum(bias_part.astype(jnp.bfloat16), "ctx").astype(jnp.float32),
        lax.psum(gain_attn_part.astype(jnp.bfloat16), "ctx").astype(jnp.float32),
        lax.psum(gain_mlp_part.astype(jnp.bfloat16), "ctx").astype(jnp.float32),
    )
    return (
        out_tokens,
        grad_tokens,
        gain_attn_part,
        grad_qkv,
        bias_part,
        grad_outp,
        gain_mlp_part,
        grad_mlp[:, 0],
        grad_mlp[:, 1],
        grad_down,
    )


def solution(mesh):
    in_specs = (
        P(("fsdp", "ctx"), None),
        P("fsdp", None),
        P("fsdp"),
        P("fsdp", None),
        P("fsdp"),
        P("fsdp", None),
        P("fsdp"),
        P("fsdp", None),
        P("fsdp", None),
        P("fsdp", None),
        P(("fsdp", "ctx"), None),
    )
    out_specs = (
        P(("fsdp", "ctx"), None),
        P(("fsdp", "ctx"), None),
        P("fsdp"),
        P("fsdp", None),
        P("fsdp"),
        P("fsdp", None),
        P("fsdp"),
        P("fsdp", None),
        P("fsdp", None),
        P("fsdp", None),
    )
    return jax.shard_map(local, mesh=mesh, in_specs=in_specs, out_specs=out_specs, check_vma=False)
```

profile of v0, /device:TPU:0, one launch (start us, length us, event | category | flops | bytes accessed | tf_op | source)
XLA Modules:
  0.0 1727.8 jit_solution(1025805456949484476)
XLA Ops:
  22.7 13.7 all-reduce.7
  41.1 17.2 all-gather.8.cloned.1.call-done
  74.2 19.7 %all-gather.10.cloned.1.call-done = bf16[1024,512]{1,0:T(8,128)(2,1)} async-done(((bf16[256,512]{1,0:T(8,128)(2,1)}), bf16[1024,512]{1,0:T(8,128)(2,1)}) %all-gather.10.cloned.1.call-update) | async-done | bytes 1048592 | tf_op jit(solution)/shard_map/all_gather | solution.py:144
  139.4 131.9 %all-gather.14.cloned.1.call-done = bf16[1536,8960]{1,0:T(8,128)(2,1)} async-done(((bf16[192,8960]{1,0:T(8,128)(2,1)}), bf16[1536,8960]{1,0:T(8,128)(2,1)}) %all-gather.14.cloned.1.call-update) | async-done | bytes 27525136 | tf_op jit(solution)/shard_map/all_gather | solution.py:180
  271.3 15.6 fusion.106
  286.9 121.5 %all-gather.16.cloned.1.call-done = bf16[1536,8960]{1,0:T(8,128)(2,1)} async-done(((bf16[192,8960]{1,0:T(8,128)(2,1)}), bf16[1536,8960]{1,0:T(8,128)(2,1)}) %all-gather.16.cloned.1.call-update) | async-done | bytes 27525136 | tf_op jit(solution)/shard_map/all_gather | solution.py:181
  408.4 15.6 fusion.107
  424.0 121.5 %all-gather.18.cloned.1.call-done = bf16[8960,1536]{1,0:T(8,128)(2,1)} async-done(((bf16[1120,1536]{1,0:T(8,128)(2,1)}), bf16[8960,1536]{1,0:T(8,128)(2,1)}) %all-gather.18.cloned.1.call-update) | async-done | bytes 27525136 | tf_op jit(solution)/shard_map/all_gather | solution.py:192
  545.4 21.5 %multiply_convert_fusion = (bf16[256,8960]{1,0:T(8,128)(2,1)}, bf16[256,8960]{1,0:T(8,128)(2,1)}, bf16[256,8960]{1,0:T(8,128)(2,1)}) fusion(f32[256,8960]{1,0:T(8,128)} %fusion.106, f32[256,8960]{1,0:T(8,128)} %fusion.107, bf16[256,1536]{1,0:T(8,128)(2,1)} %param.29, bf16[8960,1536]{1,0:T(8,128)(2,1)} %all-gather.18.cloned.1.call-done), kind=kOutput, calls=%fused_computation.71 | convolution fusion | flops 7080837120 | bytes 60424192 | tf_op jit(solution)/shard_map/dot_general | solution.py:49
  567.0 14.8 fusion.108
  581.7 27.8 %multiply_reduce_fusion = (f32[1536]{0:T(1024)}, f32[256]{0:T(256)S(1)}, f32[256,1536]{1,0:T(8,128)}) fusion(f32[256,1536]{1,0:T(8,128)} %copy-done.1, f32[256]{0:T(256)S(1)} %get-tuple-element.330, f32[1536]{0:T(1024)S(1)} %convert_element_type.160, f32[256,1536]{1,0:T(8,128)} %fusion.108, bf16[256,8960]{1,0:T(8,128)(2,1)} %get-tuple-element.308, ...), kind=kOutput, calls=%fused_computation.109 | convolution fusion | flops 7049181184 | bytes 36845568 | tf_op jit(solution)/shard_map/dot_general | solution.py:49
  630.7 18.6 %conditional.7 = (f32[1024,512]{0,1:T(8,128)}, f32[256,2,6,128]{0,3,2,1:T(8,128)}) conditional(s32[]{:T(128)} %convert_element_type.150, (f32[256,2,6,128]{3,0,2,1:T(8,128)}, f32[1024,512]{0,1:T(8,128)}) %conditional.6, (s32[512]{0:T(512)S(1)}, s32[256]{0:T(256)S(1)}, bf16[512,512]{1,0:T(8,128)(2,1)S(1)}, bf16[256,2,6,128]{0,3,2,1:T(8,128)(2,1)S(1)}, ...), branch_computations={%region_19.20_spmd, %region_20.21_spmd} | conditional | flops 2034761728 | bytes 48405548 | solution.py:267
  659.8 19.4 %reduce-scatter.6.cloned.1.call-done = bf16[256,512]{1,0:T(8,128)(2,1)} async-done(((bf16[1024,512]{1,0:T(8,128)(2,1)}), bf16[256,512]{1,0:T(8,128)(2,1)}) %reduce-scatter.6.cloned.1.call-update) | async-done | bytes 262160 | tf_op jit(solution)/shard_map/reduce_scatter | solution.py:271
  689.1 16.1 convolution_convert_fusion
  706.5 15.2 fusion.51
  721.7 15.3 fusion.50
  737.1 38.6 %pad_maximum_fusion = bf16[1536,2,8960]{2,0,1:T(8,128)(2,1)} fusion(bf16[1536,1,8960]{2,0,1:T(8,128)(2,1)} %fusion.51, bf16[1536,1,8960]{2,0,1:T(8,128)(2,1)} %fusion.50), kind=kLoop, calls=%fused_computation.65 | loop fusion | flops 27525120 | bytes 110100480 | tf_op jit(solution)/shard_map/stack | solution.py:297
  775.9 26.0 %reduce-scatter.8.cloned.1.call-done = bf16[192,2048]{1,0:T(8,128)(2,1)} async-done(((bf16[1536,2048]{1,0:T(8,128)(2,1)}), bf16[192,2048]{1,0:T(8,128)(2,1)}) %reduce-scatter.8.cloned.1.call-update) | async-done | bytes 786448 | tf_op jit(solution)/shard_map/reduce_scatter | solution.py:55
  801.9 173.1 %reduce-scatter.14.cloned.1.call-done = bf16[1120,1536]{1,0:T(8,128)(2,1)} async-done(((bf16[8960,1536]{1,0:T(8,128)(2,1)}), bf16[1120,1536]{1,0:T(8,128)(2,1)}) %reduce-scatter.14.cloned.1.call-update) | async-done | bytes 3440656 | tf_op jit(solution)/shard_map/reduce_scatter | solution.py:55
  975.0 314.4 %reduce-scatter.12.cloned.1.call-done = bf16[192,2,8960]{2,0,1:T(8,128)(2,1)} async-done(((bf16[1536,2,8960]{2,0,1:T(8,128)(2,1)}), bf16[192,2,8960]{2,0,1:T(8,128)(2,1)}) %reduce-scatter.12.cloned.1.call-update) | async-done | bytes 6881296 | tf_op jit(solution)/shard_map/reduce_scatter | solution.py:55
  1290.8 15.8 fusion.53
  1313.1 24.7 %all-reduce.6 = (bf16[1536]{0:T(1024)(128)(2,1)S(1)}, bf16[2048]{0:T(1024)(128)(2,1)S(1)}, bf16[1536]{0:T(1024)(128)(2,1)S(1)}) all-reduce(f32[1536]{0:T(1024)S(1)} %get-tuple-element.272, f32[2048]{0:T(1024)S(1)} %convert_reduce_fusion, f32[1536]{0:T(1024)S(1)} %copy-done.28), channel_id=3, replica_groups=mesh['fsdp'=8,'ctx'=4] {'fsdp'}, use_global_device_ids=true, to_apply=%region_24.25.clone | all-reduce | flops 5120 | bytes 30720
  1338.0 14.0 all-reduce.8
  1356.5 335.9 %all-reduce.12.cloned.1.call-done = (bf16[192,2048]{1,0:T(8,128)(2,1)}, bf16[192,1536]{1,0:T(8,128)(2,1)}, bf16[192,2,8960]{2,0,1:T(8,128)(2,1)}, bf16[1120,1536]{1,0:T(8,128)(2,1)}) async-done(((bf16[192,2048]{1,0:T(8,128)(2,1)}, bf16[192,1536]{1,0:T(8,128)(2,1)}, bf16[192,2,8960]{2,0,1:T(8,128)(2,1)}, bf16[1120,1536]{1,0:T(8,128)(2,1)}), (bf16[192,2048]{1,0:T(8,128)(2,1)}, bf16[192,1536]{1,0:T(8,128)(2,1)}, ...) | async-done | bytes 11698192 | tf_op jit(solution)/shard_map/psum | solution.py:311
  (211 shorter events, 211.5 us)
Async XLA Ops:
  7.2 51.2 %all-gather.8.cloned.1.call-start = ((), (), s32[]{:S(2)}) async-start(), calls=%async_computation.5 | async-start | bytes 7077888 | tf_op jit(solution)/shard_map/all_gather | solution.py:101
  7.9 86.0 %all-gather.10.cloned.1.call-start = ((), (), s32[]{:S(2)}) async-start(), calls=%async_computation.6 | async-start | bytes 1310720 | tf_op jit(solution)/shard_map/all_gather | solution.py:144
  36.5 26.8 %copy-start.24 = (f32[1536]{0:T(1024)}, f32[1536]{0:T(1024)S(1)}, u32[]{:S(2)}) copy-start(f32[1536]{0:T(1024)S(1)} %convert_element_type.152) | copy-start | bytes 18436
  39.0 34.8 %copy-start.19 = (f32[256,128]{0,1:T(8,128)}, f32[256,128]{0,1:T(8,128)S(1)}, u32[]{:S(2)}) copy-start(f32[256,128]{0,1:T(8,128)S(1)} %get-tuple-element.325) | copy-start | bytes 393220
  39.0 34.8 %copy-start.21 = (f32[256,128]{0,1:T(8,128)}, f32[256,128]{0,1:T(8,128)S(1)}, u32[]{:S(2)}) copy-start(f32[256,128]{0,1:T(8,128)S(1)} %get-tuple-element.326) | copy-start | bytes 393220
  39.1 24.7 %copy-start.23 = (f32[256,128]{1,0:T(8,128)}, f32[256,128]{1,0:T(8,128)S(1)}, u32[]{:S(2)}) copy-start(f32[256,128]{1,0:T(8,128)S(1)} %copy.147) | copy-start | bytes 393220
  65.8 68.4 %all-gather.12.cloned.1.call-start = ((), (), s32[]{:S(2)}) async-start(), calls=%async_computation.7 | async-start | bytes 5308416 | tf_op jit(solution)/shard_map/all_gather | solution.py:102
  66.6 204.7 %all-gather.14.cloned.1.call-start = ((), (), s32[]{:S(2)}) async-start(), calls=%async_computation.8 | async-start | bytes 30965760 | tf_op jit(solution)/shard_map/all_gather | solution.py:180
  67.1 341.2 %all-gather.16.cloned.1.call-start = ((), (), s32[]{:S(2)}) async-start(), calls=%async_computation.9 | async-start | bytes 30965760 | tf_op jit(solution)/shard_map/all_gather | solution.py:181
  67.7 477.7 %all-gather.18.cloned.1.call-start = ((), (), s32[]{:S(2)}) async-start(), calls=%async_computation.10 | async-start | bytes 30965760 | tf_op jit(solution)/shard_map/all_gather | solution.py:192
  68.3 610.9 %reduce-scatter.6.cloned.1.call-start = ((), (), s32[]{:S(2)}) async-start(), calls=%async_computation.11 | async-start | bytes 1310720 | tf_op jit(solution)/shard_map/reduce_scatter | solution.py:271
  139.4 269.0 %copy-start.7 = (bf16[256,1536]{1,0:T(8,128)(2,1)}, bf16[256,1536]{1,0:T(8,128)(2,1)S(1)}, u32[]{:S(2)}) copy-start(bf16[256,1536]{1,0:T(8,128)(2,1)S(1)} %multiply_convert_fusion.3) | copy-start | bytes 2359300
  581.7 30.9 %slice-start = ((s8[4718592]{0:T(1024)(128)(4,1)}), s8[4194304]{0:T(1024)(128)(4,1)S(1)}, s32[]{:S(2)}) async-start(s8[4718592]{0:T(1024)(128)(4,1)} %bitcast.241), calls=%async_computation.17 | async-start | bytes 8388608
  581.7 27.9 %copy-start.2 = (f32[256,1536]{1,0:T(8,128)S(1)}, f32[256,1536]{1,0:T(8,128)}, u32[]{:S(2)}) copy-start(f32[256,1536]{1,0:T(8,128)} %copy-done.1) | copy-start | bytes 4718596
  581.7 27.9 %copy-start.15 = (bf16[256,1536]{1,0:T(8,128)(2,1)S(1)}, bf16[256,1536]{1,0:T(8,128)(2,1)}, u32[]{:S(2)}) copy-start(bf16[256,1536]{1,0:T(8,128)(2,1)} %param.29) | copy-start | bytes 2359300
  581.7 30.9 %slice-start.1 = ((s8[4718592]{0:T(1024)(128)(4,1)}), s8[524288]{0:T(1024)(128)(4,1)S(1)}, s32[]{:S(2)}) async-start(s8[4718592]{0:T(1024)(128)(4,1)} %bitcast.241), calls=%async_computation.18 | async-start | bytes 1048576
  651.9 124.1 %reduce-scatter.10.cloned.1.call-start = ((), (), s32[]{:S(2)}) async-start(), calls=%async_computation.13 | async-start | bytes 5308416 | tf_op jit(solution)/shard_map/reduce_scatter | solution.py:55
  657.0 145.0 %reduce-scatter.8.cloned.1.call-start = ((), (), s32[]{:S(2)}) async-start(), calls=%async_computation.12 | async-start | bytes 7077888 | tf_op jit(solution)/shard_map/reduce_scatter | solution.py:55
  659.4 23.9 %copy-start.27 = (f32[256]{0:T(256)S(1)}, f32[256]{0:T(256)}, u32[]{:S(2)}) copy-start(f32[256]{0:T(256)} %copy-done.26) | copy-start | bytes 3076
  688.0 287.1 %reduce-scatter.14.cloned.1.call-start = ((), (), s32[]{:S(2)}) async-start(), calls=%async_computation.15 | async-start | bytes 30965760 | tf_op jit(solution)/shard_map/reduce_scatter | solution.py:55
  705.3 584.2 %reduce-scatter.12.cloned.1.call-start = ((), (), s32[]{:S(2)}) async-start(), calls=%async_computation.14 | async-start | bytes 61931520 | tf_op jit(solution)/shard_map/reduce_scatter | solution.py:55
  775.7 916.6 %all-reduce.12.cloned.1.call-start = ((), (), s32[]{:S(2)}) async-start(), calls=%async_computation.16 | async-start | bytes 23396352 | tf_op jit(solution)/shard_map/psum | solution.py:311
  1307.1 46.6 %copy-start.6 = (f32[256,1536]{1,0:T(8,128)S(1)}, f32[256,1536]{1,0:T(8,128)}, u32[]{:S(2)}) copy-start(f32[256,1536]{1,0:T(8,128)} %copy-done.5) | copy-start | bytes 4718596
  1307.1 46.6 %copy-start.29 = (f32[256]{0:T(256)S(1)}, f32[256]{0:T(256)}, u32[]{:S(2)}) copy-start(f32[256]{0:T(256)} %get-tuple-element.327) | copy-start | bytes 3076
  (21 other events, 144.9 us)
Sparse Core Ops, SparseCore 0:
  9.9 48.4 all-gather.7
  65.9 27.9 all-gather.9
  95.8 38.3 all-gather.11
  136.0 135.2 all-gather.13
  273.0 135.2 all-gather.15
  410.1 135.2 all-gather.17
  652.0 27.1 reduce-scatter.5
  683.6 52.5 reduce-scatter.9
  740.1 61.7 reduce-scatter.7
  805.8 169.1 reduce-scatter.13
  979.1 310.2 reduce-scatter.11
  1292.2 400.0 all-reduce.11
where the time goes:
time: 1730 us
  waiting for transfers between devices  1300 us (75%)
  matrix products  215 us (12%)
  other arithmetic  89.2 us (5%)
  blocking collectives  62.7 us (4%)
  local copies, waits for them, and re-layouts  43.1 us (2%)
  between operations  18.8 us (1%)
    reduce_scatter x4, waiting for transfers between devices, summed_rows(): lax.psum_scatter(term_rows(jnp.int32(0), lax.axis_size('fsdp') * shard_co...  514 us
    psum x1, waiting for transfers between devices, local(): lax.psum(grad_qkv.astype(jnp.bfloat16), 'ctx').astype(jnp.float32)  336 us
    all_gather x1, waiting for transfers between devices, local(): lax.all_gather(w_gate, 'fsdp', axis=0, tiled=True)  132 us
    all_gather x1, waiting for transfers between devices, local(): lax.all_gather(w_down, 'fsdp', axis=0, tiled=True)  121 us
    all_gather x1, waiting for transfers between devices, local(): lax.all_gather(w_up, 'fsdp', axis=0, tiled=True)  121 us
    dot_general x5, matrix products, contract_cols(): lax.dot_general(left_side, right_side, (((1,), (1,)), ((), ())), preferre...  72.4 us
    dot_general x5, matrix products, contract_rows(): lax.dot_general(left_side, right_side, (((0,), (0,)), ((), ())), preferre...  56.3 us
    another operation x1, other arithmetic, term_mlp(): jnp.stack([contract_rows(normed_two, grad_gate), contract_rows(normed_two...  38.6 us
  transfers between devices with their start and end apart: 12, of which 11 were waited for; matrix products, arithmetic and copies ran while one was open for 12% of the time, Pallas kernels for 0%

commit v1 on v0

--- a/solution.py
+++ b/solution.py
@@ -51,21 +51,40 @@
     )
 
 
-def summed_rows(term_rows, shard_count):
-    return lax.psum_scatter(
-        term_rows(jnp.int32(0), lax.axis_size("fsdp") * shard_count).astype(jnp.bfloat16),
-        "fsdp",
-        scatter_dimension=0,
-        tiled=True,
-    ).astype(jnp.float32)
-
-
-def rows_of(left_side, right_side):
-
-    def term_rows(start_row, count):
-        return contract_rows(left_side, right_side)
-
-    return term_rows
+def plus(left_side, right_side):
+    return (left_side.astype(jnp.float32) + right_side.astype(jnp.float32)).astype(jnp.bfloat16)
+
+
+def ctx_sums(chunks):
+    if lax.axis_size("ctx") != 4:
+        return [lax.psum(chunk, "ctx") for chunk in chunks]
+    place = lax.axis_index("ctx")
+    outer = (place == 0) | (place == 3)
+    depth = 2
+    count = len(chunks)
+    totals, results = [], []
+    for step in range(count + depth):
+        coming = chunks[step] if step < count else None
+        going = totals[step - depth] if step >= depth else None
+        if coming is None or going is None or coming.shape == going.shape:
+            if going is None:
+                payload = coming
+            elif coming is None:
+                payload = going
+            else:
+                payload = jnp.where(outer, coming, going)
+            swapped = lax.ppermute(payload, "ctx", [(0, 1), (1, 0), (2, 3), (3, 2)])
+            inward = outward = swapped
+        else:
+            inward = lax.ppermute(coming, "ctx", [(0, 1), (3, 2)])
+            outward = lax.ppermute(going, "ctx", [(1, 0), (2, 3)])
+        if going is not None:
+            results.append(jnp.where(outer, outward, going))
+        if coming is not None:
+            pair_sum = plus(coming, inward)
+            across = lax.ppermute(pair_sum, "ctx", [(1, 2), (2, 1)])
+            totals.append(plus(pair_sum, across))
+    return results
 
 
 def local(
@@ -81,11 +100,13 @@
     w_down,
     cotangent,
 ):
-    block_rows = tokens_in.shape[0]
+    block_rows, width = tokens_in.shape
+    shard_count = lax.axis_size("fsdp")
     context_count = lax.axis_size("ctx")
     seq_length = block_rows * context_count
     orders = block_order[0]
     context_index = lax.axis_index("ctx")
+    shard_index = lax.axis_index("fsdp")
     own_block = jnp.sum(
         jnp.where(jnp.arange(context_count, dtype=jnp.int32) == context_index, orders, 0)
     )
@@ -97,20 +118,27 @@
     k_width = KV_HEADS * HEAD
     score_scale = HEAD ** (-0.5)
     source = tokens_in.astype(jnp.float32)
-    qkv_all, out_all, bias_all, gain_attn, gain_mlp = (
-        lax.all_gather(w_qkv, "fsdp", axis=0, tiled=True),
-        lax.all_gather(w_out, "fsdp", axis=0, tiled=True),
-        lax.all_gather(b_qkv, "fsdp", axis=0, tiled=True),
-        lax.all_gather(norm_attn, "fsdp", axis=0, tiled=True),
-        lax.all_gather(norm_mlp, "fsdp", axis=0, tiled=True),
-    )
-    gain_attn = gain_attn.astype(jnp.float32)
-    gain_mlp = gain_mlp.astype(jnp.float32)
+    shard_rows = w_gate.shape[0]
+    ff_cols = w_gate.shape[1] // shard_count
+
+    qkv_all = lax.all_gather(w_qkv, "fsdp", axis=0, tiled=True)
+    vectors = lax.all_gather(jnp.concatenate([norm_attn, norm_mlp, b_qkv]), "fsdp", axis=0)
+    gain_attn = vectors[:, :shard_rows].reshape(-1).astype(jnp.float32)
+    gain_mlp = vectors[:, shard_rows : 2 * shard_rows].reshape(-1).astype(jnp.float32)
+    bias_all = vectors[:, 2 * shard_rows :].reshape(-1).astype(jnp.float32)
+
+    def to_columns(weight):
+        parts = weight.reshape(shard_rows, shard_count, ff_cols).transpose(1, 0, 2)
+        return lax.all_to_all(parts, "fsdp", 0, 0).reshape(width, ff_cols)
+
+    gate_cols = to_columns(w_gate)
+    up_cols = to_columns(w_up)
+    out_all = lax.all_gather(w_out, "fsdp", axis=0, tiled=True)
+    cot_all = lax.all_gather(cotangent, "fsdp", axis=0, tiled=True)
+
     scale_one = lax.rsqrt(jnp.mean(source * source, -1, keepdims=True) + norm_eps)
     normed = (source * scale_one * gain_attn).astype(jnp.bfloat16)
-    projected = jnp.dot(normed, qkv_all, preferred_element_type=jnp.float32) + bias_all.astype(
-        jnp.float32
-    )
+    projected = jnp.dot(normed, qkv_all, preferred_element_type=jnp.float32) + bias_all
     query = projected[:, :q_width].reshape(block_rows, HEADS, HEAD)
     key_heads = projected[:, q_width : q_width + k_width].reshape(block_rows, KV_HEADS, HEAD)
     query = (
@@ -142,12 +170,11 @@
     )
     carry_state = start_state
     shard_piece = lax.all_gather(keys_values, "ctx", axis=0, tiled=True)
-    start_row = jnp.int32(0)
     count = shard_piece.shape[0]
     sub_rows = min(count, 512)
     for offset in range(0, count, sub_rows):
         subpiece = shard_piece[offset : offset + sub_rows]
-        key_pos = key_positions(orders, start_row + offset, subpiece.shape[0], block_rows)
+        key_pos = key_positions(orders, jnp.int32(offset), subpiece.shape[0], block_rows)
 
         def update(state_now):
             run_max, run_sum, accum = state_now
@@ -176,33 +203,36 @@
     hidden = source + jnp.dot(mixed, out_all, preferred_element_type=jnp.float32)
     scale_two = lax.rsqrt(jnp.mean(hidden * hidden, -1, keepdims=True) + norm_eps)
     normed_two = (hidden * scale_two * gain_mlp).astype(jnp.bfloat16)
-    pieces = (
-        lax.all_gather(w_gate, "fsdp", axis=0, tiled=True),
-        lax.all_gather(w_up, "fsdp", axis=0, tiled=True),
-    )
-    columns = normed_two
-    gate_value = jnp.dot(columns, pieces[0], preferred_element_type=jnp.float32)
-    up_value = jnp.dot(columns, pieces[1], preferred_element_type=jnp.float32)
+
+    normed_all = lax.all_gather(normed_two, "fsdp", axis=0, tiled=True)
+    gate_value = jnp.dot(normed_all, gate_cols, preferred_element_type=jnp.float32)
+    up_value = jnp.dot(normed_all, up_cols, preferred_element_type=jnp.float32)
     sigmoid_gate = jax.nn.sigmoid(gate_value)
     swished = gate_value * sigmoid_gate
     activation = (swished * up_value).astype(jnp.bfloat16)
-    columns = activation
-    mlp_out = jnp.dot(
-        columns,
-        lax.all_gather(w_down, "fsdp", axis=0, tiled=True),
-        preferred_element_type=jnp.float32,
-    )
-    out_tokens = (hidden + mlp_out).astype(jnp.bfloat16)
-    grad_out = cotangent.astype(jnp.float32)
-    grad_act = contract_cols(cotangent, lax.all_gather(w_down, "fsdp", axis=0, tiled=True))
+    grad_act = contract_cols(cot_all, w_down)
     slope = sigmoid_gate * (1.0 + gate_value * (1.0 - sigmoid_gate))
     grad_gate = (grad_act * up_value * slope).astype(jnp.bfloat16)
     grad_up = (grad_act * swished).astype(jnp.bfloat16)
-    pieces = (
-        lax.all_gather(w_gate, "fsdp", axis=0, tiled=True),
-        lax.all_gather(w_up, "fsdp", axis=0, tiled=True),
-    )
-    part_grad = contract_cols(grad_gate, pieces[0]) + contract_cols(grad_up, pieces[1])
+    grad_terms = contract_cols(grad_gate, gate_cols) + contract_cols(grad_up, up_cols)
+    part_grad = lax.psum_scatter(
+        grad_terms.astype(jnp.bfloat16), "fsdp", scatter_dimension=0, tiled=True
+    ).astype(jnp.float32)
+    down_terms = contract_rows(activation, cot_all).astype(jnp.bfloat16)
+
+    def to_rows(terms):
+        parts = terms.astype(jnp.bfloat16).reshape(shard_count, shard_rows, ff_cols)
+        return lax.all_to_all(parts, "fsdp", 0, 0)
+
+    gate_terms = to_rows(contract_rows(normed_all, grad_gate))
+    up_terms = to_rows(contract_rows(normed_all, grad_up))
+    mlp_terms = jnp.dot(activation, w_down, preferred_element_type=jnp.float32)
+    mlp_out = lax.psum_scatter(
+        mlp_terms.astype(jnp.bfloat16), "fsdp", scatter_dimension=0, tiled=True
+    ).astype(jnp.float32)
+    out_tokens = (hidden + mlp_out).astype(jnp.bfloat16)
+
+    grad_out = cotangent.astype(jnp.float32)
     scaled_two = part_grad * gain_mlp
     grad_hidden = (
         grad_out
@@ -222,16 +252,11 @@
         jnp.zeros((seq_length, 2 * k_width), jnp.float32),
     )
     carry_state = start_back
-    shard_piece = lax.all_gather(keys_values, "ctx", axis=0, tiled=True)
-    start_row = jnp.int32(0)
-    count = shard_piece.shape[0]
-    sub_rows = min(count, 512)
     for offset in range(0, count, sub_rows):
         attend_subpiece = shard_piece[offset : offset + sub_rows]
         attend_key_pos = key_positions(
-            orders, start_row + offset, attend_subpiece.shape[0], block_rows
-        )
-        row_first = start_row + offset
+            orders, jnp.int32(offset), attend_subpiece.shape[0], block_rows
+        )
 
         def update(state_now):
             grad_query, kv_terms = state_now
@@ -260,8 +285,8 @@
             new_terms = jnp.concatenate(
                 [grad_keys.reshape(-1, k_width), grad_values.reshape(-1, k_width)], 1
             )
-            earlier = lax.dynamic_slice_in_dim(kv_terms, row_first, new_terms.shape[0], 0)
-            kv_terms = lax.dynamic_update_slice_in_dim(kv_terms, earlier + new_terms, row_first, 0)
+            earlier = kv_terms[offset : offset + new_terms.shape[0]]
+            kv_terms = lax.dynamic_update_slice_in_dim(kv_terms, earlier + new_terms, offset, 0)
             return (grad_query, kv_terms)
 
         carry_state = lax.cond(
@@ -293,39 +318,50 @@
     ).astype(jnp.bfloat16)
     gain_attn_local = jnp.sum(grad_normed * source * scale_one, 0)
 
-    def term_mlp(start_row, count):
-        return jnp.stack(
-            [contract_rows(normed_two, grad_gate), contract_rows(normed_two, grad_up)], 1
-        )
-
-    grad_qkv = summed_rows(rows_of(normed, grad_projected), w_qkv.shape[0])
-    grad_outp = summed_rows(rows_of(mixed, grad_branch), w_out.shape[0])
-    grad_mlp = summed_rows(term_mlp, w_gate.shape[0])
-    grad_down = summed_rows(rows_of(activation, cotangent), w_down.shape[0])
-    bias_part, gain_attn_part, gain_mlp_part = (
-        lax.psum_scatter(bias_local, "fsdp", scatter_dimension=0, tiled=True),
-        lax.psum_scatter(gain_attn_local, "fsdp", scatter_dimension=0, tiled=True),
-        lax.psum_scatter(gain_mlp_local, "fsdp", scatter_dimension=0, tiled=True),
-    )
-    grad_qkv, grad_outp, grad_mlp, grad_down, bias_part, gain_attn_part, gain_mlp_part = (
-        lax.psum(grad_qkv.astype(jnp.bfloat16), "ctx").astype(jnp.float32),
-        lax.psum(grad_outp.astype(jnp.bfloat16), "ctx").astype(jnp.float32),
-        lax.psum(grad_mlp.astype(jnp.bfloat16), "ctx").astype(jnp.float32),
-        lax.psum(grad_down.astype(jnp.bfloat16), "ctx").astype(jnp.float32),
-        lax.psum(bias_part.astype(jnp.bfloat16), "ctx").astype(jnp.float32),
-        lax.psum(gain_attn_part.astype(jnp.bfloat16), "ctx").astype(jnp.float32),
-        lax.psum(gain_mlp_part.astype(jnp.bfloat16), "ctx").astype(jnp.float32),
-    )
+    def to_owner(terms):
+        return lax.psum_scatter(
+            terms.astype(jnp.bfloat16), "fsdp", scatter_dimension=0, tiled=True
+        )
+
+    out_terms = to_owner(contract_rows(mixed, grad_branch))
+    qkv_terms = to_owner(contract_rows(normed, grad_projected))
+
+    down_cuts, col_cuts = 5, 4
+    down_step, col_step = down_terms.shape[0] // down_cuts, shard_count // col_cuts
+    chunks = [down_terms[i * down_step : (i + 1) * down_step] for i in range(down_cuts)]
+    chunks += [gate_terms[i * col_step : (i + 1) * col_step] for i in range(col_cuts)]
+    chunks += [up_terms[i * col_step : (i + 1) * col_step] for i in range(col_cuts)]
+    chunks += [out_terms, qkv_terms]
+    sums = ctx_sums(chunks)
+
+    def to_output(parts):
+        whole = jnp.concatenate(parts).astype(jnp.float32)
+        return whole.transpose(1, 0, 2).reshape(shard_rows, shard_count * ff_cols)
+
+    grad_down = jnp.concatenate(sums[:down_cuts]).astype(jnp.float32)
+    grad_gate_w = to_output(sums[down_cuts : down_cuts + col_cuts])
+    grad_up_w = to_output(sums[down_cuts + col_cuts : down_cuts + 2 * col_cuts])
+    grad_out_w = sums[-2].astype(jnp.float32)
+    grad_qkv_w = sums[-1].astype(jnp.float32)
+
+    small = lax.psum(
+        jnp.concatenate([gain_attn_local, gain_mlp_local, bias_local]), ("fsdp", "ctx")
+    )
+
+    def own_part(start, size):
+        part = size // shard_count
+        return lax.dynamic_slice_in_dim(small, start + shard_index * part, part, 0)
+
     return (
         out_tokens,
         grad_tokens,
-        gain_attn_part,
-        grad_qkv,
-        bias_part,
-        grad_outp,
-        gain_mlp_part,
-        grad_mlp[:, 0],
-        grad_mlp[:, 1],
+        own_part(0, width),
+        grad_qkv_w,
+        own_part(2 * width, bias_all.shape[0]),
+        grad_out_w,
+        own_part(width, width),
+        grad_gate_w,
+        grad_up_w,
         grad_down,
     )
 

time: 1730 us -> 995 us (0.58)
  waiting for transfers between devices: 1300 us -> 297 us
  starting transfers between devices: 1.06 us -> 182 us
  local copies, waits for them, and re-layouts: 43.1 us -> 119 us
  other arithmetic: 89.2 us -> 140 us
  matrix products: 215 us -> 176 us
    reduce_scatter x4, waiting for transfers between devices: 514 us -> 0.04 us  [the longest x1 0.02 us: local(): lax.psum_scatter(grad_terms.astype(jnp.bfloat16), 'fsdp', scatter_dimensi...]
    all_gather x5 -> x4, waiting for transfers between devices: 406 us -> 34.4 us  [the longest x1 30 us: local(): qkv_all = lax.all_gather(w_qkv, 'fsdp', axis=0, tiled=True)]
    psum x1 -> x0, waiting for transfers between devices: 336 us -> none  [local(): lax.psum(grad_qkv.astype(jnp.bfloat16), 'ctx').astype(jnp.float32)]
    ppermute x0 -> x36, starting transfers between devices: none -> 158 us  [the longest x13 124 us: ctx_sums(): swapped = lax.ppermute(payload, 'ctx', [(0, 1), (1, 0), (2, 3), (3, 2)])]
    all_to_all x0 -> x4, waiting for transfers between devices: none -> 125 us  [the longest x2 92.8 us: to_columns(): return lax.all_to_all(parts, 'fsdp', 0, 0).reshape(width, ff_cols)]
    ppermute x0 -> x36, waiting for transfers between devices: none -> 119 us  [the longest x13 65.2 us: ctx_sums(): swapped = lax.ppermute(payload, 'ctx', [(0, 1), (1, 0), (2, 3), (3, 2)])]
    reshape x0 -> x8, local copies, waits for them, and re-layouts: none -> 56.2 us  [the longest x4 30 us: to_output(): return whole.transpose(1, 0, 2).reshape(shard_rows, shard_count * ff_cols)]
    unnamed x2 -> x0, blocking collectives: 38.4 us -> none
  transfers between devices with their start and end apart: 12 -> 50, of which waited for: 11 -> 16; matrix products, arithmetic and copies ran while one was open for 12% -> 37% of each run, Pallas kernels for 0% -> 0%
where the time goes in v1:
time: 995 us; the launch traced here: 984 us
  waiting for transfers between devices  297 us (30%)
  starting transfers between devices  182 us (18%)
  matrix products  176 us (18%)
  other arithmetic  140 us (14%)
  local copies, waits for them, and re-layouts  119 us (12%)
  blocking collectives  52.2 us (5%)
  between operations  17.5 us (2%)
    ppermute x13, starting transfers between devices, ctx_sums(): swapped = lax.ppermute(payload, 'ctx', [(0, 1), (1, 0), (2, 3), (3, 2)])  124 us
    all_to_all x2, waiting for transfers between devices, to_columns(): return lax.all_to_all(parts, 'fsdp', 0, 0).reshape(width, ff_cols)  92.8 us
    ppermute x13, waiting for transfers between devices, ctx_sums(): swapped = lax.ppermute(payload, 'ctx', [(0, 1), (1, 0), (2, 3), (3, 2)])  65.2 us
    dot_general x5, matrix products, contract_cols(): lax.dot_general(left_side, right_side, (((1,), (1,)), ((), ())), preferre...  54 us
    ppermute x4, waiting for transfers between devices, ctx_sums(): inward = lax.ppermute(coming, 'ctx', [(0, 1), (3, 2)])  45.7 us
    dot_general x5, matrix products, contract_rows(): lax.dot_general(left_side, right_side, (((0,), (0,)), ((), ())), preferre...  44.1 us
    psum x1, blocking collectives, local(): lax.psum(jnp.concatenate([gain_attn_local, gain_mlp_local, bias_local]),...  41.8 us
    all_to_all x2, waiting for transfers between devices, to_rows(): return lax.all_to_all(parts, 'fsdp', 0, 0)  32.7 us
  transfers between devices with their start and end apart: 50, of which 16 were waited for; matrix products, arithmetic and copies ran while one was open for 37% of the time, Pallas kernels for 0%

profile of v1, /device:TPU:0, one launch (start us, length us, event | category | flops | bytes accessed | tf_op | source)
XLA Modules:
  0.0 983.7 jit_solution(2596103784022047295)
XLA Ops:
  28.1 30.0 %all-gather.8.cloned.1.call-done = bf16[1536,2048]{1,0:T(8,128)(2,1)} async-done(((bf16[192,2048]{1,0:T(8,128)(2,1)}), bf16[1536,2048]{1,0:T(8,128)(2,1)}) %all-gather.8.cloned.1.call-update) | async-done | bytes 6291472 | tf_op jit(solution)/shard_map/all_gather | solution.py:124
  84.8 16.3 %all-gather.10.cloned.1.call-done = bf16[1024,512]{1,0:T(8,128)(2,1)} async-done(((bf16[256,512]{1,0:T(8,128)(2,1)}), bf16[1024,512]{1,0:T(8,128)(2,1)}) %all-gather.10.cloned.1.call-update) | async-done | bytes 1048592 | tf_op jit(solution)/shard_map/all_gather | solution.py:172
  103.4 13.8 %conditional.4 = (f32[256,2,6]{0,2,1:T(8,128)}, f32[256,2,6]{0,2,1:T(8,128)S(1)}, f32[256,2,6,128]{3,0,2,1:T(8,128)}) conditional(s32[]{:T(128)} %convert_element_type.432, () %tuple.46, (s32[512]{0:T(512)S(1)}, s32[256]{0:T(256)S(1)}, bf16[512,512]{1,0:T(8,128)(2,1)}, bf16[256,2,6,128]{0,3,2,1:T(8,128)(2,1)}) %tuple.47), branch_computations={%region_6.7_spmd, %region_7.10_spmd} | conditional | flops 826290176 | bytes 25041972 | solution.py:196
  117.3 14.4 %conditional.5 = (f32[256,2,6]{0,2,1:T(8,128)S(1)}, f32[256,2,6,128]{3,0,2,1:T(8,128)}, f32[256,2,6]{0,2,1:T(8,128)}) conditional(s32[]{:T(128)} %convert_element_type.431, (f32[256,2,6]{0,2,1:T(8,128)}, f32[256,2,6]{0,2,1:T(8,128)S(1)}, f32[256,2,6,128]{3,0,2,1:T(8,128)}) %conditional.4, (s32[512]{0:T(512)S(1)}, s32[256]{0:T(256)S(1)}, ...), branch_computations={%region_10.11_spmd.clone, %region_11.14_spmd.clone} | conditional | flops 826677248 | bytes 26676276 | solution.py:196
  179.5 45.8 %all-to-all-done = bf16[8,192,1120]{2,1,0:T(8,128)(2,1)} async-done(((bf16[8,192,1120]{2,1,0:T(8,128)(2,1)}), bf16[8,192,1120]{2,1,0:T(8,128)(2,1)}, u32[]{:S(2)}, u32[]{:S(2)}) %all-to-all-start) | async-done | bytes 3440672 | tf_op jit(solution)/shard_map/all_to_all | solution.py:132
  230.0 12.9 %fusion.110 = f32[2048,1120]{0,1:T(8,128)} fusion(bf16[2048,1536]{1,0:T(8,128)(2,1)} %all-gather.14.cloned.1.call-done, bf16[1536,1120]{1,0:T(8,128)(2,1)} %bitcast.45), kind=kOutput, calls=%fused_computation.259 | convolution fusion | flops 7046430720 | bytes 18907136 | tf_op jit(solution)/shard_map/dot_general | solution.py:208
  242.9 47.0 %all-to-all-done.1 = bf16[8,192,1120]{2,1,0:T(8,128)(2,1)} async-done(((bf16[8,192,1120]{2,1,0:T(8,128)(2,1)}), bf16[8,192,1120]{2,1,0:T(8,128)(2,1)}, u32[]{:S(2)}, u32[]{:S(2)}) %all-to-all-start.1) | async-done | bytes 3440672 | tf_op jit(solution)/shard_map/all_to_all | solution.py:132
  289.9 12.7 %fusion.111 = f32[2048,1120]{0,1:T(8,128)} fusion(bf16[2048,1536]{1,0:T(8,128)(2,1)} %all-gather.14.cloned.1.call-done, bf16[1536,1120]{1,0:T(8,128)(2,1)} %bitcast.47), kind=kOutput, calls=%fused_computation.260 | convolution fusion | flops 7046430720 | bytes 18907136 | tf_op jit(solution)/shard_map/dot_general | solution.py:209
  302.6 18.2 %multiply_convert_fusion = (bf16[2048,1120]{0,1:T(8,128)(2,1)}, bf16[2048,1120]{0,1:T(8,128)(2,1)}, bf16[2048,1120]{0,1:T(8,128)(2,1)}) fusion(f32[2048,1120]{0,1:T(8,128)} %fusion.110, f32[2048,1120]{0,1:T(8,128)} %fusion.111, bf16[2048,1536]{1,0:T(8,128)(2,1)} %all-gather.16.cloned.1.call-done, bf16[1120,1536]{1,0:T(8,128)(2,1)S(1)} %copy-done), kind=kOutput, calls=%fused_computation.66 | convolution fusion | flops 7080837120 | bytes 41844736 | tf_op jit(solution)/shard_map/dot_general | solution.py:49
  332.5 13.4 %add_convert_fusion = bf16[2048,1536]{1,0:T(8,128)(2,1)} fusion(f32[2048,1536]{1,0:T(8,128)S(1)} %fusion.112, bf16[2048,1120]{0,1:T(8,128)(2,1)} %get-tuple-element.323, bf16[1536,1120]{1,0:T(8,128)(2,1)} %bitcast.47), kind=kOutput, calls=%fused_computation.65 | convolution fusion | flops 7052722176 | bytes 26902528 | tf_op jit(solution)/shard_map/dot_general | solution.py:49
  358.5 12.1 %collective-permute-done.24 = bf16[224,1536]{1,0:T(8,128)(2,1)S(1)} collective-permute-done((bf16[224,1536]{1,0:T(8,128)(2,1)S(1)}, bf16[224,1536]{1,0:T(8,128)(2,1)S(1)}, u32[]{:S(2)}, u32[]{:S(2)}) %collective-permute-start.24) | collective-permute-done | bytes 688160 | tf_op jit(solution)/shard_map/ppermute | solution.py:76
  375.7 14.5 %collective-permute-start.26 = (bf16[224,1536]{1,0:T(8,128)(2,1)}, bf16[224,1536]{1,0:T(8,128)(2,1)}, u32[]{:S(2)}, u32[]{:S(2)}) collective-permute-start(bf16[224,1536]{1,0:T(8,128)(2,1)} %broadcast_select_fusion.16), channel_id=1, source_target_pairs={{0,1},{1,0},{2,3},{3,2},{4,5},{5,4},{6,7},{7,6},{8,9},{9,8},{10,11... | collective-permute-start | bytes 2064392 | tf_op jit(solution)/shard_map/ppermute | solution.py:76
  390.2 12.6 %convolution_convert_fusion = bf16[2048,1536]{1,0:T(8,128)(2,1)} fusion(bf16[2048,1120]{0,1:T(8,128)(2,1)} %get-tuple-element.325, bf16[1120,1536]{1,0:T(8,128)(2,1)S(1)} %copy-done), kind=kOutput, calls=%fused_computation.71 | convolution fusion | flops 7049576448 | bytes 14319616 | tf_op jit(solution)/shard_map/dot_general | solution.py:229
  460.5 32.7 %all-to-all-done.2 = bf16[8,192,1120]{2,1,0:T(8,128)(2,1)} async-done(((bf16[8,192,1120]{2,1,0:T(8,128)(2,1)}), bf16[8,192,1120]{2,1,0:T(8,128)(2,1)}, u32[]{:S(2)}, u32[]{:S(2)}) %all-to-all-start.2) | async-done | bytes 3440672 | tf_op jit(solution)/shard_map/all_to_all | solution.py:225
  508.3 13.4 %collective-permute-done.6 = bf16[2,192,1120]{2,1,0:T(8,128)(2,1)S(1)} collective-permute-done((bf16[2,192,1120]{2,1,0:T(8,128)(2,1)S(1)}, bf16[2,192,1120]{2,1,0:T(8,128)(2,1)S(1)}, u32[]{:S(2)}, u32[]{:S(2)}) %collective-permute-start.6) | collective-permute-done | bytes 860192 | tf_op jit(solution)/shard_map/ppermute | solution.py:79
  559.8 18.3 %conditional.7 = (f32[1024,512]{0,1:T(8,128)}, f32[256,2,6,128]{0,3,2,1:T(8,128)}) conditional(s32[]{:T(128)} %convert_element_type.431, (f32[256,2,6,128]{3,0,2,1:T(8,128)S(1)}, f32[1024,512]{0,1:T(8,128)}) %conditional.6, (s32[512]{0:T(512)S(1)}, s32[256]{0:T(256)S(1)}, bf16[512,512]{1,0:T(8,128)(2,1)}, bf16[256,2,6,128]{0,3,2,1:T(8,128)(2,1)S(1)}, ...), branch_computations={%region_21.22_spmd, %region_22.23_spmd} | conditional | flops 2034761728 | bytes 48405548 | solution.py:292
  643.9 34.2 %collective-permute-start.13 = (bf16[2,192,1120]{2,1,0:T(8,128)(2,1)S(1)}, bf16[2,192,1120]{2,1,0:T(8,128)(2,1)S(1)}, u32[]{:S(2)}, u32[]{:S(2)}) collective-permute-start(bf16[2,192,1120]{2,1,0:T(8,128)(2,1)S(1)} %broadcast_select_fusion.9), channel_id=1, source_target_pairs={{0,1},{1,0},{2,3},{3,2},{4,5},{5,4},{6,7},{7,6},{8,9},{9,8},{10,11... | collective-permute-start | bytes 2580488 | tf_op jit(solution)/shard_map/ppermute | solution.py:76
  680.1 14.5 %collective-permute-start.11 = (bf16[2,192,1120]{2,1,0:T(8,128)(2,1)S(1)}, bf16[2,192,1120]{2,1,0:T(8,128)(2,1)S(1)}, u32[]{:S(2)}, u32[]{:S(2)}) collective-permute-start(bf16[2,192,1120]{2,1,0:T(8,128)(2,1)S(1)} %broadcast_select_fusion.11), channel_id=1, source_target_pairs={{0,1},{1,0},{2,3},{3,2},{4,5},{5,4},{6,7},{7,6},{8,9},{9,8},{10,11... | collective-permute-start | bytes 2580488 | tf_op jit(solution)/shard_map/ppermute | solution.py:76
  754.5 16.9 %collective-permute-done.15 = bf16[2,192,1120]{2,1,0:T(8,128)(2,1)S(1)} collective-permute-done((bf16[2,192,1120]{2,1,0:T(8,128)(2,1)S(1)}, bf16[2,192,1120]{2,1,0:T(8,128)(2,1)S(1)}, u32[]{:S(2)}, u32[]{:S(2)}) %collective-permute-start.15) | collective-permute-done | bytes 860192 | tf_op jit(solution)/shard_map/ppermute | solution.py:76
  771.4 13.5 %collective-permute-done.17 = bf16[2,192,1120]{2,1,0:T(8,128)(2,1)S(1)} collective-permute-done((bf16[2,192,1120]{2,1,0:T(8,128)(2,1)S(1)}, bf16[2,192,1120]{2,1,0:T(8,128)(2,1)S(1)}, u32[]{:S(2)}, u32[]{:S(2)}) %collective-permute-start.17) | collective-permute-done | bytes 860192 | tf_op jit(solution)/shard_map/ppermute | solution.py:76
  795.7 20.3 %collective-permute-start.19 = (bf16[2,192,1120]{2,1,0:T(8,128)(2,1)}, bf16[2,192,1120]{2,1,0:T(8,128)(2,1)}, u32[]{:S(2)}, u32[]{:S(2)}) collective-permute-start(bf16[2,192,1120]{2,1,0:T(8,128)(2,1)} %broadcast_select_fusion.3), channel_id=1, source_target_pairs={{0,1},{1,0},{2,3},{3,2},{4,5},{5,4},{6,7},{7,6},{8,9},{9,8},{10,11... | collective-permute-start | bytes 2580488 | tf_op jit(solution)/shard_map/ppermute | solution.py:76
  857.2 41.8 %psum.7 = f32[5120]{0:T(1024)S(1)} all-reduce(f32[5120]{0:T(1024)S(1)} %pad_maximum_fusion.5), channel_id=1, replica_groups=mesh['fsdp'=8,'ctx'=4] {'fsdp','ctx'}, use_global_device_ids=true, to_apply=%region_28.29 | all-reduce | flops 5120 | bytes 40960 | tf_op jit(solution)/shard_map/psum | solution.py:347
  919.5 13.0 %collective-permute-done = bf16[192,2048]{1,0:T(8,128)(2,1)S(1)} collective-permute-done((bf16[192,2048]{1,0:T(8,128)(2,1)}, bf16[192,2048]{1,0:T(8,128)(2,1)S(1)}, u32[]{:S(2)}, u32[]{:S(2)}) %collective-permute-start) | collective-permute-done | bytes 786464 | tf_op jit(solution)/shard_map/ppermute | solution.py:79
  940.5 15.6 %collective-permute-start.2 = (bf16[192,2048]{1,0:T(8,128)(2,1)}, bf16[192,2048]{1,0:T(8,128)(2,1)}, u32[]{:S(2)}, u32[]{:S(2)}) collective-permute-start(bf16[192,2048]{1,0:T(8,128)(2,1)} %add_convert_fusion.17), channel_id=1, source_target_pairs={{0,1},{1,0},{2,3},{3,2},{4,5},{5,4},{6,7},{7,6},{8,9},{9,8},{10,11... | collective-permute-start | bytes 2359304 | tf_op jit(solution)/shard_map/ppermute | solution.py:76
  (397 shorter events, 525.3 us)
Async XLA Ops:
  7.2 51.0 %all-gather.8.cloned.1.call-start = ((), (), s32[]{:S(2)}) async-start(), calls=%async_computation.9 | async-start | bytes 7077888 | tf_op jit(solution)/shard_map/all_gather | solution.py:124
  7.9 93.2 %all-gather.10.cloned.1.call-start = ((), (), s32[]{:S(2)}) async-start(), calls=%async_computation.10 | async-start | bytes 1310720 | tf_op jit(solution)/shard_map/all_gather | solution.py:172
  73.1 68.4 %all-gather.12.cloned.1.call-start = ((), (), s32[]{:S(2)}) async-start(), calls=%async_computation.11 | async-start | bytes 5308416 | tf_op jit(solution)/shard_map/all_gather | solution.py:136
  73.8 156.2 %all-gather.14.cloned.1.call-start = ((), (), s32[]{:S(2)}) async-start(), calls=%async_computation.12 | async-start | bytes 7077888 | tf_op jit(solution)/shard_map/all_gather | solution.py:207
  148.1 154.5 %all-gather.16.cloned.1.call-start = ((), (), s32[]{:S(2)}) async-start(), calls=%async_computation.14 | async-start | bytes 7077888 | tf_op jit(solution)/shard_map/all_gather | solution.py:137
  161.8 63.4 %all-to-all-start = ((bf16[8,192,1120]{2,1,0:T(8,128)(2,1)}), bf16[8,192,1120]{2,1,0:T(8,128)(2,1)}, u32[]{:S(2)}, u32[]{:S(2)}) async-start(bf16[8,192,1120]{2,1,0:T(8,128)(2,1)} %bitcast.251), calls=%async_computation | async-start | bytes 7077888 | tf_op jit(solution)/shard_map/all_to_all | solution.py:132
  225.2 64.7 %all-to-all-start.1 = ((bf16[8,192,1120]{2,1,0:T(8,128)(2,1)}), bf16[8,192,1120]{2,1,0:T(8,128)(2,1)}, u32[]{:S(2)}, u32[]{:S(2)}) async-start(bf16[8,192,1120]{2,1,0:T(8,128)(2,1)} %bitcast.250), calls=%async_computation.1 | async-start | bytes 7077888 | tf_op jit(solution)/shard_map/all_to_all | solution.py:132
  229.7 304.6 %reduce-scatter.8.cloned.1.call-start = ((), (), s32[]{:S(2)}) async-start(), calls=%async_computation.15 | async-start | bytes 7077888 | tf_op jit(solution)/shard_map/reduce_scatter | solution.py:218
  346.0 189.9 %reduce-scatter.6.cloned.1.call-start = ((), (), s32[]{:S(2)}) async-start(), calls=%async_computation.13 | async-start | bytes 7077888 | tf_op jit(solution)/shard_map/reduce_scatter | solution.py:230
  426.5 66.7 %all-to-all-start.2 = ((bf16[8,192,1120]{2,1,0:T(8,128)(2,1)}), bf16[8,192,1120]{2,1,0:T(8,128)(2,1)}, u32[]{:S(2)}, u32[]{:S(2)}) async-start(bf16[8,192,1120]{2,1,0:T(8,128)(2,1)} %bitcast.253), calls=%async_computation.7 | async-start | bytes 7077888 | tf_op jit(solution)/shard_map/all_to_all | solution.py:225
  439.2 63.2 %collective-permute-start.31 = (bf16[224,1536]{1,0:T(8,128)(2,1)}, bf16[224,1536]{1,0:T(8,128)(2,1)}, u32[]{:S(2)}, u32[]{:S(2)}) collective-permute-start(bf16[224,1536]{1,0:T(8,128)(2,1)} %get-tuple-element.336), channel_id=1, source_target_pairs={{0,1},{1,0},{2,3},{3,2},{4,5},{5,4},{6,7},{7,6},{8,9},{9,8},{10,11... | collective-permute-start | bytes 2064392 | tf_op jit(solution)/shard_map/ppermute | solution.py:76
  442.7 59.7 %collective-permute-start.27 = (bf16[224,1536]{1,0:T(8,128)(2,1)}, bf16[224,1536]{1,0:T(8,128)(2,1)}, u32[]{:S(2)}, u32[]{:S(2)}) collective-permute-start(bf16[224,1536]{1,0:T(8,128)(2,1)} %get-tuple-element.337), channel_id=1, source_target_pairs={{0,1},{1,0},{2,3},{3,2},{4,5},{5,4},{6,7},{7,6},{8,9},{9,8},{10,11... | collective-permute-start | bytes 2064392 | tf_op jit(solution)/shard_map/ppermute | solution.py:76
  493.2 148.4 %all-to-all-start.3 = ((bf16[8,192,1120]{2,1,0:T(8,128)(2,1)}), bf16[8,192,1120]{2,1,0:T(8,128)(2,1)}, u32[]{:S(2)}, u32[]{:S(2)}) async-start(bf16[8,192,1120]{2,1,0:T(8,128)(2,1)} %bitcast.252), calls=%async_computation.8 | async-start | bytes 7077888 | tf_op jit(solution)/shard_map/all_to_all | solution.py:225
  497.7 220.9 %reduce-scatter.10.cloned.1.call-start = ((), (), s32[]{:S(2)}) async-start(), calls=%async_computation.16 | async-start | bytes 1310720 | tf_op jit(solution)/shard_map/reduce_scatter | solution.py:296
  523.2 57.6 %collective-permute-start.7 = (bf16[2,192,1120]{2,1,0:T(8,128)(2,1)S(1)}, bf16[2,192,1120]{2,1,0:T(8,128)(2,1)}, u32[]{:S(2)}, u32[]{:S(2)}) collective-permute-start(bf16[2,192,1120]{2,1,0:T(8,128)(2,1)S(1)} %add_convert_fusion.16), channel_id=1, source_target_pairs={{1,2},{2,1},{5,6},{6,5},{9,10},{10,9},{13,14},{14,13},{17,18},{18,... | collective-permute-start | bytes 2580488 | tf_op jit(solution)/shard_map/ppermute | solution.py:85
  527.7 66.5 %collective-permute-start.29 = (bf16[224,1536]{1,0:T(8,128)(2,1)}, bf16[224,1536]{1,0:T(8,128)(2,1)}, u32[]{:S(2)}, u32[]{:S(2)}) collective-permute-start(bf16[224,1536]{1,0:T(8,128)(2,1)} %broadcast_select_fusion.15), channel_id=1, source_target_pairs={{0,1},{1,0},{2,3},{3,2},{4,5},{5,4},{6,7},{7,6},{8,9},{9,8},{10,11... | collective-permute-start | bytes 2064392 | tf_op jit(solution)/shard_map/ppermute | solution.py:76
  533.0 201.8 %collective-permute-start.35 = (bf16[224,1536]{1,0:T(8,128)(2,1)}, bf16[224,1536]{1,0:T(8,128)(2,1)}, u32[]{:S(2)}, u32[]{:S(2)}) collective-permute-start(bf16[224,1536]{1,0:T(8,128)(2,1)} %add_convert_fusion.20), channel_id=1, source_target_pairs={{1,0},{2,3},{5,4},{6,7},{9,8},{10,11},{13,12},{14,15},{17,16},{18,... | collective-permute-start | bytes 2064392 | tf_op jit(solution)/shard_map/ppermute | solution.py:80
  580.7 321.0 %reduce-scatter.14.cloned.1.call-start = ((), (), s32[]{:S(2)}) async-start(), calls=%async_computation.18 | async-start | bytes 5308416 | tf_op jit(solution)/shard_map/reduce_scatter | solution.py:322
  603.9 300.9 %reduce-scatter.12.cloned.1.call-start = ((), (), s32[]{:S(2)}) async-start(), calls=%async_computation.17 | async-start | bytes 7077888 | tf_op jit(solution)/shard_map/reduce_scatter | solution.py:322
  635.8 58.7 %collective-permute-start.33 = (bf16[224,1536]{1,0:T(8,128)(2,1)S(1)}, bf16[224,1536]{1,0:T(8,128)(2,1)}, u32[]{:S(2)}, u32[]{:S(2)}) collective-permute-start(bf16[224,1536]{1,0:T(8,128)(2,1)S(1)} %add_convert_fusion.22), channel_id=1, source_target_pairs={{1,0},{2,3},{5,4},{6,7},{9,8},{10,11},{13,12},{14,15},{17,16},{18,... | collective-permute-start | bytes 2064392 | tf_op jit(solution)/shard_map/ppermute | solution.py:80
  637.1 40.9 %collective-permute-start.10 = (bf16[2,192,1120]{2,1,0:T(8,128)(2,1)}, bf16[2,192,1120]{2,1,0:T(8,128)(2,1)}, u32[]{:S(2)}, u32[]{:S(2)}) collective-permute-start(bf16[2,192,1120]{2,1,0:T(8,128)(2,1)} %get-tuple-element.331), channel_id=1, source_target_pairs={{1,2},{2,1},{5,6},{6,5},{9,10},{10,9},{13,14},{14,13},{17,18},{18,... | collective-permute-start | bytes 2580488 | tf_op jit(solution)/shard_map/ppermute | solution.py:85
  643.9 52.8 %collective-permute-start.13 = (bf16[2,192,1120]{2,1,0:T(8,128)(2,1)S(1)}, bf16[2,192,1120]{2,1,0:T(8,128)(2,1)S(1)}, u32[]{:S(2)}, u32[]{:S(2)}) collective-permute-start(bf16[2,192,1120]{2,1,0:T(8,128)(2,1)S(1)} %broadcast_select_fusion.9), channel_id=1, source_target_pairs={{0,1},{1,0},{2,3},{3,2},{4,5},{5,4},{6,7},{7,6},{8,9},{9,8},{10,11... | collective-permute-start | bytes 2580488 | tf_op jit(solution)/shard_map/ppermute | solution.py:76
  699.3 43.7 %collective-permute-start.16 = (bf16[2,192,1120]{2,1,0:T(8,128)(2,1)}, bf16[2,192,1120]{2,1,0:T(8,128)(2,1)}, u32[]{:S(2)}, u32[]{:S(2)}) collective-permute-start(bf16[2,192,1120]{2,1,0:T(8,128)(2,1)} %add_convert_fusion.8), channel_id=1, source_target_pairs={{1,2},{2,1},{5,6},{6,5},{9,10},{10,9},{13,14},{14,13},{17,18},{18,... | collective-permute-start | bytes 2580488 | tf_op jit(solution)/shard_map/ppermute | solution.py:85
  837.0 69.4 %collective-permute-start.22 = (bf16[2,192,1120]{2,1,0:T(8,128)(2,1)}, bf16[2,192,1120]{2,1,0:T(8,128)(2,1)}, u32[]{:S(2)}, u32[]{:S(2)}) collective-permute-start(bf16[2,192,1120]{2,1,0:T(8,128)(2,1)} %add_convert_fusion.2), channel_id=1, source_target_pairs={{1,2},{2,1},{5,6},{6,5},{9,10},{10,9},{13,14},{14,13},{17,18},{18,... | collective-permute-start | bytes 2580488 | tf_op jit(solution)/shard_map/ppermute | solution.py:85
  (93 other events, 1981.2 us)
Sparse Core Ops, SparseCore 0:
  9.9 48.2 all-gather.7
  73.2 27.9 all-gather.9
  103.1 38.3 all-gather.11
  148.2 68.3 all-gather.13
  218.3 79.5 all-gather.15
  346.1 61.0 reduce-scatter.7
  411.5 104.3 reduce-scatter.5
  580.8 49.2 reduce-scatter.9
  633.9 53.3 reduce-scatter.13
  734.9 62.2 reduce-scatter.11

commit v2 on v0

v2 whole, which is shorter than its diff:
```python
import jax
import jax.numpy as jnp
from jax import lax
from jax.experimental import pallas as pl
from jax.experimental.pallas import tpu as pltpu
from jax.sharding import PartitionSpec as P

HEADS = 12
KV_HEADS = 2
HEAD = 128
GROUP = HEADS // KV_HEADS
Q_WIDTH = HEADS * HEAD
K_WIDTH = KV_HEADS * HEAD

norm_eps = 1e-06
rope_base = 1000000.0
masked_score = -1e30
score_scale = HEAD ** (-0.5)
score_scale_two = score_scale * 1.4426950408889634
bf16 = jnp.bfloat16
f32 = jnp.float32
light = pl.CostEstimate(flops=1 << 20, bytes_accessed=1 << 16, transcendentals=0)


def dot(left_side, right_side, left_dim, right_dim):
    return lax.dot_general(
        left_side,
        right_side,
        (((left_dim,), (right_dim,)), ((), ())),
        preferred_element_type=f32,
    )


def kernel_params(mib):
    return pltpu.CompilerParams(vmem_limit_bytes=mib * 1024 * 1024)


def padded(size):
    return (size + 127) // 128 * 128


def whole(shape):
    return pl.BlockSpec(shape, lambda *_: (0,) * len(shape))


def split_columns(weight, shard_count):
    rows, width = weight.shape
    cols = width // shard_count
    full = padded(cols)
    step = 48 if rows % 48 == 0 else rows

    def kernel(in_ref, out_ref):
        for shard in range(shard_count):
            out_ref[shard, :, :cols] = in_ref[:, shard * cols : (shard + 1) * cols]
            if full > cols:
                out_ref[shard, :, cols:] = jnp.zeros((step, full - cols), weight.dtype)

    return pl.pallas_call(
        kernel,
        grid=(rows // step,),
        in_specs=[pl.BlockSpec((step, width), lambda i: (i, 0))],
        out_specs=pl.BlockSpec((shard_count, step, full), lambda i: (0, i, 0)),
        out_shape=jax.ShapeDtypeStruct((shard_count, rows, full), weight.dtype),
        compiler_params=kernel_params(32),
        cost_estimate=light,
    )(weight)


def merge_columns(parts, cols):
    shards, rows, full = parts.shape
    width = shards * cols
    step = 48 if rows % 48 == 0 else rows

    def kernel(in_ref, out_ref):
        for shard in range(shards):
            part = in_ref[shard, :, :cols]
            out_ref[:, shard * cols : (shard + 1) * cols] = part.astype(f32)

    return pl.pallas_call(
        kernel,
        grid=(rows // step,),
        in_specs=[pl.BlockSpec((shards, step, full), lambda i: (0, i, 0))],
        out_specs=pl.BlockSpec((step, width), lambda i: (i, 0)),
        out_shape=jax.ShapeDtypeStruct((rows, width), f32),
        compiler_params=kernel_params(40),
        cost_estimate=light,
    )(parts)


def project(tokens_in, gain, weights, bias, cosine, sine):
    rows, width = tokens_in.shape
    tile = K_WIDTH
    query_steps = Q_WIDTH // tile

    def kernel(x_ref, gain_ref, w_ref, bias_ref, cos_ref, sin_ref, normed_ref, q_ref, kv_ref):
        step = pl.program_id(0)

        @pl.when(step == 0)
        def _():
            source = x_ref[...].astype(f32)
            scale = lax.rsqrt(jnp.mean(source * source, -1, keepdims=True) + norm_eps)
            normed_ref[...] = (source * scale * gain_ref[...]).astype(bf16)

        out = dot(normed_ref[...], w_ref[...], 1, 0) + bias_ref[...]
        heads = []
        for head in range(tile // HEAD):
            part = out[:, head * HEAD : (head + 1) * HEAD]
            turned = part * cos_ref[...] + pltpu.roll(part, HEAD // 2, 1) * sin_ref[...]
            heads.append(jnp.where(step <= query_steps, turned, part).astype(bf16))

        @pl.when(step < query_steps)
        def _():
            for head, value in enumerate(heads):
                q_ref[:, head * HEAD : (head + 1) * HEAD] = value

        @pl.when(step >= query_steps)
        def _():
            for head, value in enumerate(heads):
                kv_ref[:, head * HEAD : (head + 1) * HEAD] = value

    return pl.pallas_call(
        kernel,
        grid=(query_steps + 2,),
        in_specs=[
            whole((rows, width)),
            whole((1, width)),
            pl.BlockSpec((width, tile), lambda i: (0, i)),
            pl.BlockSpec((1, tile), lambda i: (0, i)),
            whole((rows, HEAD)),
            whole((rows, HEAD)),
        ],
        out_specs=[
            whole((rows, width)),
            pl.BlockSpec((rows, tile), lambda i: (0, jnp.minimum(i, query_steps - 1))),
            pl.BlockSpec((rows, tile), lambda i: (0, jnp.maximum(i - query_steps, 0))),
        ],
        out_shape=[
            jax.ShapeDtypeStruct((rows, width), bf16),
            jax.ShapeDtypeStruct((rows, Q_WIDTH), bf16),
            jax.ShapeDtypeStruct((rows, 2 * K_WIDTH), bf16),
        ],
        compiler_params=kernel_params(32),
        cost_estimate=light,
    )(tokens_in, gain, weights, bias, cosine, sine)


def fill_bias(info_ref, bias_ref, count, rows):
    query_pos = info_ref[0] * rows + lax.broadcasted_iota(jnp.int32, (rows, rows), 1)
    for piece in range(count):
        key_pos = info_ref[1 + piece] * rows + lax.broadcasted_iota(jnp.int32, (rows, rows), 0)
        bias_ref[piece * rows : (piece + 1) * rows, :] = jnp.where(
            key_pos <= query_pos, 0.0, masked_score
        )


def attend(info, query, kv_pieces):
    rows = query.shape[0]
    count = len(kv_pieces)

    def kernel(info_ref, q_ref, *refs):
        keys, values = refs[:count], refs[count : 2 * count]
        mixed_ref, total_ref, bias_ref, score_ref = refs[2 * count :]

        @pl.when(pl.program_id(0) == 0)
        def _():
            fill_bias(info_ref, bias_ref, count, rows)

        q = q_ref[...]
        top = None
        for piece in range(count):
            at = slice(piece * rows, (piece + 1) * rows)
            score = dot(keys[piece][...], q, 1, 1) * score_scale_two + bias_ref[at, :]
            score_ref[at, :] = score
            peak = jnp.max(score, 0, keepdims=True)
            top = peak if top is None else jnp.maximum(top, peak)
        total = jnp.zeros((1, rows), f32)
        mixed = jnp.zeros((HEAD, rows), f32)
        for piece in range(count):
            weight = jnp.exp2(score_ref[piece * rows : (piece + 1) * rows, :] - top)
            total += jnp.sum(weight, 0, keepdims=True)
            mixed += dot(values[piece][...], weight.astype(bf16), 0, 0)
        mixed_ref[...] = (mixed / total).T.astype(bf16)
        total_ref[0] = top + jnp.log2(total)

    key_spec = pl.BlockSpec((rows, HEAD), lambda h: (0, h // GROUP))
    value_spec = pl.BlockSpec((rows, HEAD), lambda h: (0, KV_HEADS + h // GROUP))
    head_spec = pl.BlockSpec((rows, HEAD), lambda h: (0, h))
    return pl.pallas_call(
        kernel,
        grid=(HEADS,),
        in_specs=[pl.BlockSpec(memory_space=pltpu.SMEM), head_spec]
        + [key_spec] * count
        + [value_spec] * count,
        out_specs=[head_spec, pl.BlockSpec((1, 1, rows), lambda h: (h, 0, 0))],
        out_shape=[
            jax.ShapeDtypeStruct((rows, Q_WIDTH), bf16),
            jax.ShapeDtypeStruct((HEADS, 1, rows), f32),
        ],
        scratch_shapes=[pltpu.VMEM((count * rows, rows), f32)] * 2,
        compiler_params=kernel_params(32),
        cost_estimate=light,
    )(info, query, *kv_pieces, *kv_pieces)


def attend_back(info, query, grad_mixed, totals, cosine, sine, kv_pieces):
    rows = query.shape[0]
    count = len(kv_pieces)

    def kernel(info_ref, q_ref, g_ref, total_ref, cos_ref, sin_ref, *refs):
        keys, values = refs[:count], refs[count : 2 * count]
        dq_ref = refs[2 * count]
        kv_refs = refs[2 * count + 1 : 3 * count + 1]
        bias_ref, p_ref, dp_ref, sum_ref = refs[3 * count + 1 :]
        head = pl.program_id(0)

        @pl.when(head == 0)
        def _():
            fill_bias(info_ref, bias_ref, count, rows)

        @pl.when(head % GROUP == 0)
        def _():
            sum_ref[...] = jnp.zeros_like(sum_ref)

        q, g, total = q_ref[...], g_ref[...], total_ref[0]
        delta = jnp.zeros((1, rows), f32)
        for piece in range(count):
            at = slice(piece * rows, (piece + 1) * rows)
            score = dot(keys[piece][...], q, 1, 1) * score_scale_two + bias_ref[at, :]
            p = jnp.exp2(score - total)
            dp = dot(values[piece][...], g, 1, 1)
            p_ref[at, :] = p
            dp_ref[at, :] = dp
            delta += jnp.sum(p * dp, 0, keepdims=True)
        dq = jnp.zeros((HEAD, rows), f32)
        for piece in range(count):
            at = slice(piece * rows, (piece + 1) * rows)
            p = p_ref[at, :]
            ds = (p * (dp_ref[at, :] - delta) * score_scale).astype(bf16)
            dq += dot(keys[piece][...], ds, 0, 0)
            sum_ref[piece, 0] += dot(ds, q, 1, 0)
            sum_ref[piece, 1] += dot(p.astype(bf16), g, 1, 0)
        dq = dq.T
        dq_ref[...] = (dq * cos_ref[...] - pltpu.roll(dq, HEAD // 2, 1) * sin_ref[...]).astype(bf16)

        @pl.when(head % GROUP == GROUP - 1)
        def _():
            for piece in range(count):
                kv_refs[piece][...] = sum_ref[piece].astype(bf16)

    key_spec = pl.BlockSpec((rows, HEAD), lambda h: (0, h // GROUP))
    value_spec = pl.BlockSpec((rows, HEAD), lambda h: (0, KV_HEADS + h // GROUP))
    head_spec = pl.BlockSpec((rows, HEAD), lambda h: (0, h))
    return pl.pallas_call(
        kernel,
        grid=(HEADS,),
        in_specs=[
            pl.BlockSpec(memory_space=pltpu.SMEM),
            head_spec,
            head_spec,
            pl.BlockSpec((1, 1, rows), lambda h: (h, 0, 0)),
            whole((rows, HEAD)),
            whole((rows, HEAD)),
        ]
        + [key_spec] * count
        + [value_spec] * count,
        out_specs=[head_spec]
        + [pl.BlockSpec((2, rows, HEAD), lambda h: (0, 0, h // GROUP))] * count,
        out_shape=[jax.ShapeDtypeStruct((rows, Q_WIDTH), bf16)]
        + [jax.ShapeDtypeStruct((2, rows, K_WIDTH), bf16)] * count,
        scratch_shapes=[pltpu.VMEM((count * rows, rows), f32)] * 3
        + [pltpu.VMEM((count, 2, rows, HEAD), f32)],
        compiler_params=kernel_params(32),
        cost_estimate=light,
    )(info, query, grad_mixed, totals, cosine, sine, *kv_pieces, *kv_pieces)


def once(shape):
    return pl.BlockSpec(shape, lambda *_: (0,) * len(shape), pipeline_mode=pl.Buffered(1))


def token_rows(count, rows):
    return 2 * rows if count % (2 * rows) == 0 else rows


def feed_forward(normed, cotangent, gate_cols, up_cols, units_here, rows, cuts):
    count, width = normed.shape
    units = gate_cols.shape[1]
    rows = token_rows(count, rows)
    steps, part, tile = count // rows, units_here // cuts, 256

    def kernel(x_ref, c_ref, wg_ref, wu_ref, act_ref, to_gate_ref, to_up_ref, *refs):
        down_refs, turned_ref = refs[:cuts], refs[cuts]
        step = pl.program_id(0)

        @pl.when(step < steps)
        def _():
            x = x_ref[...]
            gate = dot(x, wg_ref[...], 1, 0)
            up = dot(x, wu_ref[...], 1, 0)
            sigmoid = jax.nn.sigmoid(gate)
            swished = gate * sigmoid
            act = (swished * up).astype(bf16)
            act_ref[...] = act
            turned_ref[:, pl.ds(pl.multiple_of(step * rows, rows), rows)] = act.T
            to_up_ref[...] = swished.astype(bf16)
            to_gate_ref[...] = (up * sigmoid * (1.0 + gate * (1.0 - sigmoid))).astype(bf16)

        @pl.when(step >= steps)
        def _():
            for cut, down_ref in enumerate(down_refs):
                turned = turned_ref[cut * part : (cut + 1) * part, :]
                down_ref[...] = dot(turned, c_ref[...], 1, 0).astype(bf16)

    def early(i):
        return (jnp.minimum(i, steps - 1), 0)

    def late(i):
        return (0, jnp.maximum(i - steps, 0))

    return pl.pallas_call(
        kernel,
        grid=(steps + width // tile,),
        in_specs=[
            pl.BlockSpec((rows, width), early),
            pl.BlockSpec((count, tile), late),
            once((width, units)),
            once((width, units)),
        ],
        out_specs=[pl.BlockSpec((rows, units), early)] * 3 + [pl.BlockSpec((part, tile), late)] * cuts,
        out_shape=[jax.ShapeDtypeStruct((count, units), bf16)] * 3
        + [jax.ShapeDtypeStruct((part, width), bf16)] * cuts,
        scratch_shapes=[pltpu.VMEM((units, count), bf16)],
        compiler_params=kernel_params(58),
        cost_estimate=light,
    )(normed, cotangent, gate_cols, up_cols)


def unit_grads(cotangent, down_rows, to_gate, to_up, rows):
    count, width = cotangent.shape
    units = down_rows.shape[0]
    rows = token_rows(count, rows)

    def kernel(c_ref, wd_ref, tg_ref, tu_ref, dg_ref, du_ref):
        grad_act = dot(c_ref[...], wd_ref[...], 1, 1)
        dg_ref[...] = (grad_act * tg_ref[...].astype(f32)).astype(bf16)
        du_ref[...] = (grad_act * tu_ref[...].astype(f32)).astype(bf16)

    unit_spec = pl.BlockSpec((rows, units), lambda i: (i, 0))
    return pl.pallas_call(
        kernel,
        grid=(count // rows,),
        in_specs=[
            pl.BlockSpec((rows, width), lambda i: (i, 0)),
            once((units, width)),
            unit_spec,
            unit_spec,
        ],
        out_specs=[unit_spec] * 2,
        out_shape=[jax.ShapeDtypeStruct((count, units), bf16)] * 2,
        compiler_params=kernel_params(58),
        cost_estimate=light,
    )(cotangent, down_rows, to_gate, to_up)


def through_columns(grad_gate, grad_up, gate_cols, up_cols, rows):
    count, units = grad_gate.shape
    width = gate_cols.shape[0]
    rows = token_rows(count, rows)

    def kernel(dg_ref, du_ref, wg_ref, wu_ref, out_ref):
        out = dot(dg_ref[...], wg_ref[...], 1, 1) + dot(du_ref[...], wu_ref[...], 1, 1)
        out_ref[...] = out.astype(bf16)

    unit_spec = pl.BlockSpec((rows, units), lambda i: (i, 0))
    return pl.pallas_call(
        kernel,
        grid=(count // rows,),
        in_specs=[unit_spec, unit_spec, once((width, units)), once((width, units))],
        out_specs=pl.BlockSpec((rows, width), lambda i: (i, 0)),
        out_shape=jax.ShapeDtypeStruct((count, width), bf16),
        compiler_params=kernel_params(58),
        cost_estimate=light,
    )(grad_gate, grad_up, gate_cols, up_cols)


def column_grad(normed, grad, cuts):
    count, width = normed.shape
    units = grad.shape[1]
    tile = 256
    each = width // tile // cuts

    def kernel(x_ref, g_ref, *out_refs):
        step = pl.program_id(0)
        out = dot(x_ref[...].T, g_ref[...], 1, 0).astype(bf16)
        for cut, out_ref in enumerate(out_refs):

            @pl.when(step // each == cut)
            def _():
                out_ref[...] = out

    def cut_spec(cut):
        return pl.BlockSpec((tile, units), lambda i: (jnp.clip(i - cut * each, 0, each - 1), 0))

    return pl.pallas_call(
        kernel,
        grid=(width // tile,),
        in_specs=[pl.BlockSpec((count, tile), lambda i: (0, i)), once((count, units))],
        out_specs=[cut_spec(cut) for cut in range(cuts)],
        out_shape=[jax.ShapeDtypeStruct((width // cuts, units), bf16)] * cuts,
        compiler_params=kernel_params(58),
        cost_estimate=light,
    )(normed, grad)


def through_rows(activation, down_rows, rows):
    count, units = activation.shape
    width = down_rows.shape[1]
    rows = token_rows(count, rows)

    def kernel(act_ref, wd_ref, out_ref):
        out_ref[...] = dot(act_ref[...], wd_ref[...], 1, 0).astype(bf16)

    return pl.pallas_call(
        kernel,
        grid=(count // rows,),
        in_specs=[pl.BlockSpec((rows, units), lambda i: (i, 0)), once((units, width))],
        out_specs=pl.BlockSpec((rows, width), lambda i: (i, 0)),
        out_shape=jax.ShapeDtypeStruct((count, width), bf16),
        compiler_params=kernel_params(58),
        cost_estimate=light,
    )(activation, down_rows)


def rotary(positions):
    half = HEAD // 2
    frequency = rope_base ** (-(jnp.arange(half, dtype=f32) * 2.0) / HEAD)
    angles = positions.astype(f32)[:, None] * frequency[None, :]
    cosine, sine = jnp.cos(angles), jnp.sin(angles)
    return jnp.concatenate([cosine, cosine], 1), jnp.concatenate([-sine, sine], 1)


def fence(*values):
    return lax.optimization_barrier(values)


def added(left_side, right_side):
    def kernel(a_ref, b_ref, out_ref):
        out_ref[...] = (a_ref[...].astype(f32) + b_ref[...].astype(f32)).astype(out_ref.dtype)

    def one(a, b):
        steps = [n for n in (4, 5, 3, 2) if a.ndim == 2 and a.shape[0] % (16 * n) == 0]
        if not steps:
            return (a.astype(f32) + b.astype(f32)).astype(a.dtype)
        block = pl.BlockSpec((a.shape[0] // steps[0], a.shape[1]), lambda i: (i, 0))
        return pl.pallas_call(
            kernel,
            grid=(steps[0],),
            in_specs=[block] * 2,
            out_specs=block,
            out_shape=jax.ShapeDtypeStruct(a.shape, a.dtype),
            compiler_params=kernel_params(16),
            cost_estimate=light,
        )(a, b)

    return jax.tree.map(one, left_side, right_side)


class CtxLine:
    lead = 2

    def __init__(self):
        place = lax.axis_index("ctx")
        self.outer = (place == 0) | (place == 3)
        self.waiting = []
        self.chunks, self.inward, self.across, self.pair_sums = [], [], [], []
        self.totals, self.outward = [], []

    def add(self, chunks):
        self.waiting += list(chunks)
        self.send()

    def send(self):
        while self.waiting and len(self.chunks) < len(self.pair_sums) + self.lead:
            chunk = self.waiting.pop(0)
            self.chunks.append(chunk)
            self.inward.append(lax.ppermute(chunk, "ctx", [(0, 1), (3, 2)]))

    def round(self, *values):
        step = len(self.pair_sums)
        more = step < len(self.chunks)
        if more:
            self.inward[step], values = fence(self.inward[step], values)
            self.pair_sums.append(added(self.chunks[step], self.inward[step]))
        last = step - 1
        held = [
            (array, slice(max(at, 0), max(at + 1, 0)))
            for array, at in ((self.across, last), (self.outward, last - 1), (self.pair_sums, step))
        ]
        fenced, self.waiting, values = fence([array[at] for array, at in held], self.waiting, values)
        for (array, at), value in zip(held, fenced):
            array[at] = value
        if more:
            self.across.append(lax.ppermute(self.pair_sums[step], "ctx", [(1, 2), (2, 1)]))
        if step:
            total = added(self.pair_sums[last], self.across[last])
            self.totals.append(total)
            self.outward.append(lax.ppermute(total, "ctx", [(1, 0), (2, 3)]))
        self.send()
        return values

    def rest(self):
        while len(self.totals) < len(self.chunks):
            self.round()

    def sums(self, first, last):
        return jax.tree.map(
            lambda back, total: jnp.where(self.outer, back, total),
            self.outward[first:last],
            self.totals[first:last],
        )


def summed_in_plane(vector):
    size = lax.axis_size("fsdp")
    bit = 1
    while bit < size:
        vector = vector + lax.ppermute(vector, "fsdp", [(j, j ^ bit) for j in range(size)])
        bit *= 2
    return vector


def local(
    tokens_in,
    block_order,
    norm_attn,
    w_qkv,
    b_qkv,
    w_out,
    norm_mlp,
    w_gate,
    w_up,
    w_down,
    cotangent,
):
    rows, width = tokens_in.shape
    shards = lax.axis_size("fsdp")
    blocks = lax.axis_size("ctx")
    shard = lax.axis_index("fsdp")
    place = lax.axis_index("ctx")
    shard_rows = w_gate.shape[0]
    units = w_down.shape[0]
    orders = block_order[0]
    owners = jnp.concatenate([place[None], (place - jnp.arange(blocks)) % blocks])
    info = jnp.sum(
        jnp.where(owners[:, None] == jnp.arange(blocks)[None, :], orders[None, :], 0), 1
    ).astype(jnp.int32)
    cosine, sine = rotary(info[0] * rows + jnp.arange(rows, dtype=jnp.int32))

    def turn(parts):
        return lax.all_to_all(parts, "fsdp", 0, 0)

    qkv_all = lax.all_gather(w_qkv, "fsdp", axis=0, tiled=True)
    vectors = lax.all_gather(jnp.concatenate([norm_attn, norm_mlp, b_qkv]), "fsdp", axis=0)
    part = 2 * shard_rows // 3 // blocks
    shared = part * blocks
    weights = (w_gate, w_up)
    parts = jnp.concatenate(
        [lax.dynamic_slice_in_dim(weight, place * part, part, 0) for weight in weights]
    )
    vectors, parts = fence(vectors, split_columns(parts, shards))
    pieces = [turn(parts)]

    def ring(piece):
        return lax.ppermute(piece, "ctx", [(j, (j + 1) % blocks) for j in range(blocks)])

    pieces.append(ring(pieces[0]))
    full = padded(units)
    down_rows = jnp.concatenate([w_down, jnp.zeros((full - units, width), bf16)])
    direct = split_columns(jnp.concatenate([weight[shared:] for weight in weights]), shards)
    gain_attn = vectors[:, :shard_rows].reshape(1, -1).astype(f32)
    gain_mlp = vectors[:, shard_rows : 2 * shard_rows].reshape(1, -1).astype(f32)
    bias_all = vectors[:, 2 * shard_rows :].reshape(1, -1).astype(f32)
    qkv_all, pieces, direct, down_rows = fence(qkv_all, pieces, direct, down_rows)
    direct = turn(direct)
    out_all = lax.all_gather(w_out, "fsdp", axis=0, tiled=True)

    normed, query, keys_values = project(tokens_in, gain_attn, qkv_all, bias_all, cosine, sine)
    kv_pieces = [keys_values] + [
        lax.ppermute(keys_values, "ctx", [(j, (j + s) % blocks) for j in range(blocks)])
        for s in range(1, blocks)
    ]
    kv_pieces, pieces, own_cot = fence(kv_pieces, pieces, cotangent)
    for _ in range(2, blocks - 1):
        pieces.append(ring(pieces[-1]))
    mixed, totals = attend(info, query, kv_pieces)
    mixed, direct = fence(mixed, direct)
    source = tokens_in.astype(f32)
    hidden = source + dot(mixed, out_all, 1, 0)
    scale_two = lax.rsqrt(jnp.mean(hidden * hidden, -1, keepdims=True) + norm_eps)
    normed_two = (hidden * scale_two * gain_mlp).astype(bf16)

    normed_two, pieces = fence(normed_two, pieces)
    pieces.append(ring(pieces[-1]))
    normed_all = lax.all_gather(normed_two, "fsdp", axis=0, tiled=True)
    chips = range(0, shards, 2)
    own_pieces = [own_cot] + [
        lax.ppermute(own_cot, "fsdp", [(j, j ^ chip) for j in range(shards)]) for chip in chips[1:]
    ]
    own_pieces[1], pieces = fence(own_pieces[1], pieces)
    cot_pieces = []
    for chip, piece in zip(chips, own_pieces):
        other = lax.ppermute(piece, "fsdp", [(j, j ^ 1) for j in range(shards)])
        cot_pieces += [(chip, piece), (chip ^ 1, other)]
    cot_all = jnp.zeros((shards * rows, width), bf16)
    for bits, piece in cot_pieces:
        cot_all = lax.dynamic_update_slice_in_dim(cot_all, piece, (shard ^ bits) * rows, 0)
    columns = []
    for k in range(2):
        array = jnp.zeros((shards, shard_rows // part, part, full), bf16)
        rest = direct[:, k * (shard_rows - shared) : (k + 1) * (shard_rows - shared)]
        rest = rest.reshape(shards, -1, part, full)
        array = lax.dynamic_update_slice_in_dim(array, rest, blocks, 1)
        for s, piece in enumerate(pieces):
            piece = piece[:, None, k * part : (k + 1) * part]
            array = lax.dynamic_update_slice_in_dim(array, piece, (place - s) % blocks, 1)
        columns.append(array.reshape(width, full))
    gate_cols, up_cols = columns
    cuts = 2
    activation, to_gate, to_up, *down_terms = feed_forward(
        normed_all, cot_all, gate_cols, up_cols, units, rows, cuts
    )

    def to_rows(terms):
        return turn(terms.reshape(shards, shard_rows, full)).reshape(width, full)

    def merged(terms):
        return merge_columns(terms.reshape(shards, shard_rows, full), units)

    def to_owner(terms):
        return lax.psum_scatter(terms, "fsdp", scatter_dimension=0, tiled=True)

    def through_attention(part_grad):
        part_grad = part_grad.astype(f32)
        scaled = part_grad * gain_mlp
        grad_hidden = (
            cotangent.astype(f32)
            + scale_two * scaled
            - hidden * scale_two**3 * jnp.mean(hidden * scaled, -1, keepdims=True)
        )
        gain_terms = jnp.sum(part_grad * hidden * scale_two, 0)
        grad_branch = grad_hidden.astype(bf16)
        grad_mixed = dot(grad_branch, out_all, 1, 1).astype(bf16)
        grad_query, *kv_terms = attend_back(
            info, query, grad_mixed, totals, cosine, sine, kv_pieces
        )
        return grad_hidden, gain_terms, grad_branch, grad_query, *kv_terms

    def kv_exchange(kv_terms):
        return [
            lax.ppermute(kv_terms[s], "ctx", [(j, (j - s) % blocks) for j in range(blocks)])
            for s in range(1, blocks)
        ]

    def projected_grad(grad_query, own_terms, other_terms):
        grad_kv = own_terms.astype(f32)
        for terms in other_terms:
            grad_kv = grad_kv + terms.astype(f32)
        grad_key = grad_kv[0].reshape(rows, KV_HEADS, HEAD)
        rolled = jnp.concatenate([grad_key[..., HEAD // 2 :], grad_key[..., : HEAD // 2]], -1)
        grad_key = grad_key * cosine[:, None, :] - rolled * sine[:, None, :]
        return jnp.concatenate(
            [grad_query, grad_key.reshape(rows, K_WIDTH).astype(bf16), grad_kv[1].astype(bf16)], 1
        )

    def to_tokens(grad_projected, grad_hidden):
        scale_one = lax.rsqrt(jnp.mean(source * source, -1, keepdims=True) + norm_eps)
        grad_normed = dot(grad_projected, qkv_all, 1, 1)
        scaled = grad_normed * gain_attn
        grad_tokens = (
            grad_hidden
            + scale_one * scaled
            - source * scale_one**3 * jnp.mean(source * scaled, -1, keepdims=True)
        ).astype(bf16)
        bias_terms = jnp.sum(grad_projected.astype(f32), 0)
        return grad_tokens, jnp.sum(grad_normed * source * scale_one, 0), bias_terms

    def out_grad(mixed, grad_branch):
        return dot(mixed, grad_branch, 0, 0).astype(bf16)

    def own_sums(*terms):
        total = summed_in_plane(jnp.concatenate([t.reshape(shards, -1) for t in terms], 1))
        return lax.dynamic_index_in_dim(total, shard, 0, False)

    grad_gate, grad_up = unit_grads(cot_all, down_rows, to_gate, to_up, rows)
    mlp_grad = through_columns(grad_gate, grad_up, gate_cols, up_cols, rows)
    if blocks == 4:
        line = CtxLine()
        line.add(down_terms)
        mlp_grad, grad_gate, grad_up, act = line.round(
            mlp_grad, grad_gate, grad_up, activation
        )
        part_grad = to_owner(mlp_grad)
        gate_terms = column_grad(normed_all, grad_gate, cuts)
        (up_terms,) = column_grad(normed_all, grad_up, 1)
        mlp_terms = through_rows(act, down_rows, rows)
        gate_terms, up_terms, mlp_terms = line.round(gate_terms, up_terms, mlp_terms)
        line.add(gate_terms)
        up_terms = to_rows(up_terms)
        part_grad, mlp_terms = fence(part_grad, mlp_terms)
        mlp_out = to_owner(mlp_terms)
        grad_hidden, gain_mlp_terms, grad_branch, grad_query, *kv_terms = through_attention(
            part_grad
        )
        others = kv_exchange(kv_terms)
        out_terms = to_owner(out_grad(mixed, grad_branch))
        line.round()
        grad_query, up_terms = line.round(grad_query, up_terms)
        line.add([up_terms[: width // 2], up_terms[width // 2 :]])
        grad_projected = projected_grad(grad_query, kv_terms[0], others)
        qkv_terms = to_owner(dot(normed, grad_projected, 0, 0).astype(bf16))
        grad_projected, out_terms = line.round(grad_projected, out_terms)
        line.add([out_terms])
        grad_tokens, gain_attn_terms, bias_terms = to_tokens(grad_projected, grad_hidden)
        small = own_sums(gain_attn_terms, gain_mlp_terms, bias_terms)
        grad_tokens, small = line.round(grad_tokens, small)
        gate_terms = to_rows(jnp.concatenate(line.sums(cuts, 2 * cuts)))
        qkv_terms, mlp_out, hidden = line.round(qkv_terms, mlp_out, hidden)
        half = shard_rows // 2
        line.add([[qkv_terms[:half], small], [qkv_terms[half:]]])
        line.rest()
        down_sums = line.sums(0, cuts)
        up_terms = jnp.concatenate(line.sums(2 * cuts, 2 * cuts + 2))
        out_sum, (qkv_sum, small), (qkv_more,) = line.sums(2 * cuts + 2, 2 * cuts + 5)
        qkv_sum = jnp.concatenate([qkv_sum, qkv_more])
    else:
        part_grad = to_owner(mlp_grad)
        gate_terms = column_grad(normed_all, grad_gate, cuts)
        up_terms = column_grad(normed_all, grad_up, cuts)
        gate_terms, up_terms = (to_rows(jnp.concatenate(t)) for t in (gate_terms, up_terms))
        mlp_out = to_owner(through_rows(activation, down_rows, rows))
        grad_hidden, gain_mlp_terms, grad_branch, grad_query, *kv_terms = through_attention(
            part_grad
        )
        others = kv_exchange(kv_terms)
        out_terms = to_owner(out_grad(mixed, grad_branch))
        grad_projected = projected_grad(grad_query, kv_terms[0], others)
        qkv_terms = to_owner(dot(normed, grad_projected, 0, 0).astype(bf16))
        grad_tokens, gain_attn_terms, bias_terms = to_tokens(grad_projected, grad_hidden)
        small = own_sums(gain_attn_terms, gain_mlp_terms, bias_terms)
        down_sums, gate_terms, up_terms, out_sum, qkv_sum, small = lax.psum(
            (down_terms, gate_terms, up_terms, out_terms, qkv_terms, small), "ctx"
        )

    grad_down_w = jnp.concatenate(down_sums).astype(f32)
    grad_out_w = out_sum.astype(f32)
    grad_qkv_w = qkv_sum.astype(f32)
    out_tokens = (hidden + mlp_out.astype(f32)).astype(bf16)

    return (
        out_tokens,
        grad_tokens,
        small[:shard_rows],
        grad_qkv_w,
        small[2 * shard_rows :],
        grad_out_w,
        small[shard_rows : 2 * shard_rows],
        merged(gate_terms),
        merged(up_terms),
        grad_down_w,
    )


def solution(mesh):
    in_specs = (
        P(("fsdp", "ctx"), None),
        P("fsdp", None),
        P("fsdp"),
        P("fsdp", None),
        P("fsdp"),
        P("fsdp", None),
        P("fsdp"),
        P("fsdp", None),
        P("fsdp", None),
        P("fsdp", None),
        P(("fsdp", "ctx"), None),
    )
    out_specs = (
        P(("fsdp", "ctx"), None),
        P(("fsdp", "ctx"), None),
        P("fsdp"),
        P("fsdp", None),
        P("fsdp"),
        P("fsdp", None),
        P("fsdp"),
        P("fsdp", None),
        P("fsdp", None),
        P("fsdp", None),
    )
    return jax.shard_map(local, mesh=mesh, in_specs=in_specs, out_specs=out_specs, check_vma=False)
```

time: 1730 us -> 732 us (0.42)
  waiting for transfers between devices: 1300 us -> 238 us
  Pallas kernels: 0 us -> 201 us
  matrix products: 215 us -> 22.2 us
  starting transfers between devices: 1.06 us -> 124 us
  other arithmetic: 89.2 us -> 36.1 us
  blocking collectives: 62.7 us -> 33.7 us
    reduce_scatter x5 -> x4, waiting for transfers between devices: 533 us -> 10.6 us  [to_owner(): return lax.psum_scatter(terms, 'fsdp', scatter_dimension=0, tiled=True)]
    all_gather x6 -> x3, waiting for transfers between devices: 425 us -> 0.2 us  [the longest x1 0.2 us: local(): normed_all = lax.all_gather(normed_two, 'fsdp', axis=0, tiled=True)]
    psum x1 -> x0, waiting for transfers between devices: 336 us -> none  [local(): lax.psum(grad_qkv.astype(jnp.bfloat16), 'ctx').astype(jnp.float32)]
    ppermute x0 -> x49, waiting for transfers between devices: none -> 225 us  [the longest x10 88.8 us: round(): self.outward.append(lax.ppermute(total, 'ctx', [(1, 0), (2, 3)]))]
    pallas_call x0 -> x31, Pallas kernels: none -> 201 us  [the longest x18 46.3 us: one(): pl.pallas_call(kernel, grid=(steps[0],), in_specs=[block] * 2, out_specs=...]
    dot_general x29 -> x5, matrix products: 215 us -> 22.2 us  [dot(): lax.dot_general(left_side, right_side, (((left_dim,), (right_dim,)), ((),...]
    ppermute x0 -> x49, starting transfers between devices: none -> 111 us  [the longest x10 54.4 us: send(): self.inward.append(lax.ppermute(chunk, 'ctx', [(0, 1), (3, 2)]))]
    another operation x4 -> x0, other arithmetic: 40.5 us -> none  [the longest x1 38.6 us: term_mlp(): jnp.stack([contract_rows(normed_two, grad_gate), contract_rows(normed_two...]
  transfers between devices with their start and end apart: 12 -> 59, of which waited for: 11 -> 27; matrix products, arithmetic and copies ran while one was open for 12% -> 11% of each run, Pallas kernels for 0% -> 23%
where the time goes in v2:
time: 732 us; the launch traced here: 724 us
  waiting for transfers between devices  238 us (33%)
  Pallas kernels  201 us (27%)
  starting transfers between devices  124 us (17%)
  local copies, waits for them, and re-layouts  54.5 us (7%)
  other arithmetic  36.1 us (5%)
  blocking collectives  33.7 us (5%)
  matrix products  22.2 us (3%)
  between operations  15.3 us (2%)
    ppermute x10, waiting for transfers between devices, round(): self.outward.append(lax.ppermute(total, 'ctx', [(1, 0), (2, 3)]))  88.8 us
    ppermute x10, starting transfers between devices, send(): self.inward.append(lax.ppermute(chunk, 'ctx', [(0, 1), (3, 2)]))  54.4 us
    pallas_call x18, Pallas kernels, one(): pl.pallas_call(kernel, grid=(steps[0],), in_specs=[block] * 2, out_specs=...  46.3 us
    ppermute x10, waiting for transfers between devices, send(): self.inward.append(lax.ppermute(chunk, 'ctx', [(0, 1), (3, 2)]))  43.7 us
    ppermute x3, waiting for transfers between devices, local(): lax.ppermute(own_cot, 'fsdp', [(j, j ^ chip) for j in range(shards)])  34.5 us
    pallas_call x1, Pallas kernels, feed_forward(): pl.pallas_call(kernel, grid=(steps + width // tile,), in_specs=[pl.BlockS...  33.2 us
    ppermute x3, waiting for transfers between devices, ring(): lax.ppermute(piece, 'ctx', [(j, (j + 1) % blocks) for j in range(blocks)])  27.9 us
    pallas_call x2, Pallas kernels, column_grad(): pl.pallas_call(kernel, grid=(width // tile,), in_specs=[pl.BlockSpec((cou...  26.9 us
  transfers between devices with their start and end apart: 59, of which 27 were waited for; matrix products, arithmetic and copies ran while one was open for 11% of the time, Pallas kernels for 23%

profile of v2, /device:TPU:0, one launch (start us, length us, event | category | flops | bytes accessed | tf_op | source)
XLA Modules:
  0.0 724.4 jit_solution(3028205099205681070)
XLA Ops:
  9.4 10.5 %all-gather.1 = bf16[8,1,640]{2,1,0:T(2,128)(2,1)S(1)} all-gather(bf16[1,1,640]{2,1,0:T(2,128)(2,1)S(1)} %reshape.172), channel_id=2, replica_groups=mesh['fsdp'=8,'ctx'=4] {'fsdp'}, dimensions={0}, use_global_device_ids=true | all-gather | bytes 11520 | tf_op jit(solution)/shard_map/all_gather | solution.py:563
  21.7 23.2 %all_to_all.20 = bf16[8,64,1152]{2,1,0:T(8,128)(2,1)S(1)} all-to-all(bf16[8,64,1152]{2,1,0:T(8,128)(2,1)S(1)} %shard_map.186), channel_id=1, replica_groups=mesh['fsdp'=8,'ctx'=4] {'fsdp'}, dimensions={0} | all-to-all | bytes 2359296 | tf_op jit(solution)/shard_map/all_to_all | solution.py:560
  52.8 21.1 %collective-permute-done = bf16[8,64,1152]{2,1,0:T(8,128)(2,1)} collective-permute-done((bf16[8,64,1152]{2,1,0:T(8,128)(2,1)S(1)}, bf16[8,64,1152]{2,1,0:T(8,128)(2,1)}, u32[]{:S(2)}, u32[]{:S(2)}) %collective-permute-start) | collective-permute-done | bytes 1179680 | tf_op jit(solution)/shard_map/ppermute | solution.py:574
  99.7 10.2 %collective-permute-done.2.refs_2_.refs_6_ = bf16[256,512]{1,0:T(8,128)(2,1)S(1)} collective-permute-done((bf16[256,512]{1,0:T(8,128)(2,1)S(1)}, bf16[256,512]{1,0:T(8,128)(2,1)S(1)}, u32[]{:S(2)}, u32[]{:S(2)}) %collective-permute-start.2) | collective-permute-done | bytes 262176 | tf_op jit(solution)/shard_map/ppermute | solution.py:589
  115.5 12.1 %shard_map.189 = (bf16[256,1536]{1,0:T(8,128)(2,1)S(1)}, f32[12,1,256]{2,1,0:T(1,128)S(1)}) custom-call(s32[5]{0:T(128)S(1)} %select_reduce_fusion.info_ref, bf16[256,1536]{1,0:T(8,128)(2,1)S(1)} %get-tuple-element.130.q_ref, bf16[256,512]{1,0:T(8,128)(2,1)S(1)} %get-tuple-element.134.refs_0_.refs_4_, ...), custom_call_target="tpu_custom_call" | custom-call | flops 1048576 | bytes 65536 | tf_op jit(solution)/shard_map/pallas_call | solution.py:188
  152.3 34.5 %collective-permute-done.9 = bf16[256,1536]{1,0:T(8,128)(2,1)} collective-permute-done((bf16[256,1536]{1,0:T(8,128)(2,1)}, bf16[256,1536]{1,0:T(8,128)(2,1)}, u32[]{:S(2)}, u32[]{:S(2)}) %collective-permute-start.9) | collective-permute-done | bytes 786464 | tf_op jit(solution)/shard_map/ppermute | solution.py:607
  205.3 33.2 %shard_map.190 = (bf16[2048,1152]{1,0:T(8,128)(2,1)}, bf16[2048,1152]{1,0:T(8,128)(2,1)}, bf16[2048,1152]{1,0:T(8,128)(2,1)}, bf16[560,1536]{1,0:T(8,128)(2,1)}, bf16[560,1536]{1,0:T(8,128)(2,1)}) custom-call(bf16[2048,1536]{1,0:T(8,128)(2,1)} %all-gather.10.cloned.1.call-done.x_ref, bf16[2048,1536]{1,0:T(8,128)(2,1)} %constant_dynamic-update-slice_fusion.c_ref, ...), custom_call_target="tpu_custom_call" | custom-call | flops 1048576 | bytes 65536 | tf_op jit(solution)/shard_map/pallas_call | solution.py:320
  242.0 15.1 %shard_map.191 = (bf16[2048,1152]{1,0:T(8,128)(2,1)}, bf16[2048,1152]{1,0:T(8,128)(2,1)}) custom-call(bf16[2048,1536]{1,0:T(8,128)(2,1)} %constant_dynamic-update-slice_fusion.c_ref, bf16[1152,1536]{1,0:T(8,128)(2,1)} %concatenate.46.wd_ref, bf16[2048,1152]{1,0:T(8,128)(2,1)} %get-tuple-element.156.tg_ref, bf16[2048,1152]{1,0:T(8,128)(2,1)} %get-tuple-element.157.tu_ref), custom_call_target="tpu_custom_call" | custom-call | flops 1048576 | bytes 65536 | tf_op jit(solution)/shard_map/pallas_call | solution.py:349
  257.1 22.0 %shard_map.192 = bf16[2048,1536]{1,0:T(8,128)(2,1)} custom-call(bf16[2048,1152]{1,0:T(8,128)(2,1)} %get-tuple-element.168.dg_ref.g_ref, bf16[2048,1152]{1,0:T(8,128)(2,1)} %get-tuple-element.171.du_ref.g_ref, bf16[1536,1152]{1,0:T(8,128)(2,1)} %bitcast.76, bf16[1536,1152]{1,0:T(8,128)(2,1)} %bitcast.78), custom_call_target="tpu_custom_call" | custom-call | flops 1048576 | bytes 65536 | tf_op jit(solution)/shard_map/pallas_call | solution.py:375
  291.6 13.1 %shard_map.196 = bf16[2048,1536]{1,0:T(8,128)(2,1)} custom-call(bf16[2048,1152]{1,0:T(8,128)(2,1)} %get-tuple-element.172.act_ref, bf16[1152,1536]{1,0:T(8,128)(2,1)} %concatenate.46.wd_ref), custom_call_target="tpu_custom_call" | custom-call | flops 1048576 | bytes 65536 | tf_op jit(solution)/shard_map/pallas_call | solution.py:423
  304.8 13.2 %shard_map.195 = bf16[1536,1152]{1,0:T(8,128)(2,1)} custom-call(bf16[2048,1536]{1,0:T(8,128)(2,1)} %all-gather.10.cloned.1.call-done.x_ref, bf16[2048,1152]{1,0:T(8,128)(2,1)} %get-tuple-element.171.du_ref.g_ref), custom_call_target="tpu_custom_call" | custom-call | flops 1048576 | bytes 65536 | tf_op jit(solution)/shard_map/pallas_call | solution.py:404
  318.0 13.7 %shard_map.194 = (bf16[768,1152]{1,0:T(8,128)(2,1)}, bf16[768,1152]{1,0:T(8,128)(2,1)}) custom-call(bf16[2048,1536]{1,0:T(8,128)(2,1)} %all-gather.10.cloned.1.call-done.x_ref, bf16[2048,1152]{1,0:T(8,128)(2,1)} %get-tuple-element.168.dg_ref.g_ref), custom_call_target="tpu_custom_call" | custom-call | flops 1048576 | bytes 65536 | tf_op jit(solution)/shard_map/pallas_call | solution.py:404
  336.1 10.6 %reduce-scatter.5.cloned.1.call-done = bf16[256,1536]{1,0:T(8,128)(2,1)} async-done(((bf16[2048,1536]{1,0:T(8,128)(2,1)}), bf16[256,1536]{1,0:T(8,128)(2,1)}) %reduce-scatter.5.cloned.1.call-update) | async-done | bytes 786448 | tf_op jit(solution)/shard_map/reduce_scatter | solution.py:640
  380.3 18.5 %collective-permute-done.18.b_ref = bf16[768,1152]{1,0:T(8,128)(2,1)} collective-permute-done((bf16[768,1152]{1,0:T(8,128)(2,1)}, bf16[768,1152]{1,0:T(8,128)(2,1)}, u32[]{:S(2)}, u32[]{:S(2)}) %collective-permute-start.18) | collective-permute-done | bytes 1769504 | tf_op jit(solution)/shard_map/ppermute | solution.py:486
  418.3 17.6 %shard_map.201 = (bf16[256,1536]{1,0:T(8,128)(2,1)S(1)}, bf16[2,256,256]{2,1,0:T(8,128)(2,1)S(1)}, bf16[2,256,256]{2,1,0:T(8,128)(2,1)}, bf16[2,256,256]{2,1,0:T(8,128)(2,1)}, bf16[2,256,256]{2,1,0:T(8,128)(2,1)}) custom-call(s32[5]{0:T(128)S(1)} %select_reduce_fusion.info_ref, bf16[256,1536]{1,0:T(8,128)(2,1)S(1)} %copy-done.9, ...), custom_call_target="tpu_custom_call" | custom-call | flops 1048576 | bytes 65536 | tf_op jit(solution)/shard_map/pallas_call | solution.py:253
  454.1 11.1 %collective-permute-done.20 = bf16[560,1536]{1,0:T(8,128)(2,1)} collective-permute-done((bf16[560,1536]{1,0:T(8,128)(2,1)}, bf16[560,1536]{1,0:T(8,128)(2,1)}, u32[]{:S(2)}, u32[]{:S(2)}) %collective-permute-start.20) | collective-permute-done | bytes 1720352 | tf_op jit(solution)/shard_map/ppermute | solution.py:507
  497.9 9.5 %collective-permute-start.30 = (bf16[768,1152]{1,0:T(8,128)(2,1)S(1)}, bf16[768,1152]{1,0:T(8,128)(2,1)}, u32[]{:S(2)}, u32[]{:S(2)}) collective-permute-start(bf16[768,1152]{1,0:T(8,128)(2,1)S(1)} %get-tuple-element.248.a_ref), channel_id=1, source_target_pairs={{0,1},{3,2},{4,5},{7,6},{8,9},{11,10},{12,13},{15,14},{16,17},{19,... | collective-permute-start | bytes 5308424 | tf_op jit(solution)/shard_map/ppermute | solution.py:486
  509.4 16.3 %collective-permute-done.24.b_ref = bf16[768,1152]{1,0:T(8,128)(2,1)} collective-permute-done((bf16[768,1152]{1,0:T(8,128)(2,1)}, bf16[768,1152]{1,0:T(8,128)(2,1)}, u32[]{:S(2)}, u32[]{:S(2)}) %collective-permute-start.24) | collective-permute-done | bytes 1769504 | tf_op jit(solution)/shard_map/ppermute | solution.py:486
  531.4 8.4 %collective-permute-start.36 = (bf16[192,1536]{1,0:T(8,128)(2,1)}, bf16[192,1536]{1,0:T(8,128)(2,1)}, u32[]{:S(2)}, u32[]{:S(2)}) collective-permute-start(bf16[192,1536]{1,0:T(8,128)(2,1)} %reduce-scatter.7.cloned.1.call-done.a_ref), channel_id=1, source_target_pairs={{0,1},{3,2},{4,5},{7,6},{8,9},{11,10},{12,13},{15,14},{16,17},{19,... | collective-permute-start | bytes 1769480 | tf_op jit(solution)/shard_map/ppermute | solution.py:486
  567.4 21.4 %collective-permute-done.29 = bf16[768,1152]{1,0:T(8,128)(2,1)S(1)} collective-permute-done((bf16[768,1152]{1,0:T(8,128)(2,1)S(1)}, bf16[768,1152]{1,0:T(8,128)(2,1)S(1)}, u32[]{:S(2)}, u32[]{:S(2)}) %collective-permute-start.29) | collective-permute-done | bytes 1769504 | tf_op jit(solution)/shard_map/ppermute | solution.py:507
  606.1 23.3 %collective-permute-done.35 = bf16[768,1152]{1,0:T(8,128)(2,1)} collective-permute-done((bf16[768,1152]{1,0:T(8,128)(2,1)}, bf16[768,1152]{1,0:T(8,128)(2,1)}, u32[]{:S(2)}, u32[]{:S(2)}) %collective-permute-start.35) | collective-permute-done | bytes 1769504 | tf_op jit(solution)/shard_map/ppermute | solution.py:507
  638.7 8.1 %collective-permute-start.40 = (f32[640]{0:T(1024)S(1)}, f32[640]{0:T(1024)S(1)}, u32[]{:S(2)}, u32[]{:S(2)}) collective-permute-start(f32[640]{0:T(1024)S(1)} %fusion.20), channel_id=1, source_target_pairs={{0,1},{3,2},{4,5},{7,6},{8,9},{11,10},{12,13},{15,14},{16,17},{19,... | collective-permute-start | bytes 7688 | tf_op jit(solution)/shard_map/ppermute | solution.py:486
  696.0 9.0 %collective-permute-done.46 = bf16[96,2048]{1,0:T(8,128)(2,1)S(1)} collective-permute-done((bf16[96,2048]{1,0:T(8,128)(2,1)S(1)}, bf16[96,2048]{1,0:T(8,128)(2,1)S(1)}, u32[]{:S(2)}, u32[]{:S(2)}) %collective-permute-start.46) | collective-permute-done | bytes 393248 | tf_op jit(solution)/shard_map/ppermute | solution.py:507
  707.7 8.3 %collective-permute-done.48 = bf16[96,2048]{1,0:T(8,128)(2,1)S(1)} collective-permute-done((bf16[96,2048]{1,0:T(8,128)(2,1)S(1)}, bf16[96,2048]{1,0:T(8,128)(2,1)S(1)}, u32[]{:S(2)}, u32[]{:S(2)}) %collective-permute-start.48) | collective-permute-done | bytes 393248 | tf_op jit(solution)/shard_map/ppermute | solution.py:507
  (332 shorter events, 325.1 us)
Async XLA Ops:
  7.2 66.8 %all-gather.6.cloned.1.call-start = ((), (), s32[]{:S(2)}) async-start(), calls=%async_computation.8 | async-start | bytes 7077888 | tf_op jit(solution)/shard_map/all_gather | solution.py:562
  7.9 120.6 %all-gather.8.cloned.1.call-start = ((), (), s32[]{:S(2)}) async-start(), calls=%async_computation.9 | async-start | bytes 5308416 | tf_op jit(solution)/shard_map/all_gather | solution.py:585
  74.0 54.5 %all-to-all-start.1 = ((bf16[8,128,1152]{2,1,0:T(8,128)(2,1)}), bf16[8,128,1152]{2,1,0:T(8,128)(2,1)}, u32[]{:S(2)}, u32[]{:S(2)}) async-start(bf16[8,128,1152]{2,1,0:T(8,128)(2,1)} %shard_map.187), calls=%async_computation.1 | async-start | bytes 4718592 | tf_op jit(solution)/shard_map/all_to_all | solution.py:560
  78.4 126.9 %all-gather.10.cloned.1.call-start = ((), (), s32[]{:S(2)}) async-start(), calls=%async_computation.10 | async-start | bytes 7077888 | tf_op jit(solution)/shard_map/all_gather | solution.py:604
  141.6 205.1 %reduce-scatter.5.cloned.1.call-start = ((), (), s32[]{:S(2)}) async-start(), calls=%async_computation.11 | async-start | bytes 7077888 | tf_op jit(solution)/shard_map/reduce_scatter | solution.py:640
  141.6 45.2 %collective-permute-start.9 = (bf16[256,1536]{1,0:T(8,128)(2,1)}, bf16[256,1536]{1,0:T(8,128)(2,1)}, u32[]{:S(2)}, u32[]{:S(2)}) collective-permute-start(bf16[256,1536]{1,0:T(8,128)(2,1)} %param.21), channel_id=1, source_target_pairs={{0,16},{4,20},{8,24},{12,28},{16,0},{20,4},{24,8},{28,12},{1,17},{... | collective-permute-start | bytes 2359304 | tf_op jit(solution)/shard_map/ppermute | solution.py:607
  143.1 43.7 %collective-permute-start.11 = (bf16[256,1536]{1,0:T(8,128)(2,1)}, bf16[256,1536]{1,0:T(8,128)(2,1)}, u32[]{:S(2)}, u32[]{:S(2)}) collective-permute-start(bf16[256,1536]{1,0:T(8,128)(2,1)} %param.21), channel_id=1, source_target_pairs={{0,24},{4,28},{8,16},{12,20},{16,8},{20,12},{24,0},{28,4},{1,25},{... | collective-permute-start | bytes 2359304 | tf_op jit(solution)/shard_map/ppermute | solution.py:607
  144.5 42.8 %collective-permute-start.5 = (bf16[256,1536]{1,0:T(8,128)(2,1)}, bf16[256,1536]{1,0:T(8,128)(2,1)S(1)}, u32[]{:S(2)}, u32[]{:S(2)}) collective-permute-start(bf16[256,1536]{1,0:T(8,128)(2,1)} %param.21), channel_id=1, source_target_pairs={{0,4},{4,0},{8,12},{12,8},{16,20},{20,16},{24,28},{28,24},{1,5},{5... | collective-permute-start | bytes 2359304 | tf_op jit(solution)/shard_map/ppermute | solution.py:612
  144.5 46.3 %collective-permute-start.7 = (bf16[8,64,1152]{2,1,0:T(8,128)(2,1)}, bf16[8,64,1152]{2,1,0:T(8,128)(2,1)}, u32[]{:S(2)}, u32[]{:S(2)}) collective-permute-start(bf16[8,64,1152]{2,1,0:T(8,128)(2,1)} %collective-permute-done.4), channel_id=1, source_target_pairs={{0,1},{1,2},{2,3},{3,0},{4,5},{5,6},{6,7},{7,4},{8,9},{9,10},{10,1... | collective-permute-start | bytes 3538952 | tf_op jit(solution)/shard_map/ppermute | solution.py:574
  146.6 44.2 %collective-permute-start.6 = (bf16[256,1536]{1,0:T(8,128)(2,1)}, bf16[256,1536]{1,0:T(8,128)(2,1)S(1)}, u32[]{:S(2)}, u32[]{:S(2)}) collective-permute-start(bf16[256,1536]{1,0:T(8,128)(2,1)} %param.21), channel_id=1, source_target_pairs={{0,8},{4,12},{8,0},{12,4},{16,24},{20,28},{24,16},{28,20},{1,9},{5... | collective-permute-start | bytes 2359304 | tf_op jit(solution)/shard_map/ppermute | solution.py:607
  284.0 241.7 %reduce-scatter.7.cloned.1.call-start = ((), (), s32[]{:S(2)}) async-start(), calls=%async_computation.12 | async-start | bytes 5308416 | tf_op jit(solution)/shard_map/reduce_scatter | solution.py:640
  284.1 47.6 %collective-permute-start.15 = (bf16[560,1536]{1,0:T(8,128)(2,1)}, bf16[560,1536]{1,0:T(8,128)(2,1)}, u32[]{:S(2)}, u32[]{:S(2)}) collective-permute-start(bf16[560,1536]{1,0:T(8,128)(2,1)} %get-tuple-element.167.a_ref), channel_id=1, source_target_pairs={{0,1},{3,2},{4,5},{7,6},{8,9},{11,10},{12,13},{15,14},{16,17},{19,... | collective-permute-start | bytes 5160968 | tf_op jit(solution)/shard_map/ppermute | solution.py:486
  289.6 46.5 %collective-permute-start.14 = (bf16[560,1536]{1,0:T(8,128)(2,1)S(1)}, bf16[560,1536]{1,0:T(8,128)(2,1)}, u32[]{:S(2)}, u32[]{:S(2)}) collective-permute-start(bf16[560,1536]{1,0:T(8,128)(2,1)S(1)} %shard_map.193.a_ref), channel_id=1, source_target_pairs={{1,2},{2,1},{5,6},{6,5},{9,10},{10,9},{13,14},{14,13},{17,18},{18,... | collective-permute-start | bytes 5160968 | tf_op jit(solution)/shard_map/ppermute | solution.py:503
  355.5 247.2 %reduce-scatter.11.cloned.1.call-start = ((), (), s32[]{:S(2)}) async-start(), calls=%async_computation.14 | async-start | bytes 7077888 | tf_op jit(solution)/shard_map/reduce_scatter | solution.py:640
  356.1 42.7 %collective-permute-start.18 = (bf16[768,1152]{1,0:T(8,128)(2,1)}, bf16[768,1152]{1,0:T(8,128)(2,1)}, u32[]{:S(2)}, u32[]{:S(2)}) collective-permute-start(bf16[768,1152]{1,0:T(8,128)(2,1)} %get-tuple-element.180.a_ref), channel_id=1, source_target_pairs={{0,1},{3,2},{4,5},{7,6},{8,9},{11,10},{12,13},{15,14},{16,17},{19,... | collective-permute-start | bytes 5308424 | tf_op jit(solution)/shard_map/ppermute | solution.py:486
  365.2 41.2 %collective-permute-start.17 = (bf16[560,1536]{1,0:T(8,128)(2,1)}, bf16[560,1536]{1,0:T(8,128)(2,1)}, u32[]{:S(2)}, u32[]{:S(2)}) collective-permute-start(bf16[560,1536]{1,0:T(8,128)(2,1)} %shard_map.198), channel_id=1, source_target_pairs={{1,0},{2,3},{5,4},{6,7},{9,8},{10,11},{13,12},{14,15},{17,16},{18,... | collective-permute-start | bytes 5160968 | tf_op jit(solution)/shard_map/ppermute | solution.py:507
  368.4 80.2 %all-to-all-start.2 = ((bf16[8,192,1152]{2,1,0:T(8,128)(2,1)}), bf16[8,192,1152]{2,1,0:T(8,128)(2,1)}, u32[]{:S(2)}, u32[]{:S(2)}) async-start(bf16[8,192,1152]{2,1,0:T(8,128)(2,1)} %bitcast.79), calls=%async_computation.3 | async-start | bytes 7077888 | tf_op jit(solution)/shard_map/all_to_all | solution.py:560
  373.0 229.7 %reduce-scatter.9.cloned.1.call-start = ((), (), s32[]{:S(2)}) async-start(), calls=%async_computation.13 | async-start | bytes 7077888 | tf_op jit(solution)/shard_map/reduce_scatter | solution.py:640
  373.0 73.4 %collective-permute-start.21 = (bf16[768,1152]{1,0:T(8,128)(2,1)}, bf16[768,1152]{1,0:T(8,128)(2,1)S(1)}, u32[]{:S(2)}, u32[]{:S(2)}) collective-permute-start(bf16[768,1152]{1,0:T(8,128)(2,1)} %get-tuple-element.183.a_ref), channel_id=1, source_target_pairs={{0,1},{3,2},{4,5},{7,6},{8,9},{11,10},{12,13},{15,14},{16,17},{19,... | collective-permute-start | bytes 5308424 | tf_op jit(solution)/shard_map/ppermute | solution.py:486
  406.4 58.8 %collective-permute-start.19 = (bf16[768,1152]{1,0:T(8,128)(2,1)S(1)}, bf16[768,1152]{1,0:T(8,128)(2,1)}, u32[]{:S(2)}, u32[]{:S(2)}) collective-permute-start(bf16[768,1152]{1,0:T(8,128)(2,1)S(1)} %shard_map.199.a_ref), channel_id=1, source_target_pairs={{1,2},{2,1},{5,6},{6,5},{9,10},{10,9},{13,14},{14,13},{17,18},{18,... | collective-permute-start | bytes 5308424 | tf_op jit(solution)/shard_map/ppermute | solution.py:503
  413.1 52.1 %collective-permute-start.20 = (bf16[560,1536]{1,0:T(8,128)(2,1)}, bf16[560,1536]{1,0:T(8,128)(2,1)}, u32[]{:S(2)}, u32[]{:S(2)}) collective-permute-start(bf16[560,1536]{1,0:T(8,128)(2,1)} %shard_map.200), channel_id=1, source_target_pairs={{1,0},{2,3},{5,4},{6,7},{9,8},{10,11},{13,12},{14,15},{17,16},{18,... | collective-permute-start | bytes 5160968 | tf_op jit(solution)/shard_map/ppermute | solution.py:507
  497.9 65.6 %collective-permute-start.30 = (bf16[768,1152]{1,0:T(8,128)(2,1)S(1)}, bf16[768,1152]{1,0:T(8,128)(2,1)}, u32[]{:S(2)}, u32[]{:S(2)}) collective-permute-start(bf16[768,1152]{1,0:T(8,128)(2,1)S(1)} %get-tuple-element.248.a_ref), channel_id=1, source_target_pairs={{0,1},{3,2},{4,5},{7,6},{8,9},{11,10},{12,13},{15,14},{16,17},{19,... | collective-permute-start | bytes 5308424 | tf_op jit(solution)/shard_map/ppermute | solution.py:486
  531.4 71.4 %collective-permute-start.36 = (bf16[192,1536]{1,0:T(8,128)(2,1)}, bf16[192,1536]{1,0:T(8,128)(2,1)}, u32[]{:S(2)}, u32[]{:S(2)}) collective-permute-start(bf16[192,1536]{1,0:T(8,128)(2,1)} %reduce-scatter.7.cloned.1.call-done.a_ref), channel_id=1, source_target_pairs={{0,1},{3,2},{4,5},{7,6},{8,9},{11,10},{12,13},{15,14},{16,17},{19,... | collective-permute-start | bytes 1769480 | tf_op jit(solution)/shard_map/ppermute | solution.py:486
  596.2 70.3 %all-to-all-start.3 = ((bf16[8,192,1152]{2,1,0:T(8,128)(2,1)}), bf16[8,192,1152]{2,1,0:T(8,128)(2,1)S(1)}, u32[]{:S(2)}, u32[]{:S(2)}) async-start(bf16[8,192,1152]{2,1,0:T(8,128)(2,1)} %bitcast.80), calls=%async_computation.7 | async-start | bytes 7077888 | tf_op jit(solution)/shard_map/all_to_all | solution.py:560
  (90 other events, 1169.5 us)
Sparse Core Ops, SparseCore 0:
  9.9 57.3 all-gather.5
  69.2 57.7 all-gather.7
  141.7 63.5 all-gather.9
  284.2 62.4 reduce-scatter.4
  355.7 83.1 reduce-scatter.6
  442.7 61.7 reduce-scatter.10
  508.8 61.9 reduce-scatter.8

commit v3 on v2

--- a/solution.py
+++ b/solution.py
@@ -85,6 +85,33 @@
         compiler_params=kernel_params(40),
         cost_estimate=light,
     )(parts)
+
+
+def moved(moves, arrays, shapes):
+    def kernel(at_ref, *refs):
+        sources, targets, sems = refs[: len(arrays)], refs[len(arrays) : -1], refs[-1]
+        copies = [
+            pltpu.make_async_copy(
+                sources[source].at[where], targets[target].at[there], sems.at[i]
+            )
+            for i, (source, where, target, there) in enumerate(moves(at_ref[0], at_ref[1]))
+        ]
+        for copy in copies:
+            copy.start()
+        for copy in copies:
+            copy.wait()
+
+    anywhere = pl.BlockSpec(memory_space=pl.ANY)
+    at = jnp.stack([lax.axis_index("ctx"), lax.axis_index("fsdp")]).astype(jnp.int32)
+    return pl.pallas_call(
+        kernel,
+        in_specs=[pl.BlockSpec(memory_space=pltpu.SMEM)] + [anywhere] * len(arrays),
+        out_specs=[anywhere] * len(shapes),
+        out_shape=[jax.ShapeDtypeStruct(shape, bf16) for shape in shapes],
+        scratch_shapes=[pltpu.SemaphoreType.DMA((len(moves(0, 0)),))],
+        compiler_params=kernel_params(16),
+        cost_estimate=light,
+    )(at, *arrays)
 
 
 def project(tokens_in, gain, weights, bias, cosine, sine):
@@ -209,8 +236,7 @@
     def kernel(info_ref, q_ref, g_ref, total_ref, cos_ref, sin_ref, *refs):
         keys, values = refs[:count], refs[count : 2 * count]
         dq_ref = refs[2 * count]
-        kv_refs = refs[2 * count + 1 : 3 * count + 1]
-        bias_ref, p_ref, dp_ref, sum_ref = refs[3 * count + 1 :]
+        kv_ref, bias_ref, p_ref, dp_ref, sum_ref = refs[2 * count + 1 :]
         head = pl.program_id(0)
 
         @pl.when(head == 0)
@@ -245,7 +271,7 @@
         @pl.when(head % GROUP == GROUP - 1)
         def _():
             for piece in range(count):
-                kv_refs[piece][...] = sum_ref[piece].astype(bf16)
+                kv_ref[info_ref[1 + count + piece]] = sum_ref[piece].astype(bf16)
 
     key_spec = pl.BlockSpec((rows, HEAD), lambda h: (0, h // GROUP))
     value_spec = pl.BlockSpec((rows, HEAD), lambda h: (0, KV_HEADS + h // GROUP))
@@ -264,9 +290,9 @@
         + [key_spec] * count
         + [value_spec] * count,
         out_specs=[head_spec]
-        + [pl.BlockSpec((2, rows, HEAD), lambda h: (0, 0, h // GROUP))] * count,
+        + [pl.BlockSpec((count, 2, rows, HEAD), lambda h: (0, 0, 0, h // GROUP))],
         out_shape=[jax.ShapeDtypeStruct((rows, Q_WIDTH), bf16)]
-        + [jax.ShapeDtypeStruct((2, rows, K_WIDTH), bf16)] * count,
+        + [jax.ShapeDtypeStruct((count, 2, rows, K_WIDTH), bf16)],
         scratch_shapes=[pltpu.VMEM((count * rows, rows), f32)] * 3
         + [pltpu.VMEM((count, 2, rows, HEAD), f32)],
         compiler_params=kernel_params(32),
@@ -466,7 +492,7 @@
 
 
 class CtxLine:
-    lead = 2
+    lead = 1
 
     def __init__(self):
         place = lax.axis_index("ctx")
@@ -488,29 +514,27 @@
     def round(self, *values):
         step = len(self.pair_sums)
         more = step < len(self.chunks)
+        last = len(self.totals)
         if more:
             self.inward[step], values = fence(self.inward[step], values)
             self.pair_sums.append(added(self.chunks[step], self.inward[step]))
-        last = step - 1
+        ahead = slice(step + 1, step + 2 if step > 2 else step)
         held = [
-            (array, slice(max(at, 0), max(at + 1, 0)))
-            for array, at in ((self.across, last), (self.outward, last - 1), (self.pair_sums, step))
+            (self.across, slice(last, None)),
+            (self.pair_sums, slice(last + 1, None)),
+            (self.outward, slice(last - 1, None) if last else slice(0, 0)),
+            (self.inward, ahead),
         ]
         fenced, self.waiting, values = fence([array[at] for array, at in held], self.waiting, values)
         for (array, at), value in zip(held, fenced):
             array[at] = value
+        self.send()
+        if len(self.across) > last:
+            self.totals.append(added(self.pair_sums[last], self.across[last]))
+            self.outward.append(lax.ppermute(self.totals[-1], "ctx", [(1, 0), (2, 3)]))
         if more:
             self.across.append(lax.ppermute(self.pair_sums[step], "ctx", [(1, 2), (2, 1)]))
-        if step:
-            total = added(self.pair_sums[last], self.across[last])
-            self.totals.append(total)
-            self.outward.append(lax.ppermute(total, "ctx", [(1, 0), (2, 3)]))
-        self.send()
         return values
-
-    def rest(self):
-        while len(self.totals) < len(self.chunks):
-            self.round()
 
     def sums(self, first, last):
         return jax.tree.map(
@@ -553,7 +577,8 @@
     owners = jnp.concatenate([place[None], (place - jnp.arange(blocks)) % blocks])
     info = jnp.sum(
         jnp.where(owners[:, None] == jnp.arange(blocks)[None, :], orders[None, :], 0), 1
-    ).astype(jnp.int32)
+    )
+    info = jnp.concatenate([info, owners[1:]]).astype(jnp.int32)
     cosine, sine = rotary(info[0] * rows + jnp.arange(rows, dtype=jnp.int32))
 
     def turn(parts):
@@ -580,11 +605,12 @@
     gain_attn = vectors[:, :shard_rows].reshape(1, -1).astype(f32)
     gain_mlp = vectors[:, shard_rows : 2 * shard_rows].reshape(1, -1).astype(f32)
     bias_all = vectors[:, 2 * shard_rows :].reshape(1, -1).astype(f32)
-    qkv_all, pieces, direct, down_rows = fence(qkv_all, pieces, direct, down_rows)
+    qkv_all, pieces, down_rows = fence(qkv_all, pieces, down_rows)
+    out_all = lax.all_gather(w_out, "fsdp", axis=0, tiled=True)
+
+    normed, query, keys_values = project(tokens_in, gain_attn, qkv_all, bias_all, cosine, sine)
+    keys_values, direct = fence(keys_values, direct)
     direct = turn(direct)
-    out_all = lax.all_gather(w_out, "fsdp", axis=0, tiled=True)
-
-    normed, query, keys_values = project(tokens_in, gain_attn, qkv_all, bias_all, cosine, sine)
     kv_pieces = [keys_values] + [
         lax.ppermute(keys_values, "ctx", [(j, (j + s) % blocks) for j in range(blocks)])
         for s in range(1, blocks)
@@ -592,6 +618,12 @@
     kv_pieces, pieces, own_cot = fence(kv_pieces, pieces, cotangent)
     for _ in range(2, blocks - 1):
         pieces.append(ring(pieces[-1]))
+
+    def from_chip(chip):
+        return lax.ppermute(own_cot, "fsdp", [(j, j ^ chip) for j in range(shards)])
+
+    chips = [chip for chip in range(2, shards, 2) if chip & (chip - 1) == 0]
+    cot_pieces = {chip: from_chip(chip) for chip in chips}
     mixed, totals = attend(info, query, kv_pieces)
     mixed, direct = fence(mixed, direct)
     source = tokens_in.astype(f32)
@@ -599,32 +631,46 @@
     scale_two = lax.rsqrt(jnp.mean(hidden * hidden, -1, keepdims=True) + norm_eps)
     normed_two = (hidden * scale_two * gain_mlp).astype(bf16)
 
-    normed_two, pieces = fence(normed_two, pieces)
+    normed_two, pieces, cot_pieces = fence(normed_two, pieces, cot_pieces)
     pieces.append(ring(pieces[-1]))
     normed_all = lax.all_gather(normed_two, "fsdp", axis=0, tiled=True)
-    chips = range(0, shards, 2)
-    own_pieces = [own_cot] + [
-        lax.ppermute(own_cot, "fsdp", [(j, j ^ chip) for j in range(shards)]) for chip in chips[1:]
-    ]
-    own_pieces[1], pieces = fence(own_pieces[1], pieces)
-    cot_pieces = []
-    for chip, piece in zip(chips, own_pieces):
-        other = lax.ppermute(piece, "fsdp", [(j, j ^ 1) for j in range(shards)])
-        cot_pieces += [(chip, piece), (chip ^ 1, other)]
-    cot_all = jnp.zeros((shards * rows, width), bf16)
-    for bits, piece in cot_pieces:
-        cot_all = lax.dynamic_update_slice_in_dim(cot_all, piece, (shard ^ bits) * rows, 0)
-    columns = []
-    for k in range(2):
-        array = jnp.zeros((shards, shard_rows // part, part, full), bf16)
-        rest = direct[:, k * (shard_rows - shared) : (k + 1) * (shard_rows - shared)]
-        rest = rest.reshape(shards, -1, part, full)
-        array = lax.dynamic_update_slice_in_dim(array, rest, blocks, 1)
-        for s, piece in enumerate(pieces):
-            piece = piece[:, None, k * part : (k + 1) * part]
-            array = lax.dynamic_update_slice_in_dim(array, piece, (place - s) % blocks, 1)
-        columns.append(array.reshape(width, full))
-    gate_cols, up_cols = columns
+    cot_pieces[0] = own_cot
+    for chip in range(2, shards, 2):
+        if chip not in cot_pieces:
+            cot_pieces[chip] = from_chip(chip)
+            cot_pieces[chip], pieces = fence(cot_pieces[chip], pieces)
+    for chip in range(0, shards, 2):
+        cot_pieces[chip ^ 1] = lax.ppermute(
+            cot_pieces[chip], "fsdp", [(j, j ^ 1) for j in range(shards)]
+        )
+    order = list(cot_pieces)
+
+    def cot_moves(place, shard):
+        return [
+            (i, pl.ds(0, rows), 0, pl.ds((shard ^ bits) * rows, rows))
+            for i, bits in enumerate(order)
+        ]
+
+    (cot_all,) = moved(cot_moves, [cot_pieces[bits] for bits in order], [(shards * rows, width)])
+
+    groups = shard_rows // part
+    grouped = (shards, groups, part, full)
+    rest = groups - blocks
+
+    def column_moves(place, shard):
+        every = pl.ds(0, shards)
+        listed = []
+        for k in range(2):
+            for s in range(blocks):
+                group = lax.rem(place - s + blocks, blocks)
+                listed.append((s, (every, k), k, (every, group)))
+            listed.append((blocks, (every, pl.ds(k * rest, rest)), k, (every, pl.ds(blocks, rest))))
+        return listed
+
+    sources = [piece.reshape(shards, 2, part, full) for piece in pieces]
+    sources.append(direct.reshape(shards, 2 * rest, part, full))
+    columns = moved(column_moves, sources, [grouped] * 2)
+    gate_cols, up_cols = (array.reshape(width, full) for array in columns)
     cuts = 2
     activation, to_gate, to_up, *down_terms = feed_forward(
         normed_all, cot_all, gate_cols, up_cols, units, rows, cuts
@@ -650,21 +696,16 @@
         gain_terms = jnp.sum(part_grad * hidden * scale_two, 0)
         grad_branch = grad_hidden.astype(bf16)
         grad_mixed = dot(grad_branch, out_all, 1, 1).astype(bf16)
-        grad_query, *kv_terms = attend_back(
+        grad_query, kv_terms = attend_back(
             info, query, grad_mixed, totals, cosine, sine, kv_pieces
         )
-        return grad_hidden, gain_terms, grad_branch, grad_query, *kv_terms
-
-    def kv_exchange(kv_terms):
-        return [
-            lax.ppermute(kv_terms[s], "ctx", [(j, (j - s) % blocks) for j in range(blocks)])
-            for s in range(1, blocks)
-        ]
-
-    def projected_grad(grad_query, own_terms, other_terms):
-        grad_kv = own_terms.astype(f32)
-        for terms in other_terms:
-            grad_kv = grad_kv + terms.astype(f32)
+        return grad_hidden, gain_terms, grad_branch, grad_query, kv_terms
+
+    def kv_owner(kv_terms):
+        return lax.psum_scatter(kv_terms, "ctx", scatter_dimension=0)
+
+    def projected_grad(grad_query, kv_terms):
+        grad_kv = kv_terms.astype(f32)
         grad_key = grad_kv[0].reshape(rows, KV_HEADS, HEAD)
         rolled = jnp.concatenate([grad_key[..., HEAD // 2 :], grad_key[..., : HEAD // 2]], -1)
         grad_key = grad_key * cosine[:, None, :] - rolled * sine[:, None, :]
@@ -702,48 +743,53 @@
         part_grad = to_owner(mlp_grad)
         gate_terms = column_grad(normed_all, grad_gate, cuts)
         (up_terms,) = column_grad(normed_all, grad_up, 1)
-        mlp_terms = through_rows(act, down_rows, rows)
-        gate_terms, up_terms, mlp_terms = line.round(gate_terms, up_terms, mlp_terms)
+        gate_terms, up_terms, act = line.round(gate_terms, up_terms, act)
         line.add(gate_terms)
         up_terms = to_rows(up_terms)
-        part_grad, mlp_terms = fence(part_grad, mlp_terms)
+        grad_hidden, gain_mlp_terms, grad_branch, grad_query, kv_terms = through_attention(
+            part_grad
+        )
+        grad_hidden, grad_branch, grad_query, mixed_now, kv_terms, up_terms = line.round(
+            grad_hidden, grad_branch, grad_query, mixed, kv_terms, up_terms
+        )
+        kv_terms = kv_owner(kv_terms)
+        out_terms = out_grad(mixed_now, grad_branch)
+        split = width // 2
+        line.add([up_terms[:split], up_terms[split:]])
+        grad_query, out_terms = line.round(grad_query, out_terms)
+        out_terms = to_owner(out_terms)
+        grad_projected = projected_grad(grad_query, kv_terms)
+        qkv_terms = dot(normed, grad_projected, 0, 0).astype(bf16)
+        grad_tokens, gain_attn_terms, bias_terms = to_tokens(grad_projected, grad_hidden)
+        qkv_terms, grad_tokens, gain_attn_terms, bias_terms, act = line.round(
+            qkv_terms, grad_tokens, gain_attn_terms, bias_terms, act
+        )
+        qkv_terms = to_owner(qkv_terms)
+        small = own_sums(gain_attn_terms, gain_mlp_terms, bias_terms)
+        mlp_terms = through_rows(act, down_rows, rows)
+        small, mlp_terms, out_terms = line.round(small, mlp_terms, out_terms)
         mlp_out = to_owner(mlp_terms)
-        grad_hidden, gain_mlp_terms, grad_branch, grad_query, *kv_terms = through_attention(
-            part_grad
-        )
-        others = kv_exchange(kv_terms)
-        out_terms = to_owner(out_grad(mixed, grad_branch))
+        line.add([out_terms])
+        gate_terms = to_rows(jnp.concatenate(line.sums(cuts, 2 * cuts)))
+        (qkv_terms,) = line.round(qkv_terms)
+        line.add([[qkv_terms, small]])
         line.round()
-        grad_query, up_terms = line.round(grad_query, up_terms)
-        line.add([up_terms[: width // 2], up_terms[width // 2 :]])
-        grad_projected = projected_grad(grad_query, kv_terms[0], others)
-        qkv_terms = to_owner(dot(normed, grad_projected, 0, 0).astype(bf16))
-        grad_projected, out_terms = line.round(grad_projected, out_terms)
-        line.add([out_terms])
-        grad_tokens, gain_attn_terms, bias_terms = to_tokens(grad_projected, grad_hidden)
-        small = own_sums(gain_attn_terms, gain_mlp_terms, bias_terms)
-        grad_tokens, small = line.round(grad_tokens, small)
-        gate_terms = to_rows(jnp.concatenate(line.sums(cuts, 2 * cuts)))
-        qkv_terms, mlp_out, hidden = line.round(qkv_terms, mlp_out, hidden)
-        half = shard_rows // 2
-        line.add([[qkv_terms[:half], small], [qkv_terms[half:]]])
-        line.rest()
+        (gate_terms,) = line.round(gate_terms)
         down_sums = line.sums(0, cuts)
-        up_terms = jnp.concatenate(line.sums(2 * cuts, 2 * cuts + 2))
-        out_sum, (qkv_sum, small), (qkv_more,) = line.sums(2 * cuts + 2, 2 * cuts + 5)
-        qkv_sum = jnp.concatenate([qkv_sum, qkv_more])
+        up_sum, up_more, out_sum, (qkv_sum, small) = line.sums(2 * cuts, 2 * cuts + 4)
+        up_terms = jnp.concatenate([up_sum, up_more])
     else:
         part_grad = to_owner(mlp_grad)
         gate_terms = column_grad(normed_all, grad_gate, cuts)
         up_terms = column_grad(normed_all, grad_up, cuts)
         gate_terms, up_terms = (to_rows(jnp.concatenate(t)) for t in (gate_terms, up_terms))
         mlp_out = to_owner(through_rows(activation, down_rows, rows))
-        grad_hidden, gain_mlp_terms, grad_branch, grad_query, *kv_terms = through_attention(
+        grad_hidden, gain_mlp_terms, grad_branch, grad_query, kv_terms = through_attention(
             part_grad
         )
-        others = kv_exchange(kv_terms)
+        kv_terms = kv_owner(kv_terms)
         out_terms = to_owner(out_grad(mixed, grad_branch))
-        grad_projected = projected_grad(grad_query, kv_terms[0], others)
+        grad_projected = projected_grad(grad_query, kv_terms)
         qkv_terms = to_owner(dot(normed, grad_projected, 0, 0).astype(bf16))
         grad_tokens, gain_attn_terms, bias_terms = to_tokens(grad_projected, grad_hidden)
         small = own_sums(gain_attn_terms, gain_mlp_terms, bias_terms)

time: 732 us -> 703 us (0.960)
  blocking collectives: 33.7 us -> 10.5 us
  waiting for transfers between devices: 238 us -> 222 us
  Pallas kernels: 201 us -> 210 us
    ppermute x20 -> x16, waiting for transfers between devices: 132 us -> 87.7 us  [the longest x9 53.8 us: round(): self.outward.append(lax.ppermute(self.totals[-1], 'ctx', [(1, 0), (2, 3)]))]
    all_to_all x1 -> x0, blocking collectives: 23.2 us -> none  [turn(): return lax.all_to_all(parts, 'fsdp', 0, 0)]
    ppermute x10 -> x9, waiting for transfers between devices: 43.7 us -> 65.9 us  [send(): self.inward.append(lax.ppermute(chunk, 'ctx', [(0, 1), (3, 2)]))]
    dynamic_update_slice x14 -> x0, local copies, waits for them, and re-layouts: 17 us -> none  [the longest x8 11.9 us: local(): lax.dynamic_update_slice_in_dim(cot_all, piece, (shard ^ bits) * rows, 0)]
    all_to_all x3 -> x4, waiting for transfers between devices: 0.01 us -> 15.1 us  [turn(): return lax.all_to_all(parts, 'fsdp', 0, 0)]
    ppermute x20 -> x16, starting transfers between devices: 26.9 us -> 17.3 us  [the longest x9 11.8 us: round(): self.outward.append(lax.ppermute(self.totals[-1], 'ctx', [(1, 0), (2, 3)]))]
    unnamed x109 -> x105, local copies, waits for them, and re-layouts: 22.6 us -> 32.2 us
    reduce_scatter x4, waiting for transfers between devices: 10.6 us -> 1 us  [to_owner(): return lax.psum_scatter(terms, 'fsdp', scatter_dimension=0, tiled=True)]
  transfers between devices with their start and end apart: 59 -> 55, of which waited for: 27 -> 25; matrix products, arithmetic and copies ran while one was open for 11% -> 11% of each run, Pallas kernels for 23% -> 26%
where the time goes in v3:
time: 703 us; the launch traced here: 691 us
  waiting for transfers between devices  222 us (32%)
  Pallas kernels  210 us (30%)
  starting transfers between devices  120 us (17%)
  local copies, waits for them, and re-layouts  48.4 us (7%)
  other arithmetic  41.5 us (6%)
  matrix products  23 us (3%)
  between operations  15.4 us (2%)
  blocking collectives  10.5 us (1%)
    ppermute x9, waiting for transfers between devices, send(): self.inward.append(lax.ppermute(chunk, 'ctx', [(0, 1), (3, 2)]))  65.9 us
    ppermute x9, starting transfers between devices, send(): self.inward.append(lax.ppermute(chunk, 'ctx', [(0, 1), (3, 2)]))  54.8 us
    ppermute x9, waiting for transfers between devices, round(): self.outward.append(lax.ppermute(self.totals[-1], 'ctx', [(1, 0), (2, 3)]))  53.8 us
    pallas_call x16, Pallas kernels, one(): pl.pallas_call(kernel, grid=(steps[0],), in_specs=[block] * 2, out_specs=...  49.7 us
    ppermute x3, waiting for transfers between devices, from_chip(): return lax.ppermute(own_cot, 'fsdp', [(j, j ^ chip) for j in range(shards)])  33.9 us
    pallas_call x1, Pallas kernels, feed_forward(): pl.pallas_call(kernel, grid=(steps + width // tile,), in_specs=[pl.BlockS...  33.2 us
    unnamed x105, local copies, waits for them, and re-layouts  32.2 us
    pallas_call x2, Pallas kernels, column_grad(): pl.pallas_call(kernel, grid=(width // tile,), in_specs=[pl.BlockSpec((cou...  27.3 us
  transfers between devices with their start and end apart: 55, of which 25 were waited for; matrix products, arithmetic and copies ran while one was open for 11% of the time, Pallas kernels for 26%

profile of v3, /device:TPU:0, one launch (start us, length us, event | category | flops | bytes accessed | tf_op | source)
XLA Modules:
  0.0 690.7 jit_solution(448706019040812017)
XLA Ops:
  9.4 10.5 %all-gather.1 = bf16[8,1,640]{2,1,0:T(2,128)(2,1)S(1)} all-gather(bf16[1,1,640]{2,1,0:T(2,128)(2,1)S(1)} %reshape.199), channel_id=2, replica_groups=mesh['fsdp'=8,'ctx'=4] {'fsdp'}, dimensions={0}, use_global_device_ids=true | all-gather | bytes 11520 | tf_op jit(solution)/shard_map/all_gather | solution.py:588
  33.1 11.9 %all-to-all-done = bf16[8,64,1152]{2,1,0:T(8,128)(2,1)S(1)} async-done(((bf16[8,64,1152]{2,1,0:T(8,128)(2,1)}), bf16[8,64,1152]{2,1,0:T(8,128)(2,1)S(1)}, u32[]{:S(2)}, u32[]{:S(2)}) %all-to-all-start) | async-done | bytes 1179680 | tf_op jit(solution)/shard_map/all_to_all | solution.py:585
  50.6 21.2 %collective-permute-done = bf16[8,64,1152]{2,1,0:T(8,128)(2,1)} collective-permute-done((bf16[8,64,1152]{2,1,0:T(8,128)(2,1)S(1)}, bf16[8,64,1152]{2,1,0:T(8,128)(2,1)}, u32[]{:S(2)}, u32[]{:S(2)}) %collective-permute-start) | collective-permute-done | bytes 1179680 | tf_op jit(solution)/shard_map/ppermute | solution.py:599
  98.3 10.3 %collective-permute-done.2.refs_2_.refs_6_ = bf16[256,512]{1,0:T(8,128)(2,1)} collective-permute-done((bf16[256,512]{1,0:T(8,128)(2,1)S(1)}, bf16[256,512]{1,0:T(8,128)(2,1)}, u32[]{:S(2)}, u32[]{:S(2)}) %collective-permute-start.2) | collective-permute-done | bytes 262176 | tf_op jit(solution)/shard_map/ppermute | solution.py:615
  118.5 12.5 %shard_map.189 = (bf16[256,1536]{1,0:T(8,128)(2,1)S(1)}, f32[12,1,256]{2,1,0:T(1,128)S(1)}) custom-call(s32[9]{0:T(128)S(1)} %pad_add_fusion.1.info_ref, bf16[256,1536]{1,0:T(8,128)(2,1)S(1)} %copy-done.11, bf16[256,512]{1,0:T(8,128)(2,1)S(1)} %get-tuple-element.153.refs_0_.refs_4_, bf16[256,512]{1,0:T(8,128)(2,1)} %collective-permute-done.1.refs_1_.refs_5_, ...), custom_call_target="tpu_custom_call" | custom-call | flops 1048576 | bytes 65536 | tf_op jit(solution)/shard_map/pallas_call | solution.py:215
  138.2 6.8 collective-permute-done.5.refs_0_
  147.3 27.1 %collective-permute-done.7.refs_3_ = bf16[256,1536]{1,0:T(8,128)(2,1)} collective-permute-done((bf16[256,1536]{1,0:T(8,128)(2,1)}, bf16[256,1536]{1,0:T(8,128)(2,1)}, u32[]{:S(2)}, u32[]{:S(2)}) %collective-permute-start.7) | collective-permute-done | bytes 786464 | tf_op jit(solution)/shard_map/ppermute | solution.py:623
  191.4 9.6 %all-gather.10.cloned.1.call-done.x_ref = bf16[2048,1536]{1,0:T(8,128)(2,1)} async-done(((bf16[256,1536]{1,0:T(8,128)(2,1)}), bf16[2048,1536]{1,0:T(8,128)(2,1)}) %all-gather.10.cloned.1.call-update) | async-done | bytes 6291472 | tf_op jit(solution)/shard_map/all_gather | solution.py:636
  201.0 33.2 %shard_map.192 = (bf16[2048,1152]{1,0:T(8,128)(2,1)}, bf16[2048,1152]{1,0:T(8,128)(2,1)}, bf16[2048,1152]{1,0:T(8,128)(2,1)}, bf16[560,1536]{1,0:T(8,128)(2,1)}, bf16[560,1536]{1,0:T(8,128)(2,1)}) custom-call(bf16[2048,1536]{1,0:T(8,128)(2,1)} %all-gather.10.cloned.1.call-done.x_ref, bf16[2048,1536]{1,0:T(8,128)(2,1)} %copy-done, ...), custom_call_target="tpu_custom_call" | custom-call | flops 1048576 | bytes 65536 | tf_op jit(solution)/shard_map/pallas_call | solution.py:346
  237.7 15.0 %shard_map.193 = (bf16[2048,1152]{1,0:T(8,128)(2,1)}, bf16[2048,1152]{1,0:T(8,128)(2,1)}) custom-call(bf16[2048,1536]{1,0:T(8,128)(2,1)} %copy-done, bf16[1152,1536]{1,0:T(8,128)(2,1)} %concatenate.46.wd_ref, bf16[2048,1152]{1,0:T(8,128)(2,1)} %get-tuple-element.179.tg_ref, bf16[2048,1152]{1,0:T(8,128)(2,1)} %get-tuple-element.180.tu_ref), custom_call_target="tpu_custom_call" | custom-call | flops 1048576 | bytes 65536 | tf_op jit(solution)/shard_map/pallas_call | solution.py:375
  252.7 22.0 %shard_map.194 = bf16[2048,1536]{1,0:T(8,128)(2,1)} custom-call(bf16[2048,1152]{1,0:T(8,128)(2,1)} %get-tuple-element.191.dg_ref.g_ref, bf16[2048,1152]{1,0:T(8,128)(2,1)} %get-tuple-element.194.du_ref.g_ref, bf16[1536,1152]{1,0:T(8,128)(2,1)} %bitcast.51, bf16[1536,1152]{1,0:T(8,128)(2,1)} %bitcast.53), custom_call_target="tpu_custom_call" | custom-call | flops 1048576 | bytes 65536 | tf_op jit(solution)/shard_map/pallas_call | solution.py:401
  289.3 13.7 %shard_map.197 = bf16[1536,1152]{1,0:T(8,128)(2,1)} custom-call(bf16[2048,1536]{1,0:T(8,128)(2,1)} %all-gather.10.cloned.1.call-done.x_ref, bf16[2048,1152]{1,0:T(8,128)(2,1)} %get-tuple-element.194.du_ref.g_ref), custom_call_target="tpu_custom_call" | custom-call | flops 1048576 | bytes 65536 | tf_op jit(solution)/shard_map/pallas_call | solution.py:430
  303.0 13.6 %shard_map.196 = (bf16[768,1152]{1,0:T(8,128)(2,1)}, bf16[768,1152]{1,0:T(8,128)(2,1)}) custom-call(bf16[2048,1536]{1,0:T(8,128)(2,1)} %all-gather.10.cloned.1.call-done.x_ref, bf16[2048,1152]{1,0:T(8,128)(2,1)} %get-tuple-element.191.dg_ref.g_ref), custom_call_target="tpu_custom_call" | custom-call | flops 1048576 | bytes 65536 | tf_op jit(solution)/shard_map/pallas_call | solution.py:430
  353.7 17.0 %shard_map.199 = (bf16[256,1536]{1,0:T(8,128)(2,1)S(1)}, bf16[4,2,256,256]{3,2,1,0:T(8,128)(2,1)S(1)}) custom-call(s32[9]{0:T(128)S(1)} %pad_add_fusion.1.info_ref, bf16[256,1536]{1,0:T(8,128)(2,1)S(1)} %copy-done.12, bf16[256,1536]{1,0:T(8,128)(2,1)S(1)} %convolution_convert_fusion.2.g_ref, f32[12,1,256]{2,1,0:T(1,128)S(1)} %get-tuple-element.204.total_ref, ...), custom_call_target="tpu_custom_call" | custom-call | flops 1048576 | bytes 65536 | tf_op jit(solution)/shard_map/pallas_call | solution.py:279
  381.7 8.0 %collective-permute-start.20 = (bf16[768,1152]{1,0:T(8,128)(2,1)}, bf16[768,1152]{1,0:T(8,128)(2,1)}, u32[]{:S(2)}, u32[]{:S(2)}) collective-permute-start(bf16[768,1152]{1,0:T(8,128)(2,1)} %get-tuple-element.218.a_ref), channel_id=1, source_target_pairs={{0,1},{3,2},{4,5},{7,6},{8,9},{11,10},{12,13},{15,14},{16,17},{19,... | collective-permute-start | bytes 5308424 | tf_op jit(solution)/shard_map/ppermute | solution.py:512
  404.4 38.0 %collective-permute-done.20.b_ref = bf16[768,1152]{1,0:T(8,128)(2,1)} collective-permute-done((bf16[768,1152]{1,0:T(8,128)(2,1)}, bf16[768,1152]{1,0:T(8,128)(2,1)}, u32[]{:S(2)}, u32[]{:S(2)}) %collective-permute-start.20) | collective-permute-done | bytes 1769504 | tf_op jit(solution)/shard_map/ppermute | solution.py:512
  456.9 7.0 %collective-permute-start.23 = (bf16[768,1152]{1,0:T(8,128)(2,1)}, bf16[768,1152]{1,0:T(8,128)(2,1)}, u32[]{:S(2)}, u32[]{:S(2)}) collective-permute-start(bf16[768,1152]{1,0:T(8,128)(2,1)} %get-tuple-element.228.a_ref), channel_id=1, source_target_pairs={{0,1},{3,2},{4,5},{7,6},{8,9},{11,10},{12,13},{15,14},{16,17},{19,... | collective-permute-start | bytes 5308424 | tf_op jit(solution)/shard_map/ppermute | solution.py:512
  483.8 15.8 %collective-permute-done.23.b_ref = bf16[768,1152]{1,0:T(8,128)(2,1)} collective-permute-done((bf16[768,1152]{1,0:T(8,128)(2,1)}, bf16[768,1152]{1,0:T(8,128)(2,1)}, u32[]{:S(2)}, u32[]{:S(2)}) %collective-permute-start.23) | collective-permute-done | bytes 1769504 | tf_op jit(solution)/shard_map/ppermute | solution.py:512
  526.3 12.4 %shard_map.206 = bf16[2048,1536]{1,0:T(8,128)(2,1)} custom-call(bf16[2048,1152]{1,0:T(8,128)(2,1)} %get-tuple-element.246.act_ref, bf16[1152,1536]{1,0:T(8,128)(2,1)} %concatenate.46.wd_ref), custom_call_target="tpu_custom_call" | custom-call | flops 1048576 | bytes 65536 | tf_op jit(solution)/shard_map/pallas_call | solution.py:449
  564.2 11.1 %collective-permute-start.32 = (bf16[192,1536]{1,0:T(8,128)(2,1)}, bf16[192,1536]{1,0:T(8,128)(2,1)}, u32[]{:S(2)}, u32[]{:S(2)}) collective-permute-start(bf16[192,1536]{1,0:T(8,128)(2,1)} %reduce-scatter.10.cloned.1.call-done.a_ref), channel_id=1, source_target_pairs={{0,1},{3,2},{4,5},{7,6},{8,9},{11,10},{12,13},{15,14},{16,17},{19,... | collective-permute-start | bytes 1769480 | tf_op jit(solution)/shard_map/ppermute | solution.py:512
  586.9 14.4 %collective-permute-done.33 = bf16[768,1152]{1,0:T(8,128)(2,1)} collective-permute-done((bf16[768,1152]{1,0:T(8,128)(2,1)}, bf16[768,1152]{1,0:T(8,128)(2,1)}, u32[]{:S(2)}, u32[]{:S(2)}) %collective-permute-start.33) | collective-permute-done | bytes 1769504 | tf_op jit(solution)/shard_map/ppermute | solution.py:534
  607.3 7.0 %collective-permute-start.35 = (bf16[192,2048]{1,0:T(8,128)(2,1)S(1)}, bf16[192,2048]{1,0:T(8,128)(2,1)S(1)}, u32[]{:S(2)}, u32[]{:S(2)}) collective-permute-start(bf16[192,2048]{1,0:T(8,128)(2,1)S(1)} %copy-done.32), channel_id=1, source_target_pairs={{0,1},{3,2},{4,5},{7,6},{8,9},{11,10},{12,13},{15,14},{16,17},{19,... | collective-permute-start | bytes 2359304 | tf_op jit(solution)/shard_map/ppermute | solution.py:512
  628.5 16.5 %collective-permute-done.37 = bf16[768,1152]{1,0:T(8,128)(2,1)S(1)} collective-permute-done((bf16[768,1152]{1,0:T(8,128)(2,1)S(1)}, bf16[768,1152]{1,0:T(8,128)(2,1)S(1)}, u32[]{:S(2)}, u32[]{:S(2)}) %collective-permute-start.37) | collective-permute-done | bytes 1769504 | tf_op jit(solution)/shard_map/ppermute | solution.py:534
  671.6 7.2 %collective-permute-done.41 = f32[640]{0:T(1024)S(1)} collective-permute-done((f32[640]{0:T(1024)S(1)}, f32[640]{0:T(1024)S(1)}, u32[]{:S(2)}, u32[]{:S(2)}) %collective-permute-start.41) | collective-permute-done | bytes 2592 | tf_op jit(solution)/shard_map/ppermute | solution.py:534
  (299 shorter events, 313.7 us)
Async XLA Ops:
  7.2 64.7 %all-gather.6.cloned.1.call-start = ((), (), s32[]{:S(2)}) async-start(), calls=%async_computation.9 | async-start | bytes 7077888 | tf_op jit(solution)/shard_map/all_gather | solution.py:587
  7.9 124.0 %all-gather.8.cloned.1.call-start = ((), (), s32[]{:S(2)}) async-start(), calls=%async_computation.10 | async-start | bytes 5308416 | tf_op jit(solution)/shard_map/all_gather | solution.py:609
  82.1 49.8 %all-to-all-start.1 = ((bf16[8,128,1152]{2,1,0:T(8,128)(2,1)}), bf16[8,128,1152]{2,1,0:T(8,128)(2,1)S(1)}, u32[]{:S(2)}, u32[]{:S(2)}) async-start(bf16[8,128,1152]{2,1,0:T(8,128)(2,1)} %copy-done.3), calls=%async_computation.1 | async-start | bytes 4718592 | tf_op jit(solution)/shard_map/all_to_all | solution.py:585
  87.0 114.0 %all-gather.10.cloned.1.call-start = ((), (), s32[]{:S(2)}) async-start(), calls=%async_computation.11 | async-start | bytes 7077888 | tf_op jit(solution)/shard_map/all_gather | solution.py:636
  145.0 199.0 %reduce-scatter.6.cloned.1.call-start = ((), (), s32[]{:S(2)}) async-start(), calls=%async_computation.12 | async-start | bytes 7077888 | tf_op jit(solution)/shard_map/reduce_scatter | solution.py:686
  234.2 40.9 %collective-permute-start.13 = (bf16[560,1536]{1,0:T(8,128)(2,1)}, bf16[560,1536]{1,0:T(8,128)(2,1)S(1)}, u32[]{:S(2)}, u32[]{:S(2)}) collective-permute-start(bf16[560,1536]{1,0:T(8,128)(2,1)} %get-tuple-element.177.a_ref), channel_id=1, source_target_pairs={{0,1},{3,2},{4,5},{7,6},{8,9},{11,10},{12,13},{15,14},{16,17},{19,... | collective-permute-start | bytes 5160968 | tf_op jit(solution)/shard_map/ppermute | solution.py:512
  277.8 40.7 %collective-permute-start.15 = (bf16[560,1536]{1,0:T(8,128)(2,1)S(1)}, bf16[560,1536]{1,0:T(8,128)(2,1)}, u32[]{:S(2)}, u32[]{:S(2)}) collective-permute-start(bf16[560,1536]{1,0:T(8,128)(2,1)S(1)} %copy-done.22), channel_id=1, source_target_pairs={{0,1},{3,2},{4,5},{7,6},{8,9},{11,10},{12,13},{15,14},{16,17},{19,... | collective-permute-start | bytes 5160968 | tf_op jit(solution)/shard_map/ppermute | solution.py:512
  323.2 52.6 %all-to-all-start.2 = ((bf16[8,192,1152]{2,1,0:T(8,128)(2,1)}), bf16[8,192,1152]{2,1,0:T(8,128)(2,1)}, u32[]{:S(2)}, u32[]{:S(2)}) async-start(bf16[8,192,1152]{2,1,0:T(8,128)(2,1)} %bitcast.58), calls=%async_computation.3 | async-start | bytes 7077888 | tf_op jit(solution)/shard_map/all_to_all | solution.py:585
  328.0 138.1 %reduce-scatter.8.cloned.1.call-start = ((), (), s32[]{:S(2)}) async-start(), calls=%async_computation.13 | async-start | bytes 1310720 | tf_op jit(solution)/shard_map/reduce_scatter | solution.py:705
  328.1 44.5 %collective-permute-start.17 = (bf16[768,1152]{1,0:T(8,128)(2,1)}, bf16[768,1152]{1,0:T(8,128)(2,1)}, u32[]{:S(2)}, u32[]{:S(2)}) collective-permute-start(bf16[768,1152]{1,0:T(8,128)(2,1)} %get-tuple-element.202.a_ref), channel_id=1, source_target_pairs={{0,1},{3,2},{4,5},{7,6},{8,9},{11,10},{12,13},{15,14},{16,17},{19,... | collective-permute-start | bytes 5308424 | tf_op jit(solution)/shard_map/ppermute | solution.py:512
  339.7 41.9 %collective-permute-start.18 = (bf16[560,1536]{1,0:T(8,128)(2,1)}, bf16[560,1536]{1,0:T(8,128)(2,1)}, u32[]{:S(2)}, u32[]{:S(2)}) collective-permute-start(bf16[560,1536]{1,0:T(8,128)(2,1)} %shard_map.201), channel_id=1, source_target_pairs={{1,0},{2,3},{5,4},{6,7},{9,8},{10,11},{13,12},{14,15},{17,16},{18,... | collective-permute-start | bytes 5160968 | tf_op jit(solution)/shard_map/ppermute | solution.py:534
  341.1 40.4 %collective-permute-start.16 = (bf16[560,1536]{1,0:T(8,128)(2,1)S(1)}, bf16[560,1536]{1,0:T(8,128)(2,1)}, u32[]{:S(2)}, u32[]{:S(2)}) collective-permute-start(bf16[560,1536]{1,0:T(8,128)(2,1)S(1)} %shard_map.198.a_ref), channel_id=1, source_target_pairs={{1,2},{2,1},{5,6},{6,5},{9,10},{10,9},{13,14},{14,13},{17,18},{18,... | collective-permute-start | bytes 5160968 | tf_op jit(solution)/shard_map/ppermute | solution.py:536
  381.6 162.4 %reduce-scatter.10.cloned.1.call-start = ((), (), s32[]{:S(2)}) async-start(), calls=%async_computation.14 | async-start | bytes 5308416 | tf_op jit(solution)/shard_map/reduce_scatter | solution.py:686
  381.7 60.8 %collective-permute-start.20 = (bf16[768,1152]{1,0:T(8,128)(2,1)}, bf16[768,1152]{1,0:T(8,128)(2,1)}, u32[]{:S(2)}, u32[]{:S(2)}) collective-permute-start(bf16[768,1152]{1,0:T(8,128)(2,1)} %get-tuple-element.218.a_ref), channel_id=1, source_target_pairs={{0,1},{3,2},{4,5},{7,6},{8,9},{11,10},{12,13},{15,14},{16,17},{19,... | collective-permute-start | bytes 5308424 | tf_op jit(solution)/shard_map/ppermute | solution.py:512
  389.6 60.8 %collective-permute-start.19 = (bf16[768,1152]{1,0:T(8,128)(2,1)}, bf16[768,1152]{1,0:T(8,128)(2,1)}, u32[]{:S(2)}, u32[]{:S(2)}) collective-permute-start(bf16[768,1152]{1,0:T(8,128)(2,1)} %shard_map.200.a_ref), channel_id=1, source_target_pairs={{1,2},{2,1},{5,6},{6,5},{9,10},{10,9},{13,14},{14,13},{17,18},{18,... | collective-permute-start | bytes 5308424 | tf_op jit(solution)/shard_map/ppermute | solution.py:536
  395.9 54.6 %collective-permute-start.21 = (bf16[560,1536]{1,0:T(8,128)(2,1)}, bf16[560,1536]{1,0:T(8,128)(2,1)}, u32[]{:S(2)}, u32[]{:S(2)}) collective-permute-start(bf16[560,1536]{1,0:T(8,128)(2,1)} %shard_map.203), channel_id=1, source_target_pairs={{1,0},{2,3},{5,4},{6,7},{9,8},{10,11},{13,12},{14,15},{17,16},{18,... | collective-permute-start | bytes 5160968 | tf_op jit(solution)/shard_map/ppermute | solution.py:534
  450.5 134.0 %reduce-scatter.14.cloned.1.call-start = ((), (), s32[]{:S(2)}) async-start(), calls=%async_computation.16 | async-start | bytes 7077888 | tf_op jit(solution)/shard_map/reduce_scatter | solution.py:686
  455.6 48.2 %collective-permute-start.24 = (bf16[768,1152]{1,0:T(8,128)(2,1)}, bf16[768,1152]{1,0:T(8,128)(2,1)}, u32[]{:S(2)}, u32[]{:S(2)}) collective-permute-start(bf16[768,1152]{1,0:T(8,128)(2,1)} %shard_map.205), channel_id=1, source_target_pairs={{1,0},{2,3},{5,4},{6,7},{9,8},{10,11},{13,12},{14,15},{17,16},{18,... | collective-permute-start | bytes 5308424 | tf_op jit(solution)/shard_map/ppermute | solution.py:534
  456.9 42.7 %collective-permute-start.23 = (bf16[768,1152]{1,0:T(8,128)(2,1)}, bf16[768,1152]{1,0:T(8,128)(2,1)}, u32[]{:S(2)}, u32[]{:S(2)}) collective-permute-start(bf16[768,1152]{1,0:T(8,128)(2,1)} %get-tuple-element.228.a_ref), channel_id=1, source_target_pairs={{0,1},{3,2},{4,5},{7,6},{8,9},{11,10},{12,13},{15,14},{16,17},{19,... | collective-permute-start | bytes 5308424 | tf_op jit(solution)/shard_map/ppermute | solution.py:512
  503.8 177.4 %reduce-scatter.12.cloned.1.call-start = ((), (), s32[]{:S(2)}) async-start(), calls=%async_computation.15 | async-start | bytes 7077888 | tf_op jit(solution)/shard_map/reduce_scatter | solution.py:686
  559.3 42.0 %collective-permute-start.33 = (bf16[768,1152]{1,0:T(8,128)(2,1)}, bf16[768,1152]{1,0:T(8,128)(2,1)}, u32[]{:S(2)}, u32[]{:S(2)}) collective-permute-start(bf16[768,1152]{1,0:T(8,128)(2,1)} %shard_map.210), channel_id=1, source_target_pairs={{1,0},{2,3},{5,4},{6,7},{9,8},{10,11},{13,12},{14,15},{17,16},{18,... | collective-permute-start | bytes 5308424 | tf_op jit(solution)/shard_map/ppermute | solution.py:534
  560.6 40.7 %collective-permute-start.31 = (bf16[768,1152]{1,0:T(8,128)(2,1)}, bf16[768,1152]{1,0:T(8,128)(2,1)}, u32[]{:S(2)}, u32[]{:S(2)}) collective-permute-start(bf16[768,1152]{1,0:T(8,128)(2,1)} %shard_map.207.a_ref), channel_id=1, source_target_pairs={{1,2},{2,1},{5,6},{6,5},{9,10},{10,9},{13,14},{14,13},{17,18},{18,... | collective-permute-start | bytes 5308424 | tf_op jit(solution)/shard_map/ppermute | solution.py:536
  579.0 75.1 %all-to-all-start.3 = ((bf16[8,192,1152]{2,1,0:T(8,128)(2,1)}), bf16[8,192,1152]{2,1,0:T(8,128)(2,1)S(1)}, u32[]{:S(2)}, u32[]{:S(2)}) async-start(bf16[8,192,1152]{2,1,0:T(8,128)(2,1)} %bitcast.59), calls=%async_computation.8 | async-start | bytes 7077888 | tf_op jit(solution)/shard_map/all_to_all | solution.py:585
  604.2 40.8 %collective-permute-start.37 = (bf16[768,1152]{1,0:T(8,128)(2,1)S(1)}, bf16[768,1152]{1,0:T(8,128)(2,1)S(1)}, u32[]{:S(2)}, u32[]{:S(2)}) collective-permute-start(bf16[768,1152]{1,0:T(8,128)(2,1)S(1)} %shard_map.212), channel_id=1, source_target_pairs={{1,0},{2,3},{5,4},{6,7},{9,8},{10,11},{13,12},{14,15},{17,16},{18,... | collective-permute-start | bytes 5308424 | tf_op jit(solution)/shard_map/ppermute | solution.py:534
  (83 other events, 1064.1 us)
Sparse Core Ops, SparseCore 0:
  9.9 53.7 all-gather.5
  65.6 57.7 all-gather.7
  145.1 55.8 all-gather.9
  276.5 67.4 reduce-scatter.5
  381.7 50.1 reduce-scatter.7
  450.6 54.9 reduce-scatter.9
  510.0 61.7 reduce-scatter.13
  575.2 84.0 reduce-scatter.11

commit v4 on v3

--- a/solution.py
+++ b/solution.py
@@ -474,7 +474,7 @@
         out_ref[...] = (a_ref[...].astype(f32) + b_ref[...].astype(f32)).astype(out_ref.dtype)
 
     def one(a, b):
-        steps = [n for n in (4, 5, 3, 2) if a.ndim == 2 and a.shape[0] % (16 * n) == 0]
+        steps = [n for n in (2, 3, 5) if a.ndim == 2 and a.shape[0] % (16 * n) == 0]
         if not steps:
             return (a.astype(f32) + b.astype(f32)).astype(a.dtype)
         block = pl.BlockSpec((a.shape[0] // steps[0], a.shape[1]), lambda i: (i, 0))
@@ -492,8 +492,6 @@
 
 
 class CtxLine:
-    lead = 1
-
     def __init__(self):
         place = lax.axis_index("ctx")
         self.outer = (place == 0) | (place == 3)
@@ -506,8 +504,11 @@
         self.send()
 
     def send(self):
-        while self.waiting and len(self.chunks) < len(self.pair_sums) + self.lead:
+        ready = len(self.pair_sums)
+        while self.waiting and len(self.chunks) < ready + (2 if ready > 2 else 1):
             chunk = self.waiting.pop(0)
+            if ready > 2:
+                self.inward[-1], chunk = fence(self.inward[-1], chunk)
             self.chunks.append(chunk)
             self.inward.append(lax.ppermute(chunk, "ctx", [(0, 1), (3, 2)]))
 
@@ -518,12 +519,10 @@
         if more:
             self.inward[step], values = fence(self.inward[step], values)
             self.pair_sums.append(added(self.chunks[step], self.inward[step]))
-        ahead = slice(step + 1, step + 2 if step > 2 else step)
         held = [
             (self.across, slice(last, None)),
             (self.pair_sums, slice(last + 1, None)),
             (self.outward, slice(last - 1, None) if last else slice(0, 0)),
-            (self.inward, ahead),
         ]
         fenced, self.waiting, values = fence([array[at] for array, at in held], self.waiting, values)
         for (array, at), value in zip(held, fenced):
@@ -749,16 +748,16 @@
         grad_hidden, gain_mlp_terms, grad_branch, grad_query, kv_terms = through_attention(
             part_grad
         )
+        kv_sums = kv_owner(kv_terms)
         grad_hidden, grad_branch, grad_query, mixed_now, kv_terms, up_terms = line.round(
             grad_hidden, grad_branch, grad_query, mixed, kv_terms, up_terms
         )
-        kv_terms = kv_owner(kv_terms)
         out_terms = out_grad(mixed_now, grad_branch)
         split = width // 2
         line.add([up_terms[:split], up_terms[split:]])
         grad_query, out_terms = line.round(grad_query, out_terms)
         out_terms = to_owner(out_terms)
-        grad_projected = projected_grad(grad_query, kv_terms)
+        grad_projected = projected_grad(grad_query, kv_sums)
         qkv_terms = dot(normed, grad_projected, 0, 0).astype(bf16)
         grad_tokens, gain_attn_terms, bias_terms = to_tokens(grad_projected, grad_hidden)
         qkv_terms, grad_tokens, gain_attn_terms, bias_terms, act = line.round(

time: 703 us -> 693 us (0.986)
  Pallas kernels: 210 us -> 200 us
  waiting for transfers between devices: 222 us -> 232 us
    ppermute x9, waiting for transfers between devices: 65.9 us -> 76.8 us  [send(): self.inward.append(lax.ppermute(chunk, 'ctx', [(0, 1), (3, 2)]))]
    pallas_call x16, Pallas kernels: 49.7 us -> 39.9 us  [one(): pl.pallas_call(kernel, grid=(steps[0],), in_specs=[block] * 2, out_specs=...]
    unnamed x105 -> x101, local copies, waits for them, and re-layouts: 32.2 us -> 30.7 us
  transfers between devices with their start and end apart: 55 -> 55, of which waited for: 25 -> 24; matrix products, arithmetic and copies ran while one was open for 11% -> 11% of each run, Pallas kernels for 26% -> 24%
where the time goes in v4:
time: 693 us; the launch traced here: 685 us
  waiting for transfers between devices  232 us (33%)
  Pallas kernels  200 us (29%)
  starting transfers between devices  116 us (17%)
  local copies, waits for them, and re-layouts  46.8 us (7%)
  other arithmetic  41.5 us (6%)
  matrix products  23 us (3%)
  between operations  15.4 us (2%)
  blocking collectives  10.5 us (2%)
    ppermute x9, waiting for transfers between devices, send(): self.inward.append(lax.ppermute(chunk, 'ctx', [(0, 1), (3, 2)]))  76.8 us
    ppermute x9, waiting for transfers between devices, round(): self.outward.append(lax.ppermute(self.totals[-1], 'ctx', [(1, 0), (2, 3)]))  56.1 us
    ppermute x9, starting transfers between devices, send(): self.inward.append(lax.ppermute(chunk, 'ctx', [(0, 1), (3, 2)]))  53.3 us
    pallas_call x16, Pallas kernels, one(): pl.pallas_call(kernel, grid=(steps[0],), in_specs=[block] * 2, out_specs=...  39.9 us
    ppermute x3, waiting for transfers between devices, from_chip(): return lax.ppermute(own_cot, 'fsdp', [(j, j ^ chip) for j in range(shards)])  33.9 us
    pallas_call x1, Pallas kernels, feed_forward(): pl.pallas_call(kernel, grid=(steps + width // tile,), in_specs=[pl.BlockS...  33.2 us
    unnamed x101, local copies, waits for them, and re-layouts  30.7 us
    pallas_call x2, Pallas kernels, column_grad(): pl.pallas_call(kernel, grid=(width // tile,), in_specs=[pl.BlockSpec((cou...  27.3 us
  transfers between devices with their start and end apart: 55, of which 24 were waited for; matrix products, arithmetic and copies ran while one was open for 11% of the time, Pallas kernels for 24%

profile of v4, /device:TPU:0, one launch (start us, length us, event | category | flops | bytes accessed | tf_op | source)
XLA Modules:
  0.0 685.2 jit_solution(2939609053674568740)
XLA Ops:
  9.4 10.5 %all-gather.1 = bf16[8,1,640]{2,1,0:T(2,128)(2,1)S(1)} all-gather(bf16[1,1,640]{2,1,0:T(2,128)(2,1)S(1)} %reshape.199), channel_id=2, replica_groups=mesh['fsdp'=8,'ctx'=4] {'fsdp'}, dimensions={0}, use_global_device_ids=true | all-gather | bytes 11520 | tf_op jit(solution)/shard_map/all_gather | solution.py:587
  33.1 11.9 %all-to-all-done = bf16[8,64,1152]{2,1,0:T(8,128)(2,1)S(1)} async-done(((bf16[8,64,1152]{2,1,0:T(8,128)(2,1)}), bf16[8,64,1152]{2,1,0:T(8,128)(2,1)S(1)}, u32[]{:S(2)}, u32[]{:S(2)}) %all-to-all-start) | async-done | bytes 1179680 | tf_op jit(solution)/shard_map/all_to_all | solution.py:584
  50.6 21.2 %collective-permute-done = bf16[8,64,1152]{2,1,0:T(8,128)(2,1)} collective-permute-done((bf16[8,64,1152]{2,1,0:T(8,128)(2,1)S(1)}, bf16[8,64,1152]{2,1,0:T(8,128)(2,1)}, u32[]{:S(2)}, u32[]{:S(2)}) %collective-permute-start) | collective-permute-done | bytes 1179680 | tf_op jit(solution)/shard_map/ppermute | solution.py:598
  98.3 10.3 %collective-permute-done.2.refs_2_.refs_6_ = bf16[256,512]{1,0:T(8,128)(2,1)} collective-permute-done((bf16[256,512]{1,0:T(8,128)(2,1)S(1)}, bf16[256,512]{1,0:T(8,128)(2,1)}, u32[]{:S(2)}, u32[]{:S(2)}) %collective-permute-start.2) | collective-permute-done | bytes 262176 | tf_op jit(solution)/shard_map/ppermute | solution.py:614
  118.5 12.5 %shard_map.189 = (bf16[256,1536]{1,0:T(8,128)(2,1)S(1)}, f32[12,1,256]{2,1,0:T(1,128)S(1)}) custom-call(s32[9]{0:T(128)S(1)} %pad_add_fusion.1.info_ref, bf16[256,1536]{1,0:T(8,128)(2,1)S(1)} %copy-done.11, bf16[256,512]{1,0:T(8,128)(2,1)S(1)} %get-tuple-element.157.refs_0_.refs_4_, bf16[256,512]{1,0:T(8,128)(2,1)} %collective-permute-done.1.refs_1_.refs_5_, ...), custom_call_target="tpu_custom_call" | custom-call | flops 1048576 | bytes 65536 | tf_op jit(solution)/shard_map/pallas_call | solution.py:215
  147.3 27.1 %collective-permute-done.7.refs_3_ = bf16[256,1536]{1,0:T(8,128)(2,1)} collective-permute-done((bf16[256,1536]{1,0:T(8,128)(2,1)}, bf16[256,1536]{1,0:T(8,128)(2,1)}, u32[]{:S(2)}, u32[]{:S(2)}) %collective-permute-start.7) | collective-permute-done | bytes 786464 | tf_op jit(solution)/shard_map/ppermute | solution.py:622
  191.4 9.6 %all-gather.10.cloned.1.call-done.x_ref = bf16[2048,1536]{1,0:T(8,128)(2,1)} async-done(((bf16[256,1536]{1,0:T(8,128)(2,1)}), bf16[2048,1536]{1,0:T(8,128)(2,1)}) %all-gather.10.cloned.1.call-update) | async-done | bytes 6291472 | tf_op jit(solution)/shard_map/all_gather | solution.py:635
  201.0 33.2 %shard_map.192 = (bf16[2048,1152]{1,0:T(8,128)(2,1)}, bf16[2048,1152]{1,0:T(8,128)(2,1)}, bf16[2048,1152]{1,0:T(8,128)(2,1)}, bf16[560,1536]{1,0:T(8,128)(2,1)}, bf16[560,1536]{1,0:T(8,128)(2,1)}) custom-call(bf16[2048,1536]{1,0:T(8,128)(2,1)} %all-gather.10.cloned.1.call-done.x_ref, bf16[2048,1536]{1,0:T(8,128)(2,1)} %copy-done, ...), custom_call_target="tpu_custom_call" | custom-call | flops 1048576 | bytes 65536 | tf_op jit(solution)/shard_map/pallas_call | solution.py:346
  237.7 15.0 %shard_map.193 = (bf16[2048,1152]{1,0:T(8,128)(2,1)}, bf16[2048,1152]{1,0:T(8,128)(2,1)}) custom-call(bf16[2048,1536]{1,0:T(8,128)(2,1)} %copy-done, bf16[1152,1536]{1,0:T(8,128)(2,1)} %concatenate.46.wd_ref, bf16[2048,1152]{1,0:T(8,128)(2,1)} %get-tuple-element.183.tg_ref, bf16[2048,1152]{1,0:T(8,128)(2,1)} %get-tuple-element.184.tu_ref), custom_call_target="tpu_custom_call" | custom-call | flops 1048576 | bytes 65536 | tf_op jit(solution)/shard_map/pallas_call | solution.py:375
  252.8 22.0 %shard_map.194 = bf16[2048,1536]{1,0:T(8,128)(2,1)} custom-call(bf16[2048,1152]{1,0:T(8,128)(2,1)} %get-tuple-element.195.dg_ref.g_ref, bf16[2048,1152]{1,0:T(8,128)(2,1)} %get-tuple-element.198.du_ref.g_ref, bf16[1536,1152]{1,0:T(8,128)(2,1)} %bitcast.51, bf16[1536,1152]{1,0:T(8,128)(2,1)} %bitcast.53), custom_call_target="tpu_custom_call" | custom-call | flops 1048576 | bytes 65536 | tf_op jit(solution)/shard_map/pallas_call | solution.py:401
  289.2 13.7 %shard_map.197 = bf16[1536,1152]{1,0:T(8,128)(2,1)} custom-call(bf16[2048,1536]{1,0:T(8,128)(2,1)} %all-gather.10.cloned.1.call-done.x_ref, bf16[2048,1152]{1,0:T(8,128)(2,1)} %get-tuple-element.198.du_ref.g_ref), custom_call_target="tpu_custom_call" | custom-call | flops 1048576 | bytes 65536 | tf_op jit(solution)/shard_map/pallas_call | solution.py:430
  302.9 13.6 %shard_map.196 = (bf16[768,1152]{1,0:T(8,128)(2,1)}, bf16[768,1152]{1,0:T(8,128)(2,1)}) custom-call(bf16[2048,1536]{1,0:T(8,128)(2,1)} %all-gather.10.cloned.1.call-done.x_ref, bf16[2048,1152]{1,0:T(8,128)(2,1)} %get-tuple-element.195.dg_ref.g_ref), custom_call_target="tpu_custom_call" | custom-call | flops 1048576 | bytes 65536 | tf_op jit(solution)/shard_map/pallas_call | solution.py:430
  335.3 7.0 %collective-permute-start.17 = (bf16[768,1152]{1,0:T(8,128)(2,1)}, bf16[768,1152]{1,0:T(8,128)(2,1)}, u32[]{:S(2)}, u32[]{:S(2)}) collective-permute-start(bf16[768,1152]{1,0:T(8,128)(2,1)} %get-tuple-element.206.a_ref), channel_id=1, source_target_pairs={{0,1},{3,2},{4,5},{7,6},{8,9},{11,10},{12,13},{15,14},{16,17},{19,... | collective-permute-start | bytes 5308424 | tf_op jit(solution)/shard_map/ppermute | solution.py:513
  353.9 17.0 %shard_map.199 = (bf16[256,1536]{1,0:T(8,128)(2,1)S(1)}, bf16[4,2,256,256]{3,2,1,0:T(8,128)(2,1)S(1)}) custom-call(s32[9]{0:T(128)S(1)} %pad_add_fusion.1.info_ref, bf16[256,1536]{1,0:T(8,128)(2,1)S(1)} %copy-done.12, bf16[256,1536]{1,0:T(8,128)(2,1)S(1)} %convolution_convert_fusion.2.g_ref, f32[12,1,256]{2,1,0:T(1,128)S(1)} %get-tuple-element.208.total_ref, ...), custom_call_target="tpu_custom_call" | custom-call | flops 1048576 | bytes 65536 | tf_op jit(solution)/shard_map/pallas_call | solution.py:279
  372.9 6.9 %collective-permute-done.17.b_ref = bf16[768,1152]{1,0:T(8,128)(2,1)} collective-permute-done((bf16[768,1152]{1,0:T(8,128)(2,1)}, bf16[768,1152]{1,0:T(8,128)(2,1)}, u32[]{:S(2)}, u32[]{:S(2)}) %collective-permute-start.17) | collective-permute-done | bytes 1769504 | tf_op jit(solution)/shard_map/ppermute | solution.py:513
  403.3 38.8 %collective-permute-done.20.b_ref = bf16[768,1152]{1,0:T(8,128)(2,1)} collective-permute-done((bf16[768,1152]{1,0:T(8,128)(2,1)}, bf16[768,1152]{1,0:T(8,128)(2,1)}, u32[]{:S(2)}, u32[]{:S(2)}) %collective-permute-start.20) | collective-permute-done | bytes 1769504 | tf_op jit(solution)/shard_map/ppermute | solution.py:513
  452.5 7.1 %collective-permute-start.23 = (bf16[768,1152]{1,0:T(8,128)(2,1)}, bf16[768,1152]{1,0:T(8,128)(2,1)}, u32[]{:S(2)}, u32[]{:S(2)}) collective-permute-start(bf16[768,1152]{1,0:T(8,128)(2,1)} %get-tuple-element.233.a_ref), channel_id=1, source_target_pairs={{0,1},{3,2},{4,5},{7,6},{8,9},{11,10},{12,13},{15,14},{16,17},{19,... | collective-permute-start | bytes 5308424 | tf_op jit(solution)/shard_map/ppermute | solution.py:513
  479.4 16.3 %collective-permute-done.23.b_ref = bf16[768,1152]{1,0:T(8,128)(2,1)} collective-permute-done((bf16[768,1152]{1,0:T(8,128)(2,1)}, bf16[768,1152]{1,0:T(8,128)(2,1)}, u32[]{:S(2)}, u32[]{:S(2)}) %collective-permute-start.23) | collective-permute-done | bytes 1769504 | tf_op jit(solution)/shard_map/ppermute | solution.py:513
  520.5 12.5 %shard_map.206 = bf16[2048,1536]{1,0:T(8,128)(2,1)} custom-call(bf16[2048,1152]{1,0:T(8,128)(2,1)} %get-tuple-element.251.act_ref, bf16[1152,1536]{1,0:T(8,128)(2,1)} %concatenate.46.wd_ref), custom_call_target="tpu_custom_call" | custom-call | flops 1048576 | bytes 65536 | tf_op jit(solution)/shard_map/pallas_call | solution.py:449
  558.1 10.7 %collective-permute-start.32 = (bf16[192,1536]{1,0:T(8,128)(2,1)}, bf16[192,1536]{1,0:T(8,128)(2,1)}, u32[]{:S(2)}, u32[]{:S(2)}) collective-permute-start(bf16[192,1536]{1,0:T(8,128)(2,1)} %reduce-scatter.10.cloned.1.call-done.a_ref), channel_id=1, source_target_pairs={{0,1},{3,2},{4,5},{7,6},{8,9},{11,10},{12,13},{15,14},{16,17},{19,... | collective-permute-start | bytes 1769480 | tf_op jit(solution)/shard_map/ppermute | solution.py:513
  578.7 16.6 %collective-permute-done.33 = bf16[768,1152]{1,0:T(8,128)(2,1)} collective-permute-done((bf16[768,1152]{1,0:T(8,128)(2,1)}, bf16[768,1152]{1,0:T(8,128)(2,1)}, u32[]{:S(2)}, u32[]{:S(2)}) %collective-permute-start.33) | collective-permute-done | bytes 1769504 | tf_op jit(solution)/shard_map/ppermute | solution.py:533
  622.2 17.0 %collective-permute-done.37 = bf16[768,1152]{1,0:T(8,128)(2,1)S(1)} collective-permute-done((bf16[768,1152]{1,0:T(8,128)(2,1)S(1)}, bf16[768,1152]{1,0:T(8,128)(2,1)S(1)}, u32[]{:S(2)}, u32[]{:S(2)}) %collective-permute-start.37) | collective-permute-done | bytes 1769504 | tf_op jit(solution)/shard_map/ppermute | solution.py:533
  647.8 7.5 %collective-permute-done.40 = bf16[192,1536]{1,0:T(8,128)(2,1)} collective-permute-done((bf16[192,1536]{1,0:T(8,128)(2,1)}, bf16[192,1536]{1,0:T(8,128)(2,1)}, u32[]{:S(2)}, u32[]{:S(2)}) %collective-permute-start.40) | collective-permute-done | bytes 589856 | tf_op jit(solution)/shard_map/ppermute | solution.py:533
  665.2 8.1 %collective-permute-done.41 = f32[640]{0:T(1024)S(1)} collective-permute-done((f32[640]{0:T(1024)S(1)}, f32[640]{0:T(1024)S(1)}, u32[]{:S(2)}, u32[]{:S(2)}) %collective-permute-start.41) | collective-permute-done | bytes 2592 | tf_op jit(solution)/shard_map/ppermute | solution.py:533
  (295 shorter events, 303.8 us)
Async XLA Ops:
  7.2 64.7 %all-gather.6.cloned.1.call-start = ((), (), s32[]{:S(2)}) async-start(), calls=%async_computation.9 | async-start | bytes 7077888 | tf_op jit(solution)/shard_map/all_gather | solution.py:586
  7.9 124.0 %all-gather.8.cloned.1.call-start = ((), (), s32[]{:S(2)}) async-start(), calls=%async_computation.10 | async-start | bytes 5308416 | tf_op jit(solution)/shard_map/all_gather | solution.py:608
  82.1 49.8 %all-to-all-start.1 = ((bf16[8,128,1152]{2,1,0:T(8,128)(2,1)}), bf16[8,128,1152]{2,1,0:T(8,128)(2,1)S(1)}, u32[]{:S(2)}, u32[]{:S(2)}) async-start(bf16[8,128,1152]{2,1,0:T(8,128)(2,1)} %copy-done.3), calls=%async_computation.1 | async-start | bytes 4718592 | tf_op jit(solution)/shard_map/all_to_all | solution.py:584
  87.0 114.0 %all-gather.10.cloned.1.call-start = ((), (), s32[]{:S(2)}) async-start(), calls=%async_computation.11 | async-start | bytes 7077888 | tf_op jit(solution)/shard_map/all_gather | solution.py:635
  145.0 199.2 %reduce-scatter.6.cloned.1.call-start = ((), (), s32[]{:S(2)}) async-start(), calls=%async_computation.12 | async-start | bytes 7077888 | tf_op jit(solution)/shard_map/reduce_scatter | solution.py:685
  234.2 40.9 %collective-permute-start.13 = (bf16[560,1536]{1,0:T(8,128)(2,1)}, bf16[560,1536]{1,0:T(8,128)(2,1)S(1)}, u32[]{:S(2)}, u32[]{:S(2)}) collective-permute-start(bf16[560,1536]{1,0:T(8,128)(2,1)} %get-tuple-element.181.a_ref), channel_id=1, source_target_pairs={{0,1},{3,2},{4,5},{7,6},{8,9},{11,10},{12,13},{15,14},{16,17},{19,... | collective-permute-start | bytes 5160968 | tf_op jit(solution)/shard_map/ppermute | solution.py:513
  277.8 40.7 %collective-permute-start.15 = (bf16[560,1536]{1,0:T(8,128)(2,1)S(1)}, bf16[560,1536]{1,0:T(8,128)(2,1)}, u32[]{:S(2)}, u32[]{:S(2)}) collective-permute-start(bf16[560,1536]{1,0:T(8,128)(2,1)S(1)} %copy-done.20), channel_id=1, source_target_pairs={{0,1},{3,2},{4,5},{7,6},{8,9},{11,10},{12,13},{15,14},{16,17},{19,... | collective-permute-start | bytes 5160968 | tf_op jit(solution)/shard_map/ppermute | solution.py:513
  323.2 56.5 %all-to-all-start.2 = ((bf16[8,192,1152]{2,1,0:T(8,128)(2,1)}), bf16[8,192,1152]{2,1,0:T(8,128)(2,1)}, u32[]{:S(2)}, u32[]{:S(2)}) async-start(bf16[8,192,1152]{2,1,0:T(8,128)(2,1)} %bitcast.58), calls=%async_computation.3 | async-start | bytes 7077888 | tf_op jit(solution)/shard_map/all_to_all | solution.py:584
  328.0 133.7 %reduce-scatter.8.cloned.1.call-start = ((), (), s32[]{:S(2)}) async-start(), calls=%async_computation.13 | async-start | bytes 1310720 | tf_op jit(solution)/shard_map/reduce_scatter | solution.py:704
  333.9 48.9 %collective-permute-start.18 = (bf16[560,1536]{1,0:T(8,128)(2,1)}, bf16[560,1536]{1,0:T(8,128)(2,1)}, u32[]{:S(2)}, u32[]{:S(2)}) collective-permute-start(bf16[560,1536]{1,0:T(8,128)(2,1)} %shard_map.201), channel_id=1, source_target_pairs={{1,0},{2,3},{5,4},{6,7},{9,8},{10,11},{13,12},{14,15},{17,16},{18,... | collective-permute-start | bytes 5160968 | tf_op jit(solution)/shard_map/ppermute | solution.py:533
  335.3 44.4 %collective-permute-start.17 = (bf16[768,1152]{1,0:T(8,128)(2,1)}, bf16[768,1152]{1,0:T(8,128)(2,1)}, u32[]{:S(2)}, u32[]{:S(2)}) collective-permute-start(bf16[768,1152]{1,0:T(8,128)(2,1)} %get-tuple-element.206.a_ref), channel_id=1, source_target_pairs={{0,1},{3,2},{4,5},{7,6},{8,9},{11,10},{12,13},{15,14},{16,17},{19,... | collective-permute-start | bytes 5308424 | tf_op jit(solution)/shard_map/ppermute | solution.py:513
  372.8 166.7 %reduce-scatter.10.cloned.1.call-start = ((), (), s32[]{:S(2)}) async-start(), calls=%async_computation.14 | async-start | bytes 5308416 | tf_op jit(solution)/shard_map/reduce_scatter | solution.py:685
  382.8 59.3 %collective-permute-start.20 = (bf16[768,1152]{1,0:T(8,128)(2,1)}, bf16[768,1152]{1,0:T(8,128)(2,1)}, u32[]{:S(2)}, u32[]{:S(2)}) collective-permute-start(bf16[768,1152]{1,0:T(8,128)(2,1)} %get-tuple-element.222.a_ref), channel_id=1, source_target_pairs={{0,1},{3,2},{4,5},{7,6},{8,9},{11,10},{12,13},{15,14},{16,17},{19,... | collective-permute-start | bytes 5308424 | tf_op jit(solution)/shard_map/ppermute | solution.py:513
  388.7 58.4 %collective-permute-start.19 = (bf16[768,1152]{1,0:T(8,128)(2,1)}, bf16[768,1152]{1,0:T(8,128)(2,1)}, u32[]{:S(2)}, u32[]{:S(2)}) collective-permute-start(bf16[768,1152]{1,0:T(8,128)(2,1)} %shard_map.200.a_ref), channel_id=1, source_target_pairs={{1,2},{2,1},{5,6},{6,5},{9,10},{10,9},{13,14},{14,13},{17,18},{18,... | collective-permute-start | bytes 5308424 | tf_op jit(solution)/shard_map/ppermute | solution.py:535
  394.9 52.2 %collective-permute-start.21 = (bf16[560,1536]{1,0:T(8,128)(2,1)}, bf16[560,1536]{1,0:T(8,128)(2,1)}, u32[]{:S(2)}, u32[]{:S(2)}) collective-permute-start(bf16[560,1536]{1,0:T(8,128)(2,1)} %shard_map.203), channel_id=1, source_target_pairs={{1,0},{2,3},{5,4},{6,7},{9,8},{10,11},{13,12},{14,15},{17,16},{18,... | collective-permute-start | bytes 5160968 | tf_op jit(solution)/shard_map/ppermute | solution.py:533
  447.1 130.4 %reduce-scatter.14.cloned.1.call-start = ((), (), s32[]{:S(2)}) async-start(), calls=%async_computation.16 | async-start | bytes 7077888 | tf_op jit(solution)/shard_map/reduce_scatter | solution.py:685
  451.2 47.6 %collective-permute-start.24 = (bf16[768,1152]{1,0:T(8,128)(2,1)}, bf16[768,1152]{1,0:T(8,128)(2,1)}, u32[]{:S(2)}, u32[]{:S(2)}) collective-permute-start(bf16[768,1152]{1,0:T(8,128)(2,1)} %shard_map.205), channel_id=1, source_target_pairs={{1,0},{2,3},{5,4},{6,7},{9,8},{10,11},{13,12},{14,15},{17,16},{18,... | collective-permute-start | bytes 5308424 | tf_op jit(solution)/shard_map/ppermute | solution.py:533
  452.5 43.2 %collective-permute-start.23 = (bf16[768,1152]{1,0:T(8,128)(2,1)}, bf16[768,1152]{1,0:T(8,128)(2,1)}, u32[]{:S(2)}, u32[]{:S(2)}) collective-permute-start(bf16[768,1152]{1,0:T(8,128)(2,1)} %get-tuple-element.233.a_ref), channel_id=1, source_target_pairs={{0,1},{3,2},{4,5},{7,6},{8,9},{11,10},{12,13},{15,14},{16,17},{19,... | collective-permute-start | bytes 5308424 | tf_op jit(solution)/shard_map/ppermute | solution.py:513
  498.9 176.8 %reduce-scatter.12.cloned.1.call-start = ((), (), s32[]{:S(2)}) async-start(), calls=%async_computation.15 | async-start | bytes 7077888 | tf_op jit(solution)/shard_map/reduce_scatter | solution.py:685
  499.0 40.6 %collective-permute-start.26 = (bf16[768,1152]{1,0:T(8,128)(2,1)S(1)}, bf16[768,1152]{1,0:T(8,128)(2,1)}, u32[]{:S(2)}, u32[]{:S(2)}) collective-permute-start(bf16[768,1152]{1,0:T(8,128)(2,1)S(1)} %get-tuple-element.248.a_ref), channel_id=1, source_target_pairs={{0,1},{3,2},{4,5},{7,6},{8,9},{11,10},{12,13},{15,14},{16,17},{19,... | collective-permute-start | bytes 5308424 | tf_op jit(solution)/shard_map/ppermute | solution.py:513
  553.3 42.1 %collective-permute-start.33 = (bf16[768,1152]{1,0:T(8,128)(2,1)}, bf16[768,1152]{1,0:T(8,128)(2,1)}, u32[]{:S(2)}, u32[]{:S(2)}) collective-permute-start(bf16[768,1152]{1,0:T(8,128)(2,1)} %shard_map.210), channel_id=1, source_target_pairs={{1,0},{2,3},{5,4},{6,7},{9,8},{10,11},{13,12},{14,15},{17,16},{18,... | collective-permute-start | bytes 5308424 | tf_op jit(solution)/shard_map/ppermute | solution.py:533
  554.5 40.8 %collective-permute-start.31 = (bf16[768,1152]{1,0:T(8,128)(2,1)}, bf16[768,1152]{1,0:T(8,128)(2,1)}, u32[]{:S(2)}, u32[]{:S(2)}) collective-permute-start(bf16[768,1152]{1,0:T(8,128)(2,1)} %shard_map.207.a_ref), channel_id=1, source_target_pairs={{1,2},{2,1},{5,6},{6,5},{9,10},{10,9},{13,14},{14,13},{17,18},{18,... | collective-permute-start | bytes 5308424 | tf_op jit(solution)/shard_map/ppermute | solution.py:535
  572.6 75.2 %all-to-all-start.3 = ((bf16[8,192,1152]{2,1,0:T(8,128)(2,1)}), bf16[8,192,1152]{2,1,0:T(8,128)(2,1)S(1)}, u32[]{:S(2)}, u32[]{:S(2)}) async-start(bf16[8,192,1152]{2,1,0:T(8,128)(2,1)} %bitcast.59), calls=%async_computation.8 | async-start | bytes 7077888 | tf_op jit(solution)/shard_map/all_to_all | solution.py:584
  597.7 41.5 %collective-permute-start.37 = (bf16[768,1152]{1,0:T(8,128)(2,1)S(1)}, bf16[768,1152]{1,0:T(8,128)(2,1)S(1)}, u32[]{:S(2)}, u32[]{:S(2)}) collective-permute-start(bf16[768,1152]{1,0:T(8,128)(2,1)S(1)} %shard_map.212), channel_id=1, source_target_pairs={{1,0},{2,3},{5,4},{6,7},{9,8},{10,11},{13,12},{14,15},{17,16},{18,... | collective-permute-start | bytes 5308424 | tf_op jit(solution)/shard_map/ppermute | solution.py:533
  (81 other events, 1015.2 us)
Sparse Core Ops, SparseCore 0:
  9.9 53.7 all-gather.5
  65.6 57.7 all-gather.7
  145.1 55.8 all-gather.9
  276.5 67.4 reduce-scatter.5
  372.9 53.5 reduce-scatter.7
  447.2 54.6 reduce-scatter.9
  506.2 61.7 reduce-scatter.13
  571.3 80.0 reduce-scatter.11

commit v5 on v4

--- a/solution.py
+++ b/solution.py
@@ -227,6 +227,45 @@
         compiler_params=kernel_params(32),
         cost_estimate=light,
     )(info, query, *kv_pieces, *kv_pieces)
+
+
+def norm_back(part_grad, cotangent, hidden, gain, out_all):
+    rows, width = hidden.shape
+    tile = 256
+
+    def kernel(p_ref, c_ref, h_ref, gain_ref, w_ref, gh_ref, gain_out_ref, branch_ref, mixed_ref):
+        @pl.when(pl.program_id(0) == 0)
+        def _():
+            part, h = p_ref[...].astype(f32), h_ref[...]
+            scale = lax.rsqrt(jnp.mean(h * h, -1, keepdims=True) + norm_eps)
+            scaled = part * gain_ref[...]
+            grad = (
+                c_ref[...].astype(f32)
+                + scale * scaled
+                - h * (scale * scale * scale) * jnp.mean(h * scaled, -1, keepdims=True)
+            )
+            gh_ref[...] = grad
+            gain_out_ref[...] = jnp.sum(part * h * scale, 0, keepdims=True)
+            branch_ref[...] = grad.astype(bf16)
+
+        mixed_ref[...] = dot(branch_ref[...], w_ref[...], 1, 1).astype(bf16)
+
+    return pl.pallas_call(
+        kernel,
+        grid=(out_all.shape[0] // tile,),
+        in_specs=[whole((rows, width))] * 3
+        + [whole((1, width)), pl.BlockSpec((tile, width), lambda i: (i, 0))],
+        out_specs=[whole((rows, width)), whole((1, width)), whole((rows, width))]
+        + [pl.BlockSpec((rows, tile), lambda i: (0, i))],
+        out_shape=[
+            jax.ShapeDtypeStruct((rows, width), f32),
+            jax.ShapeDtypeStruct((1, width), f32),
+            jax.ShapeDtypeStruct((rows, width), bf16),
+            jax.ShapeDtypeStruct((rows, out_all.shape[0]), bf16),
+        ],
+        compiler_params=kernel_params(32),
+        cost_estimate=light,
+    )(part_grad, cotangent, hidden, gain, out_all)
 
 
 def attend_back(info, query, grad_mixed, totals, cosine, sine, kv_pieces):
@@ -685,16 +724,10 @@
         return lax.psum_scatter(terms, "fsdp", scatter_dimension=0, tiled=True)
 
     def through_attention(part_grad):
-        part_grad = part_grad.astype(f32)
-        scaled = part_grad * gain_mlp
-        grad_hidden = (
-            cotangent.astype(f32)
-            + scale_two * scaled
-            - hidden * scale_two**3 * jnp.mean(hidden * scaled, -1, keepdims=True)
-        )
-        gain_terms = jnp.sum(part_grad * hidden * scale_two, 0)
-        grad_branch = grad_hidden.astype(bf16)
-        grad_mixed = dot(grad_branch, out_all, 1, 1).astype(bf16)
+        grad_hidden, gain_terms, grad_branch, grad_mixed = norm_back(
+            part_grad, cotangent, hidden, gain_mlp, out_all
+        )
+        gain_terms = gain_terms[0]
         grad_query, kv_terms = attend_back(
             info, query, grad_mixed, totals, cosine, sine, kv_pieces
         )

time: 693 us -> 689 us (level)
  waiting for transfers between devices: 232 us -> 200 us
  starting transfers between devices: 116 us -> 139 us
  Pallas kernels: 200 us -> 208 us
    ppermute x9, waiting for transfers between devices: 76.8 us -> 42.9 us  [send(): self.inward.append(lax.ppermute(chunk, 'ctx', [(0, 1), (3, 2)]))]
    all_to_all x4, starting transfers between devices: 17.3 us -> 30.8 us  [turn(): return lax.all_to_all(parts, 'fsdp', 0, 0)]
    ppermute x9, starting transfers between devices: 53.3 us -> 63 us  [send(): self.inward.append(lax.ppermute(chunk, 'ctx', [(0, 1), (3, 2)]))]
    unnamed x101 -> x103, local copies, waits for them, and re-layouts: 30.7 us -> 35.8 us
    dot_general x5 -> x4, matrix products: 23 us -> 19 us  [dot(): lax.dot_general(left_side, right_side, (((left_dim,), (right_dim,)), ((),...]
  transfers between devices with their start and end apart: 55 -> 55, of which waited for: 24 -> 23; matrix products, arithmetic and copies ran while one was open for 11% -> 10% of each run, Pallas kernels for 24% -> 26%
where the time goes in v5:
time: 689 us; the launch traced here: 680 us
  Pallas kernels  208 us (30%)
  waiting for transfers between devices  200 us (29%)
  starting transfers between devices  139 us (20%)
  local copies, waits for them, and re-layouts  52 us (8%)
  other arithmetic  35.8 us (5%)
  matrix products  19 us (3%)
  between operations  15.1 us (2%)
  blocking collectives  10.5 us (2%)
    ppermute x9, starting transfers between devices, send(): self.inward.append(lax.ppermute(chunk, 'ctx', [(0, 1), (3, 2)]))  63 us
    ppermute x9, waiting for transfers between devices, round(): self.outward.append(lax.ppermute(self.totals[-1], 'ctx', [(1, 0), (2, 3)]))  60.3 us
    pallas_call x16, Pallas kernels, one(): pl.pallas_call(kernel, grid=(steps[0],), in_specs=[block] * 2, out_specs=...  43.6 us
    ppermute x9, waiting for transfers between devices, send(): self.inward.append(lax.ppermute(chunk, 'ctx', [(0, 1), (3, 2)]))  42.9 us
    unnamed x103, local copies, waits for them, and re-layouts  35.8 us
    pallas_call x1, Pallas kernels, feed_forward(): pl.pallas_call(kernel, grid=(steps + width // tile,), in_specs=[pl.BlockS...  33.2 us
    ppermute x3, waiting for transfers between devices, from_chip(): return lax.ppermute(own_cot, 'fsdp', [(j, j ^ chip) for j in range(shards)])  32.9 us
    all_to_all x4, starting transfers between devices, turn(): return lax.all_to_all(parts, 'fsdp', 0, 0)  30.8 us
  transfers between devices with their start and end apart: 55, of which 23 were waited for; matrix products, arithmetic and copies ran while one was open for 10% of the time, Pallas kernels for 26%

profile of v5, /device:TPU:0, one launch (start us, length us, event | category | flops | bytes accessed | tf_op | source)
XLA Modules:
  0.0 679.9 jit_solution(63961981493048084)
XLA Ops:
  9.4 10.5 %all-gather.1 = bf16[8,1,640]{2,1,0:T(2,128)(2,1)S(1)} all-gather(bf16[1,1,640]{2,1,0:T(2,128)(2,1)S(1)} %reshape.194), channel_id=2, replica_groups=mesh['fsdp'=8,'ctx'=4] {'fsdp'}, dimensions={0}, use_global_device_ids=true | all-gather | bytes 11520 | tf_op jit(solution)/shard_map/all_gather | solution.py:626
  33.1 11.9 %all-to-all-done = bf16[8,64,1152]{2,1,0:T(8,128)(2,1)S(1)} async-done(((bf16[8,64,1152]{2,1,0:T(8,128)(2,1)}), bf16[8,64,1152]{2,1,0:T(8,128)(2,1)S(1)}, u32[]{:S(2)}, u32[]{:S(2)}) %all-to-all-start) | async-done | bytes 1179680 | tf_op jit(solution)/shard_map/all_to_all | solution.py:623
  50.6 21.2 %collective-permute-done = bf16[8,64,1152]{2,1,0:T(8,128)(2,1)} collective-permute-done((bf16[8,64,1152]{2,1,0:T(8,128)(2,1)S(1)}, bf16[8,64,1152]{2,1,0:T(8,128)(2,1)}, u32[]{:S(2)}, u32[]{:S(2)}) %collective-permute-start) | collective-permute-done | bytes 1179680 | tf_op jit(solution)/shard_map/ppermute | solution.py:637
  98.3 10.3 %collective-permute-done.2.refs_2_.refs_6_ = bf16[256,512]{1,0:T(8,128)(2,1)} collective-permute-done((bf16[256,512]{1,0:T(8,128)(2,1)S(1)}, bf16[256,512]{1,0:T(8,128)(2,1)}, u32[]{:S(2)}, u32[]{:S(2)}) %collective-permute-start.2) | collective-permute-done | bytes 262176 | tf_op jit(solution)/shard_map/ppermute | solution.py:653
  118.5 12.4 %shard_map.189 = (bf16[256,1536]{1,0:T(8,128)(2,1)S(1)}, f32[12,1,256]{2,1,0:T(1,128)S(1)}) custom-call(s32[9]{0:T(128)S(1)} %pad_add_fusion.1.info_ref, bf16[256,1536]{1,0:T(8,128)(2,1)S(1)} %copy-done.16, bf16[256,512]{1,0:T(8,128)(2,1)S(1)} %get-tuple-element.161.refs_0_.refs_4_, bf16[256,512]{1,0:T(8,128)(2,1)} %collective-permute-done.1.refs_1_.refs_5_, ...), custom_call_target="tpu_custom_call" | custom-call | flops 1048576 | bytes 65536 | tf_op jit(solution)/shard_map/pallas_call | solution.py:215
  147.4 26.9 %collective-permute-done.7.refs_3_ = bf16[256,1536]{1,0:T(8,128)(2,1)} collective-permute-done((bf16[256,1536]{1,0:T(8,128)(2,1)S(1)}, bf16[256,1536]{1,0:T(8,128)(2,1)}, u32[]{:S(2)}, u32[]{:S(2)}) %collective-permute-start.7) | collective-permute-done | bytes 786464 | tf_op jit(solution)/shard_map/ppermute | solution.py:661
  192.8 8.1 %all-gather.10.cloned.1.call-done.x_ref = bf16[2048,1536]{1,0:T(8,128)(2,1)} async-done(((bf16[256,1536]{1,0:T(8,128)(2,1)}), bf16[2048,1536]{1,0:T(8,128)(2,1)}) %all-gather.10.cloned.1.call-update) | async-done | bytes 6291472 | tf_op jit(solution)/shard_map/all_gather | solution.py:674
  200.9 33.2 %shard_map.192 = (bf16[2048,1152]{1,0:T(8,128)(2,1)}, bf16[2048,1152]{1,0:T(8,128)(2,1)}, bf16[2048,1152]{1,0:T(8,128)(2,1)}, bf16[560,1536]{1,0:T(8,128)(2,1)}, bf16[560,1536]{1,0:T(8,128)(2,1)}) custom-call(bf16[2048,1536]{1,0:T(8,128)(2,1)} %all-gather.10.cloned.1.call-done.x_ref, bf16[2048,1536]{1,0:T(8,128)(2,1)} %copy-done, ...), custom_call_target="tpu_custom_call" | custom-call | flops 1048576 | bytes 65536 | tf_op jit(solution)/shard_map/pallas_call | solution.py:385
  238.7 15.0 %shard_map.193 = (bf16[2048,1152]{1,0:T(8,128)(2,1)}, bf16[2048,1152]{1,0:T(8,128)(2,1)}) custom-call(bf16[2048,1536]{1,0:T(8,128)(2,1)} %copy-done, bf16[1152,1536]{1,0:T(8,128)(2,1)} %concatenate.46.wd_ref, bf16[2048,1152]{1,0:T(8,128)(2,1)} %get-tuple-element.187.tg_ref, bf16[2048,1152]{1,0:T(8,128)(2,1)} %get-tuple-element.188.tu_ref), custom_call_target="tpu_custom_call" | custom-call | flops 1048576 | bytes 65536 | tf_op jit(solution)/shard_map/pallas_call | solution.py:414
  253.7 22.0 %shard_map.194 = bf16[2048,1536]{1,0:T(8,128)(2,1)} custom-call(bf16[2048,1152]{1,0:T(8,128)(2,1)} %get-tuple-element.199.dg_ref.g_ref, bf16[2048,1152]{1,0:T(8,128)(2,1)} %get-tuple-element.202.du_ref.g_ref, bf16[1536,1152]{1,0:T(8,128)(2,1)} %bitcast.49, bf16[1536,1152]{1,0:T(8,128)(2,1)} %bitcast.51), custom_call_target="tpu_custom_call" | custom-call | flops 1048576 | bytes 65536 | tf_op jit(solution)/shard_map/pallas_call | solution.py:440
  287.6 13.8 %shard_map.197 = bf16[1536,1152]{1,0:T(8,128)(2,1)} custom-call(bf16[2048,1536]{1,0:T(8,128)(2,1)} %all-gather.10.cloned.1.call-done.x_ref, bf16[2048,1152]{1,0:T(8,128)(2,1)} %get-tuple-element.202.du_ref.g_ref), custom_call_target="tpu_custom_call" | custom-call | flops 1048576 | bytes 65536 | tf_op jit(solution)/shard_map/pallas_call | solution.py:469
  301.4 13.6 %shard_map.196 = (bf16[768,1152]{1,0:T(8,128)(2,1)}, bf16[768,1152]{1,0:T(8,128)(2,1)}) custom-call(bf16[2048,1536]{1,0:T(8,128)(2,1)} %all-gather.10.cloned.1.call-done.x_ref, bf16[2048,1152]{1,0:T(8,128)(2,1)} %get-tuple-element.199.dg_ref.g_ref), custom_call_target="tpu_custom_call" | custom-call | flops 1048576 | bytes 65536 | tf_op jit(solution)/shard_map/pallas_call | solution.py:469
  321.9 18.7 %all-to-all-start.2 = ((bf16[8,192,1152]{2,1,0:T(8,128)(2,1)}), bf16[8,192,1152]{2,1,0:T(8,128)(2,1)}, u32[]{:S(2)}, u32[]{:S(2)}) async-start(bf16[8,192,1152]{2,1,0:T(8,128)(2,1)} %bitcast.56), calls=%async_computation.3 | async-start | bytes 7077888 | tf_op jit(solution)/shard_map/all_to_all | solution.py:623
  364.7 17.8 %shard_map.200 = (bf16[256,1536]{1,0:T(8,128)(2,1)S(1)}, bf16[4,2,256,256]{3,2,1,0:T(8,128)(2,1)}) custom-call(s32[9]{0:T(128)S(1)} %copy-done.42, bf16[256,1536]{1,0:T(8,128)(2,1)S(1)} %copy-done.17, bf16[256,1536]{1,0:T(8,128)(2,1)S(1)} %get-tuple-element.214.g_ref, f32[12,1,256]{2,1,0:T(1,128)S(1)} %copy-done.40, ...), custom_call_target="tpu_custom_call" | custom-call | flops 1048576 | bytes 65536 | tf_op jit(solution)/shard_map/pallas_call | solution.py:318
  394.0 17.4 %collective-permute-start.20 = (bf16[768,1152]{1,0:T(8,128)(2,1)}, bf16[768,1152]{1,0:T(8,128)(2,1)}, u32[]{:S(2)}, u32[]{:S(2)}) collective-permute-start(bf16[768,1152]{1,0:T(8,128)(2,1)} %get-tuple-element.229.a_ref), channel_id=1, source_target_pairs={{0,1},{3,2},{4,5},{7,6},{8,9},{11,10},{12,13},{15,14},{16,17},{19,... | collective-permute-start | bytes 5308424 | tf_op jit(solution)/shard_map/ppermute | solution.py:552
  426.4 21.3 %collective-permute-done.20.b_ref = bf16[768,1152]{1,0:T(8,128)(2,1)} collective-permute-done((bf16[768,1152]{1,0:T(8,128)(2,1)}, bf16[768,1152]{1,0:T(8,128)(2,1)}, u32[]{:S(2)}, u32[]{:S(2)}) %collective-permute-start.20) | collective-permute-done | bytes 1769504 | tf_op jit(solution)/shard_map/ppermute | solution.py:552
  458.0 7.0 %collective-permute-start.23 = (bf16[768,1152]{1,0:T(8,128)(2,1)}, bf16[768,1152]{1,0:T(8,128)(2,1)}, u32[]{:S(2)}, u32[]{:S(2)}) collective-permute-start(bf16[768,1152]{1,0:T(8,128)(2,1)} %get-tuple-element.240.a_ref), channel_id=1, source_target_pairs={{0,1},{3,2},{4,5},{7,6},{8,9},{11,10},{12,13},{15,14},{16,17},{19,... | collective-permute-start | bytes 5308424 | tf_op jit(solution)/shard_map/ppermute | solution.py:552
  484.6 14.7 %collective-permute-done.23.b_ref = bf16[768,1152]{1,0:T(8,128)(2,1)} collective-permute-done((bf16[768,1152]{1,0:T(8,128)(2,1)}, bf16[768,1152]{1,0:T(8,128)(2,1)}, u32[]{:S(2)}, u32[]{:S(2)}) %collective-permute-start.23) | collective-permute-done | bytes 1769504 | tf_op jit(solution)/shard_map/ppermute | solution.py:552
  525.4 12.8 %shard_map.207 = bf16[2048,1536]{1,0:T(8,128)(2,1)} custom-call(bf16[2048,1152]{1,0:T(8,128)(2,1)} %get-tuple-element.259.act_ref, bf16[1152,1536]{1,0:T(8,128)(2,1)} %concatenate.46.wd_ref), custom_call_target="tpu_custom_call" | custom-call | flops 1048576 | bytes 65536 | tf_op jit(solution)/shard_map/pallas_call | solution.py:488
  559.9 9.3 %collective-permute-start.32 = (bf16[192,1536]{1,0:T(8,128)(2,1)}, bf16[192,1536]{1,0:T(8,128)(2,1)}, u32[]{:S(2)}, u32[]{:S(2)}) collective-permute-start(bf16[192,1536]{1,0:T(8,128)(2,1)} %reduce-scatter.10.cloned.1.call-done.a_ref), channel_id=1, source_target_pairs={{0,1},{3,2},{4,5},{7,6},{8,9},{11,10},{12,13},{15,14},{16,17},{19,... | collective-permute-start | bytes 1769480 | tf_op jit(solution)/shard_map/ppermute | solution.py:552
  578.0 17.4 %collective-permute-done.33 = bf16[768,1152]{1,0:T(8,128)(2,1)} collective-permute-done((bf16[768,1152]{1,0:T(8,128)(2,1)}, bf16[768,1152]{1,0:T(8,128)(2,1)}, u32[]{:S(2)}, u32[]{:S(2)}) %collective-permute-start.33) | collective-permute-done | bytes 1769504 | tf_op jit(solution)/shard_map/ppermute | solution.py:572
  600.7 7.1 %collective-permute-start.35 = (bf16[192,2048]{1,0:T(8,128)(2,1)S(1)}, bf16[192,2048]{1,0:T(8,128)(2,1)S(1)}, u32[]{:S(2)}, u32[]{:S(2)}) collective-permute-start(bf16[192,2048]{1,0:T(8,128)(2,1)S(1)} %copy-done.37), channel_id=1, source_target_pairs={{0,1},{3,2},{4,5},{7,6},{8,9},{11,10},{12,13},{15,14},{16,17},{19,... | collective-permute-start | bytes 2359304 | tf_op jit(solution)/shard_map/ppermute | solution.py:552
  619.6 17.0 %collective-permute-done.37 = bf16[768,1152]{1,0:T(8,128)(2,1)S(1)} collective-permute-done((bf16[768,1152]{1,0:T(8,128)(2,1)S(1)}, bf16[768,1152]{1,0:T(8,128)(2,1)S(1)}, u32[]{:S(2)}, u32[]{:S(2)}) %collective-permute-start.37) | collective-permute-done | bytes 1769504 | tf_op jit(solution)/shard_map/ppermute | solution.py:572
  645.2 7.5 %collective-permute-done.40 = bf16[192,1536]{1,0:T(8,128)(2,1)} collective-permute-done((bf16[192,1536]{1,0:T(8,128)(2,1)}, bf16[192,1536]{1,0:T(8,128)(2,1)}, u32[]{:S(2)}, u32[]{:S(2)}) %collective-permute-start.40) | collective-permute-done | bytes 589856 | tf_op jit(solution)/shard_map/ppermute | solution.py:572
  (296 shorter events, 297.8 us)
Async XLA Ops:
  7.2 64.7 %all-gather.6.cloned.1.call-start = ((), (), s32[]{:S(2)}) async-start(), calls=%async_computation.9 | async-start | bytes 7077888 | tf_op jit(solution)/shard_map/all_gather | solution.py:625
  7.9 125.9 %all-gather.8.cloned.1.call-start = ((), (), s32[]{:S(2)}) async-start(), calls=%async_computation.10 | async-start | bytes 5308416 | tf_op jit(solution)/shard_map/all_gather | solution.py:647
  82.1 50.3 %all-to-all-start.1 = ((bf16[8,128,1152]{2,1,0:T(8,128)(2,1)}), bf16[8,128,1152]{2,1,0:T(8,128)(2,1)S(1)}, u32[]{:S(2)}, u32[]{:S(2)}) async-start(bf16[8,128,1152]{2,1,0:T(8,128)(2,1)} %copy-done.7), calls=%async_computation.1 | async-start | bytes 4718592 | tf_op jit(solution)/shard_map/all_to_all | solution.py:623
  87.0 113.9 %all-gather.10.cloned.1.call-start = ((), (), s32[]{:S(2)}) async-start(), calls=%async_computation.11 | async-start | bytes 7077888 | tf_op jit(solution)/shard_map/all_gather | solution.py:674
  145.0 210.5 %reduce-scatter.6.cloned.1.call-start = ((), (), s32[]{:S(2)}) async-start(), calls=%async_computation.12 | async-start | bytes 7077888 | tf_op jit(solution)/shard_map/reduce_scatter | solution.py:724
  146.9 39.9 %collective-permute-start.9 = (bf16[256,1536]{1,0:T(8,128)(2,1)S(1)}, bf16[256,1536]{1,0:T(8,128)(2,1)}, u32[]{:S(2)}, u32[]{:S(2)}) collective-permute-start(bf16[256,1536]{1,0:T(8,128)(2,1)S(1)} %copy-done.20), channel_id=1, source_target_pairs={{0,4},{4,0},{8,12},{12,8},{16,20},{20,16},{24,28},{28,24},{1,5},{5... | collective-permute-start | bytes 2359304 | tf_op jit(solution)/shard_map/ppermute | solution.py:681
  146.9 39.9 %collective-permute-start.10 = (bf16[256,1536]{1,0:T(8,128)(2,1)}, bf16[256,1536]{1,0:T(8,128)(2,1)}, u32[]{:S(2)}, u32[]{:S(2)}) collective-permute-start(bf16[256,1536]{1,0:T(8,128)(2,1)} %collective-permute-done.5.refs_0_), channel_id=1, source_target_pairs={{0,4},{4,0},{8,12},{12,8},{16,20},{20,16},{24,28},{28,24},{1,5},{5... | collective-permute-start | bytes 2359304 | tf_op jit(solution)/shard_map/ppermute | solution.py:681
  147.4 39.4 %collective-permute-start.11 = (bf16[256,1536]{1,0:T(8,128)(2,1)}, bf16[256,1536]{1,0:T(8,128)(2,1)}, u32[]{:S(2)}, u32[]{:S(2)}) collective-permute-start(bf16[256,1536]{1,0:T(8,128)(2,1)} %collective-permute-done.6.refs_1_), channel_id=1, source_target_pairs={{0,4},{4,0},{8,12},{12,8},{16,20},{20,16},{24,28},{28,24},{1,5},{5... | collective-permute-start | bytes 2359304 | tf_op jit(solution)/shard_map/ppermute | solution.py:681
  234.1 41.6 %collective-permute-start.13 = (bf16[560,1536]{1,0:T(8,128)(2,1)}, bf16[560,1536]{1,0:T(8,128)(2,1)}, u32[]{:S(2)}, u32[]{:S(2)}) collective-permute-start(bf16[560,1536]{1,0:T(8,128)(2,1)} %get-tuple-element.185.a_ref), channel_id=1, source_target_pairs={{0,1},{3,2},{4,5},{7,6},{8,9},{11,10},{12,13},{15,14},{16,17},{19,... | collective-permute-start | bytes 5160968 | tf_op jit(solution)/shard_map/ppermute | solution.py:552
  275.8 40.4 %collective-permute-start.15 = (bf16[560,1536]{1,0:T(8,128)(2,1)}, bf16[560,1536]{1,0:T(8,128)(2,1)}, u32[]{:S(2)}, u32[]{:S(2)}) collective-permute-start(bf16[560,1536]{1,0:T(8,128)(2,1)} %get-tuple-element.198.a_ref), channel_id=1, source_target_pairs={{0,1},{3,2},{4,5},{7,6},{8,9},{11,10},{12,13},{15,14},{16,17},{19,... | collective-permute-start | bytes 5160968 | tf_op jit(solution)/shard_map/ppermute | solution.py:552
  321.9 61.9 %all-to-all-start.2 = ((bf16[8,192,1152]{2,1,0:T(8,128)(2,1)}), bf16[8,192,1152]{2,1,0:T(8,128)(2,1)}, u32[]{:S(2)}, u32[]{:S(2)}) async-start(bf16[8,192,1152]{2,1,0:T(8,128)(2,1)} %bitcast.56), calls=%async_computation.3 | async-start | bytes 7077888 | tf_op jit(solution)/shard_map/all_to_all | solution.py:623
  340.7 126.2 %reduce-scatter.8.cloned.1.call-start = ((), (), s32[]{:S(2)}) async-start(), calls=%async_computation.13 | async-start | bytes 1310720 | tf_op jit(solution)/shard_map/reduce_scatter | solution.py:737
  340.7 43.2 %collective-permute-start.17 = (bf16[768,1152]{1,0:T(8,128)(2,1)}, bf16[768,1152]{1,0:T(8,128)(2,1)}, u32[]{:S(2)}, u32[]{:S(2)}) collective-permute-start(bf16[768,1152]{1,0:T(8,128)(2,1)} %get-tuple-element.210.a_ref), channel_id=1, source_target_pairs={{0,1},{3,2},{4,5},{7,6},{8,9},{11,10},{12,13},{15,14},{16,17},{19,... | collective-permute-start | bytes 5308424 | tf_op jit(solution)/shard_map/ppermute | solution.py:552
  352.3 41.7 %collective-permute-start.18 = (bf16[560,1536]{1,0:T(8,128)(2,1)}, bf16[560,1536]{1,0:T(8,128)(2,1)}, u32[]{:S(2)}, u32[]{:S(2)}) collective-permute-start(bf16[560,1536]{1,0:T(8,128)(2,1)} %shard_map.202), channel_id=1, source_target_pairs={{1,0},{2,3},{5,4},{6,7},{9,8},{10,11},{13,12},{14,15},{17,16},{18,... | collective-permute-start | bytes 5160968 | tf_op jit(solution)/shard_map/ppermute | solution.py:572
  353.6 40.4 %collective-permute-start.16 = (bf16[560,1536]{1,0:T(8,128)(2,1)}, bf16[560,1536]{1,0:T(8,128)(2,1)}, u32[]{:S(2)}, u32[]{:S(2)}) collective-permute-start(bf16[560,1536]{1,0:T(8,128)(2,1)} %shard_map.198.a_ref), channel_id=1, source_target_pairs={{1,2},{2,1},{5,6},{6,5},{9,10},{10,9},{13,14},{14,13},{17,18},{18,... | collective-permute-start | bytes 5160968 | tf_op jit(solution)/shard_map/ppermute | solution.py:574
  383.5 157.8 %reduce-scatter.10.cloned.1.call-start = ((), (), s32[]{:S(2)}) async-start(), calls=%async_computation.14 | async-start | bytes 5308416 | tf_op jit(solution)/shard_map/reduce_scatter | solution.py:724
  394.0 53.7 %collective-permute-start.20 = (bf16[768,1152]{1,0:T(8,128)(2,1)}, bf16[768,1152]{1,0:T(8,128)(2,1)}, u32[]{:S(2)}, u32[]{:S(2)}) collective-permute-start(bf16[768,1152]{1,0:T(8,128)(2,1)} %get-tuple-element.229.a_ref), channel_id=1, source_target_pairs={{0,1},{3,2},{4,5},{7,6},{8,9},{11,10},{12,13},{15,14},{16,17},{19,... | collective-permute-start | bytes 5308424 | tf_op jit(solution)/shard_map/ppermute | solution.py:552
  411.3 41.0 %collective-permute-start.19 = (bf16[768,1152]{1,0:T(8,128)(2,1)}, bf16[768,1152]{1,0:T(8,128)(2,1)}, u32[]{:S(2)}, u32[]{:S(2)}) collective-permute-start(bf16[768,1152]{1,0:T(8,128)(2,1)} %shard_map.201.a_ref), channel_id=1, source_target_pairs={{1,2},{2,1},{5,6},{6,5},{9,10},{10,9},{13,14},{14,13},{17,18},{18,... | collective-permute-start | bytes 5308424 | tf_op jit(solution)/shard_map/ppermute | solution.py:574
  452.4 124.2 %reduce-scatter.14.cloned.1.call-start = ((), (), s32[]{:S(2)}) async-start(), calls=%async_computation.16 | async-start | bytes 7077888 | tf_op jit(solution)/shard_map/reduce_scatter | solution.py:724
  456.6 45.9 %collective-permute-start.24 = (bf16[768,1152]{1,0:T(8,128)(2,1)}, bf16[768,1152]{1,0:T(8,128)(2,1)}, u32[]{:S(2)}, u32[]{:S(2)}) collective-permute-start(bf16[768,1152]{1,0:T(8,128)(2,1)} %shard_map.206), channel_id=1, source_target_pairs={{1,0},{2,3},{5,4},{6,7},{9,8},{10,11},{13,12},{14,15},{17,16},{18,... | collective-permute-start | bytes 5308424 | tf_op jit(solution)/shard_map/ppermute | solution.py:572
  458.0 41.3 %collective-permute-start.23 = (bf16[768,1152]{1,0:T(8,128)(2,1)}, bf16[768,1152]{1,0:T(8,128)(2,1)}, u32[]{:S(2)}, u32[]{:S(2)}) collective-permute-start(bf16[768,1152]{1,0:T(8,128)(2,1)} %get-tuple-element.240.a_ref), channel_id=1, source_target_pairs={{0,1},{3,2},{4,5},{7,6},{8,9},{11,10},{12,13},{15,14},{16,17},{19,... | collective-permute-start | bytes 5308424 | tf_op jit(solution)/shard_map/ppermute | solution.py:552
  502.5 168.2 %reduce-scatter.12.cloned.1.call-start = ((), (), s32[]{:S(2)}) async-start(), calls=%async_computation.15 | async-start | bytes 7077888 | tf_op jit(solution)/shard_map/reduce_scatter | solution.py:724
  555.0 40.3 %collective-permute-start.33 = (bf16[768,1152]{1,0:T(8,128)(2,1)}, bf16[768,1152]{1,0:T(8,128)(2,1)}, u32[]{:S(2)}, u32[]{:S(2)}) collective-permute-start(bf16[768,1152]{1,0:T(8,128)(2,1)} %shard_map.211), channel_id=1, source_target_pairs={{1,0},{2,3},{5,4},{6,7},{9,8},{10,11},{13,12},{14,15},{17,16},{18,... | collective-permute-start | bytes 5308424 | tf_op jit(solution)/shard_map/ppermute | solution.py:572
  572.9 72.3 %all-to-all-start.3 = ((bf16[8,192,1152]{2,1,0:T(8,128)(2,1)}), bf16[8,192,1152]{2,1,0:T(8,128)(2,1)S(1)}, u32[]{:S(2)}, u32[]{:S(2)}) async-start(bf16[8,192,1152]{2,1,0:T(8,128)(2,1)} %bitcast.57), calls=%async_computation.8 | async-start | bytes 7077888 | tf_op jit(solution)/shard_map/all_to_all | solution.py:623
  (82 other events, 1260.3 us)
Sparse Core Ops, SparseCore 0:
  9.9 53.7 all-gather.5
  65.6 57.7 all-gather.7
  145.1 55.7 all-gather.9
  275.9 61.1 reduce-scatter.5
  383.6 32.8 reduce-scatter.7
  452.5 55.8 reduce-scatter.9
  512.8 61.7 reduce-scatter.13
  577.9 74.9 reduce-scatter.11

commit v6 on v5

--- a/solution.py
+++ b/solution.py
@@ -448,33 +448,39 @@
     )(grad_gate, grad_up, gate_cols, up_cols)
 
 
-def column_grad(normed, grad, cuts):
+def column_grads(normed, grad_gate, grad_up, cuts):
     count, width = normed.shape
-    units = grad.shape[1]
+    units = grad_gate.shape[1]
     tile = 256
     each = width // tile // cuts
 
-    def kernel(x_ref, g_ref, *out_refs):
+    def kernel(x_ref, g_ref, u_ref, *out_refs):
         step = pl.program_id(0)
-        out = dot(x_ref[...].T, g_ref[...], 1, 0).astype(bf16)
-        for cut, out_ref in enumerate(out_refs):
+        x = x_ref[...].T
+        out = dot(x, g_ref[...], 1, 0).astype(bf16)
+        for cut, out_ref in enumerate(out_refs[:cuts]):
 
             @pl.when(step // each == cut)
             def _():
                 out_ref[...] = out
 
+        out_refs[cuts][...] = dot(x, u_ref[...], 1, 0).astype(bf16)
+
     def cut_spec(cut):
         return pl.BlockSpec((tile, units), lambda i: (jnp.clip(i - cut * each, 0, each - 1), 0))
 
-    return pl.pallas_call(
+    *gate, up = pl.pallas_call(
         kernel,
         grid=(width // tile,),
-        in_specs=[pl.BlockSpec((count, tile), lambda i: (0, i)), once((count, units))],
-        out_specs=[cut_spec(cut) for cut in range(cuts)],
-        out_shape=[jax.ShapeDtypeStruct((width // cuts, units), bf16)] * cuts,
+        in_specs=[pl.BlockSpec((count, tile), lambda i: (0, i))] + [once((count, units))] * 2,
+        out_specs=[cut_spec(cut) for cut in range(cuts)]
+        + [pl.BlockSpec((tile, units), lambda i: (i, 0))],
+        out_shape=[jax.ShapeDtypeStruct((width // cuts, units), bf16)] * cuts
+        + [jax.ShapeDtypeStruct((width, units), bf16)],
         compiler_params=kernel_params(58),
         cost_estimate=light,
-    )(normed, grad)
+    )(normed, grad_gate, grad_up)
+    return gate, up
 
 
 def through_rows(activation, down_rows, rows):
@@ -773,8 +779,7 @@
             mlp_grad, grad_gate, grad_up, activation
         )
         part_grad = to_owner(mlp_grad)
-        gate_terms = column_grad(normed_all, grad_gate, cuts)
-        (up_terms,) = column_grad(normed_all, grad_up, 1)
+        gate_terms, up_terms = column_grads(normed_all, grad_gate, grad_up, cuts)
         gate_terms, up_terms, act = line.round(gate_terms, up_terms, act)
         line.add(gate_terms)
         up_terms = to_rows(up_terms)
@@ -812,9 +817,8 @@
         up_terms = jnp.concatenate([up_sum, up_more])
     else:
         part_grad = to_owner(mlp_grad)
-        gate_terms = column_grad(normed_all, grad_gate, cuts)
-        up_terms = column_grad(normed_all, grad_up, cuts)
-        gate_terms, up_terms = (to_rows(jnp.concatenate(t)) for t in (gate_terms, up_terms))
+        gate_terms, up_terms = column_grads(normed_all, grad_gate, grad_up, cuts)
+        gate_terms, up_terms = to_rows(jnp.concatenate(gate_terms)), to_rows(up_terms)
         mlp_out = to_owner(through_rows(activation, down_rows, rows))
         grad_hidden, gain_mlp_terms, grad_branch, grad_query, kv_terms = through_attention(
             part_grad

time: 689 us -> 691 us (level)
  waiting for transfers between devices: 200 us -> 223 us
  starting transfers between devices: 139 us -> 119 us
    ppermute x9, waiting for transfers between devices: 42.9 us -> 66.7 us  [send(): self.inward.append(lax.ppermute(chunk, 'ctx', [(0, 1), (3, 2)]))]
    all_to_all x4, starting transfers between devices: 30.8 us -> 18.4 us  [turn(): return lax.all_to_all(parts, 'fsdp', 0, 0)]
    ppermute x9, starting transfers between devices: 63 us -> 54.6 us  [send(): self.inward.append(lax.ppermute(chunk, 'ctx', [(0, 1), (3, 2)]))]
    pallas_call x2 -> x1, Pallas kernels: 27.4 us -> 24.6 us  [column_grads(): pl.pallas_call(kernel, grid=(width // tile,), in_specs=[pl.BlockSpec((cou...]
  transfers between devices with their start and end apart: 55 -> 55, of which waited for: 23 -> 24; matrix products, arithmetic and copies ran while one was open for 10% -> 10% of each run, Pallas kernels for 26% -> 25%
where the time goes in v6:
time: 691 us; the launch traced here: 681 us
  waiting for transfers between devices  223 us (32%)
  Pallas kernels  206 us (30%)
  starting transfers between devices  119 us (17%)
  local copies, waits for them, and re-layouts  52.1 us (8%)
  other arithmetic  36.1 us (5%)
  matrix products  18.9 us (3%)
  between operations  15.3 us (2%)
  blocking collectives  10.5 us (2%)
    ppermute x9, waiting for transfers between devices, send(): self.inward.append(lax.ppermute(chunk, 'ctx', [(0, 1), (3, 2)]))  66.7 us
    ppermute x9, waiting for transfers between devices, round(): self.outward.append(lax.ppermute(self.totals[-1], 'ctx', [(1, 0), (2, 3)]))  55.4 us
    ppermute x9, starting transfers between devices, send(): self.inward.append(lax.ppermute(chunk, 'ctx', [(0, 1), (3, 2)]))  54.6 us
    pallas_call x16, Pallas kernels, one(): pl.pallas_call(kernel, grid=(steps[0],), in_specs=[block] * 2, out_specs=...  44.5 us
    unnamed x103, local copies, waits for them, and re-layouts  35.8 us
    pallas_call x1, Pallas kernels, feed_forward(): pl.pallas_call(kernel, grid=(steps + width // tile,), in_specs=[pl.BlockS...  33.2 us
    ppermute x3, waiting for transfers between devices, from_chip(): return lax.ppermute(own_cot, 'fsdp', [(j, j ^ chip) for j in range(shards)])  32.8 us
    pallas_call x1, Pallas kernels, column_grads(): pl.pallas_call(kernel, grid=(width // tile,), in_specs=[pl.BlockSpec((cou...  24.6 us
  transfers between devices with their start and end apart: 55, of which 24 were waited for; matrix products, arithmetic and copies ran while one was open for 10% of the time, Pallas kernels for 25%

profile of v6, /device:TPU:0, one launch (start us, length us, event | category | flops | bytes accessed | tf_op | source)
XLA Modules:
  0.0 681.1 jit_solution(17890011815158895814)
XLA Ops:
  9.4 10.5 %all-gather.1 = bf16[8,1,640]{2,1,0:T(2,128)(2,1)S(1)} all-gather(bf16[1,1,640]{2,1,0:T(2,128)(2,1)S(1)} %reshape.194), channel_id=2, replica_groups=mesh['fsdp'=8,'ctx'=4] {'fsdp'}, dimensions={0}, use_global_device_ids=true | all-gather | bytes 11520 | tf_op jit(solution)/shard_map/all_gather | solution.py:632
  33.1 11.9 %all-to-all-done = bf16[8,64,1152]{2,1,0:T(8,128)(2,1)S(1)} async-done(((bf16[8,64,1152]{2,1,0:T(8,128)(2,1)}), bf16[8,64,1152]{2,1,0:T(8,128)(2,1)S(1)}, u32[]{:S(2)}, u32[]{:S(2)}) %all-to-all-start) | async-done | bytes 1179680 | tf_op jit(solution)/shard_map/all_to_all | solution.py:629
  50.6 21.2 %collective-permute-done = bf16[8,64,1152]{2,1,0:T(8,128)(2,1)} collective-permute-done((bf16[8,64,1152]{2,1,0:T(8,128)(2,1)S(1)}, bf16[8,64,1152]{2,1,0:T(8,128)(2,1)}, u32[]{:S(2)}, u32[]{:S(2)}) %collective-permute-start) | collective-permute-done | bytes 1179680 | tf_op jit(solution)/shard_map/ppermute | solution.py:643
  91.7 6.5 collective-permute-done.1.refs_1_.refs_5_
  98.3 10.3 %collective-permute-done.2.refs_2_.refs_6_ = bf16[256,512]{1,0:T(8,128)(2,1)} collective-permute-done((bf16[256,512]{1,0:T(8,128)(2,1)S(1)}, bf16[256,512]{1,0:T(8,128)(2,1)}, u32[]{:S(2)}, u32[]{:S(2)}) %collective-permute-start.2) | collective-permute-done | bytes 262176 | tf_op jit(solution)/shard_map/ppermute | solution.py:659
  118.5 12.5 %shard_map.189 = (bf16[256,1536]{1,0:T(8,128)(2,1)S(1)}, f32[12,1,256]{2,1,0:T(1,128)S(1)}) custom-call(s32[9]{0:T(128)S(1)} %pad_add_fusion.1.info_ref, bf16[256,1536]{1,0:T(8,128)(2,1)S(1)} %copy-done.16, bf16[256,512]{1,0:T(8,128)(2,1)S(1)} %get-tuple-element.162.refs_0_.refs_4_, bf16[256,512]{1,0:T(8,128)(2,1)} %collective-permute-done.1.refs_1_.refs_5_, ...), custom_call_target="tpu_custom_call" | custom-call | flops 1048576 | bytes 65536 | tf_op jit(solution)/shard_map/pallas_call | solution.py:215
  147.4 26.9 %collective-permute-done.7.refs_3_ = bf16[256,1536]{1,0:T(8,128)(2,1)} collective-permute-done((bf16[256,1536]{1,0:T(8,128)(2,1)S(1)}, bf16[256,1536]{1,0:T(8,128)(2,1)}, u32[]{:S(2)}, u32[]{:S(2)}) %collective-permute-start.7) | collective-permute-done | bytes 786464 | tf_op jit(solution)/shard_map/ppermute | solution.py:667
  192.7 8.1 %all-gather.10.cloned.1.call-done.x_ref = bf16[2048,1536]{1,0:T(8,128)(2,1)} async-done(((bf16[256,1536]{1,0:T(8,128)(2,1)}), bf16[2048,1536]{1,0:T(8,128)(2,1)}) %all-gather.10.cloned.1.call-update) | async-done | bytes 6291472 | tf_op jit(solution)/shard_map/all_gather | solution.py:680
  200.8 33.2 %shard_map.192 = (bf16[2048,1152]{1,0:T(8,128)(2,1)}, bf16[2048,1152]{1,0:T(8,128)(2,1)}, bf16[2048,1152]{1,0:T(8,128)(2,1)}, bf16[560,1536]{1,0:T(8,128)(2,1)}, bf16[560,1536]{1,0:T(8,128)(2,1)}) custom-call(bf16[2048,1536]{1,0:T(8,128)(2,1)} %all-gather.10.cloned.1.call-done.x_ref, bf16[2048,1536]{1,0:T(8,128)(2,1)} %copy-done, ...), custom_call_target="tpu_custom_call" | custom-call | flops 1048576 | bytes 65536 | tf_op jit(solution)/shard_map/pallas_call | solution.py:385
  238.6 15.0 %shard_map.193 = (bf16[2048,1152]{1,0:T(8,128)(2,1)}, bf16[2048,1152]{1,0:T(8,128)(2,1)}) custom-call(bf16[2048,1536]{1,0:T(8,128)(2,1)} %copy-done, bf16[1152,1536]{1,0:T(8,128)(2,1)} %concatenate.46.wd_ref, bf16[2048,1152]{1,0:T(8,128)(2,1)} %get-tuple-element.188.tg_ref, bf16[2048,1152]{1,0:T(8,128)(2,1)} %get-tuple-element.189.tu_ref), custom_call_target="tpu_custom_call" | custom-call | flops 1048576 | bytes 65536 | tf_op jit(solution)/shard_map/pallas_call | solution.py:414
  253.6 22.0 %shard_map.194 = bf16[2048,1536]{1,0:T(8,128)(2,1)} custom-call(bf16[2048,1152]{1,0:T(8,128)(2,1)} %get-tuple-element.200.dg_ref.g_ref, bf16[2048,1152]{1,0:T(8,128)(2,1)} %get-tuple-element.201.du_ref.u_ref, bf16[1536,1152]{1,0:T(8,128)(2,1)} %bitcast.49, bf16[1536,1152]{1,0:T(8,128)(2,1)} %bitcast.51), custom_call_target="tpu_custom_call" | custom-call | flops 1048576 | bytes 65536 | tf_op jit(solution)/shard_map/pallas_call | solution.py:440
  287.5 24.6 %shard_map.196 = (bf16[768,1152]{1,0:T(8,128)(2,1)}, bf16[768,1152]{1,0:T(8,128)(2,1)}, bf16[1536,1152]{1,0:T(8,128)(2,1)}) custom-call(bf16[2048,1536]{1,0:T(8,128)(2,1)} %all-gather.10.cloned.1.call-done.x_ref, bf16[2048,1152]{1,0:T(8,128)(2,1)} %get-tuple-element.200.dg_ref.g_ref, bf16[2048,1152]{1,0:T(8,128)(2,1)} %get-tuple-element.201.du_ref.u_ref), custom_call_target="tpu_custom_call" | custom-call | flops 1048576 | bytes 65536 | tf_op jit(solution)/shard_map/pallas_call | solution.py:472
  352.3 17.8 %shard_map.199 = (bf16[256,1536]{1,0:T(8,128)(2,1)S(1)}, bf16[4,2,256,256]{3,2,1,0:T(8,128)(2,1)}) custom-call(s32[9]{0:T(128)S(1)} %copy-done.42, bf16[256,1536]{1,0:T(8,128)(2,1)S(1)} %copy-done.17, bf16[256,1536]{1,0:T(8,128)(2,1)S(1)} %get-tuple-element.216.g_ref, f32[12,1,256]{2,1,0:T(1,128)S(1)} %copy-done.40, ...), custom_call_target="tpu_custom_call" | custom-call | flops 1048576 | bytes 65536 | tf_op jit(solution)/shard_map/pallas_call | solution.py:318
  380.1 8.0 %collective-permute-start.20 = (bf16[768,1152]{1,0:T(8,128)(2,1)}, bf16[768,1152]{1,0:T(8,128)(2,1)}, u32[]{:S(2)}, u32[]{:S(2)}) collective-permute-start(bf16[768,1152]{1,0:T(8,128)(2,1)} %get-tuple-element.231.a_ref), channel_id=1, source_target_pairs={{0,1},{3,2},{4,5},{7,6},{8,9},{11,10},{12,13},{15,14},{16,17},{19,... | collective-permute-start | bytes 5308424 | tf_op jit(solution)/shard_map/ppermute | solution.py:558
  403.1 37.7 %collective-permute-done.20.b_ref = bf16[768,1152]{1,0:T(8,128)(2,1)} collective-permute-done((bf16[768,1152]{1,0:T(8,128)(2,1)}, bf16[768,1152]{1,0:T(8,128)(2,1)}, u32[]{:S(2)}, u32[]{:S(2)}) %collective-permute-start.20) | collective-permute-done | bytes 1769504 | tf_op jit(solution)/shard_map/ppermute | solution.py:558
  451.4 7.0 %collective-permute-start.23 = (bf16[768,1152]{1,0:T(8,128)(2,1)}, bf16[768,1152]{1,0:T(8,128)(2,1)}, u32[]{:S(2)}, u32[]{:S(2)}) collective-permute-start(bf16[768,1152]{1,0:T(8,128)(2,1)} %get-tuple-element.242.a_ref), channel_id=1, source_target_pairs={{0,1},{3,2},{4,5},{7,6},{8,9},{11,10},{12,13},{15,14},{16,17},{19,... | collective-permute-start | bytes 5308424 | tf_op jit(solution)/shard_map/ppermute | solution.py:558
  463.4 6.7 fusion.6
  477.9 16.1 %collective-permute-done.23.b_ref = bf16[768,1152]{1,0:T(8,128)(2,1)} collective-permute-done((bf16[768,1152]{1,0:T(8,128)(2,1)}, bf16[768,1152]{1,0:T(8,128)(2,1)}, u32[]{:S(2)}, u32[]{:S(2)}) %collective-permute-start.23) | collective-permute-done | bytes 1769504 | tf_op jit(solution)/shard_map/ppermute | solution.py:558
  520.6 12.4 %shard_map.206 = bf16[2048,1536]{1,0:T(8,128)(2,1)} custom-call(bf16[2048,1152]{1,0:T(8,128)(2,1)} %get-tuple-element.261.act_ref, bf16[1152,1536]{1,0:T(8,128)(2,1)} %concatenate.46.wd_ref), custom_call_target="tpu_custom_call" | custom-call | flops 1048576 | bytes 65536 | tf_op jit(solution)/shard_map/pallas_call | solution.py:494
  556.4 10.8 %collective-permute-start.32 = (bf16[192,1536]{1,0:T(8,128)(2,1)}, bf16[192,1536]{1,0:T(8,128)(2,1)}, u32[]{:S(2)}, u32[]{:S(2)}) collective-permute-start(bf16[192,1536]{1,0:T(8,128)(2,1)} %reduce-scatter.10.cloned.1.call-done.a_ref), channel_id=1, source_target_pairs={{0,1},{3,2},{4,5},{7,6},{8,9},{11,10},{12,13},{15,14},{16,17},{19,... | collective-permute-start | bytes 1769480 | tf_op jit(solution)/shard_map/ppermute | solution.py:558
  577.7 15.9 %collective-permute-done.33 = bf16[768,1152]{1,0:T(8,128)(2,1)} collective-permute-done((bf16[768,1152]{1,0:T(8,128)(2,1)}, bf16[768,1152]{1,0:T(8,128)(2,1)}, u32[]{:S(2)}, u32[]{:S(2)}) %collective-permute-start.33) | collective-permute-done | bytes 1769504 | tf_op jit(solution)/shard_map/ppermute | solution.py:578
  619.6 17.0 %collective-permute-done.37 = bf16[768,1152]{1,0:T(8,128)(2,1)S(1)} collective-permute-done((bf16[768,1152]{1,0:T(8,128)(2,1)S(1)}, bf16[768,1152]{1,0:T(8,128)(2,1)S(1)}, u32[]{:S(2)}, u32[]{:S(2)}) %collective-permute-start.37) | collective-permute-done | bytes 1769504 | tf_op jit(solution)/shard_map/ppermute | solution.py:578
  645.3 6.7 collective-permute-done.40
  661.9 7.2 %collective-permute-done.41 = f32[640]{0:T(1024)S(1)} collective-permute-done((f32[640]{0:T(1024)S(1)}, f32[640]{0:T(1024)S(1)}, u32[]{:S(2)}, u32[]{:S(2)}) %collective-permute-start.41) | collective-permute-done | bytes 2592 | tf_op jit(solution)/shard_map/ppermute | solution.py:578
  (295 shorter events, 299.6 us)
Async XLA Ops:
  7.2 64.7 %all-gather.6.cloned.1.call-start = ((), (), s32[]{:S(2)}) async-start(), calls=%async_computation.9 | async-start | bytes 7077888 | tf_op jit(solution)/shard_map/all_gather | solution.py:631
  7.9 126.0 %all-gather.8.cloned.1.call-start = ((), (), s32[]{:S(2)}) async-start(), calls=%async_computation.10 | async-start | bytes 5308416 | tf_op jit(solution)/shard_map/all_gather | solution.py:653
  82.1 50.4 %all-to-all-start.1 = ((bf16[8,128,1152]{2,1,0:T(8,128)(2,1)}), bf16[8,128,1152]{2,1,0:T(8,128)(2,1)S(1)}, u32[]{:S(2)}, u32[]{:S(2)}) async-start(bf16[8,128,1152]{2,1,0:T(8,128)(2,1)} %copy-done.7), calls=%async_computation.1 | async-start | bytes 4718592 | tf_op jit(solution)/shard_map/all_to_all | solution.py:629
  87.0 113.8 %all-gather.10.cloned.1.call-start = ((), (), s32[]{:S(2)}) async-start(), calls=%async_computation.11 | async-start | bytes 7077888 | tf_op jit(solution)/shard_map/all_gather | solution.py:680
  145.0 198.1 %reduce-scatter.6.cloned.1.call-start = ((), (), s32[]{:S(2)}) async-start(), calls=%async_computation.12 | async-start | bytes 7077888 | tf_op jit(solution)/shard_map/reduce_scatter | solution.py:730
  234.0 41.6 %collective-permute-start.13 = (bf16[560,1536]{1,0:T(8,128)(2,1)}, bf16[560,1536]{1,0:T(8,128)(2,1)}, u32[]{:S(2)}, u32[]{:S(2)}) collective-permute-start(bf16[560,1536]{1,0:T(8,128)(2,1)} %get-tuple-element.186.a_ref), channel_id=1, source_target_pairs={{0,1},{3,2},{4,5},{7,6},{8,9},{11,10},{12,13},{15,14},{16,17},{19,... | collective-permute-start | bytes 5160968 | tf_op jit(solution)/shard_map/ppermute | solution.py:558
  275.7 40.4 %collective-permute-start.15 = (bf16[560,1536]{1,0:T(8,128)(2,1)}, bf16[560,1536]{1,0:T(8,128)(2,1)}, u32[]{:S(2)}, u32[]{:S(2)}) collective-permute-start(bf16[560,1536]{1,0:T(8,128)(2,1)} %get-tuple-element.199.a_ref), channel_id=1, source_target_pairs={{0,1},{3,2},{4,5},{7,6},{8,9},{11,10},{12,13},{15,14},{16,17},{19,... | collective-permute-start | bytes 5160968 | tf_op jit(solution)/shard_map/ppermute | solution.py:558
  321.9 52.7 %all-to-all-start.2 = ((bf16[8,192,1152]{2,1,0:T(8,128)(2,1)}), bf16[8,192,1152]{2,1,0:T(8,128)(2,1)}, u32[]{:S(2)}, u32[]{:S(2)}) async-start(bf16[8,192,1152]{2,1,0:T(8,128)(2,1)} %bitcast.57), calls=%async_computation.3 | async-start | bytes 7077888 | tf_op jit(solution)/shard_map/all_to_all | solution.py:629
  326.4 133.8 %reduce-scatter.8.cloned.1.call-start = ((), (), s32[]{:S(2)}) async-start(), calls=%async_computation.13 | async-start | bytes 1310720 | tf_op jit(solution)/shard_map/reduce_scatter | solution.py:743
  326.5 44.6 %collective-permute-start.17 = (bf16[768,1152]{1,0:T(8,128)(2,1)}, bf16[768,1152]{1,0:T(8,128)(2,1)}, u32[]{:S(2)}, u32[]{:S(2)}) collective-permute-start(bf16[768,1152]{1,0:T(8,128)(2,1)} %get-tuple-element.212.a_ref), channel_id=1, source_target_pairs={{0,1},{3,2},{4,5},{7,6},{8,9},{11,10},{12,13},{15,14},{16,17},{19,... | collective-permute-start | bytes 5308424 | tf_op jit(solution)/shard_map/ppermute | solution.py:558
  338.4 41.7 %collective-permute-start.18 = (bf16[560,1536]{1,0:T(8,128)(2,1)}, bf16[560,1536]{1,0:T(8,128)(2,1)}, u32[]{:S(2)}, u32[]{:S(2)}) collective-permute-start(bf16[560,1536]{1,0:T(8,128)(2,1)} %shard_map.201), channel_id=1, source_target_pairs={{1,0},{2,3},{5,4},{6,7},{9,8},{10,11},{13,12},{14,15},{17,16},{18,... | collective-permute-start | bytes 5160968 | tf_op jit(solution)/shard_map/ppermute | solution.py:578
  339.7 40.4 %collective-permute-start.16 = (bf16[560,1536]{1,0:T(8,128)(2,1)}, bf16[560,1536]{1,0:T(8,128)(2,1)}, u32[]{:S(2)}, u32[]{:S(2)}) collective-permute-start(bf16[560,1536]{1,0:T(8,128)(2,1)} %shard_map.197.a_ref), channel_id=1, source_target_pairs={{1,2},{2,1},{5,6},{6,5},{9,10},{10,9},{13,14},{14,13},{17,18},{18,... | collective-permute-start | bytes 5160968 | tf_op jit(solution)/shard_map/ppermute | solution.py:580
  371.1 166.3 %reduce-scatter.10.cloned.1.call-start = ((), (), s32[]{:S(2)}) async-start(), calls=%async_computation.14 | async-start | bytes 5308416 | tf_op jit(solution)/shard_map/reduce_scatter | solution.py:730
  380.1 60.8 %collective-permute-start.20 = (bf16[768,1152]{1,0:T(8,128)(2,1)}, bf16[768,1152]{1,0:T(8,128)(2,1)}, u32[]{:S(2)}, u32[]{:S(2)}) collective-permute-start(bf16[768,1152]{1,0:T(8,128)(2,1)} %get-tuple-element.231.a_ref), channel_id=1, source_target_pairs={{0,1},{3,2},{4,5},{7,6},{8,9},{11,10},{12,13},{15,14},{16,17},{19,... | collective-permute-start | bytes 5308424 | tf_op jit(solution)/shard_map/ppermute | solution.py:558
  388.0 57.8 %collective-permute-start.19 = (bf16[768,1152]{1,0:T(8,128)(2,1)}, bf16[768,1152]{1,0:T(8,128)(2,1)}, u32[]{:S(2)}, u32[]{:S(2)}) collective-permute-start(bf16[768,1152]{1,0:T(8,128)(2,1)} %shard_map.200.a_ref), channel_id=1, source_target_pairs={{1,2},{2,1},{5,6},{6,5},{9,10},{10,9},{13,14},{14,13},{17,18},{18,... | collective-permute-start | bytes 5308424 | tf_op jit(solution)/shard_map/ppermute | solution.py:580
  394.6 51.2 %collective-permute-start.21 = (bf16[560,1536]{1,0:T(8,128)(2,1)}, bf16[560,1536]{1,0:T(8,128)(2,1)}, u32[]{:S(2)}, u32[]{:S(2)}) collective-permute-start(bf16[560,1536]{1,0:T(8,128)(2,1)} %shard_map.203), channel_id=1, source_target_pairs={{1,0},{2,3},{5,4},{6,7},{9,8},{10,11},{13,12},{14,15},{17,16},{18,... | collective-permute-start | bytes 5160968 | tf_op jit(solution)/shard_map/ppermute | solution.py:578
  445.8 130.6 %reduce-scatter.14.cloned.1.call-start = ((), (), s32[]{:S(2)}) async-start(), calls=%async_computation.16 | async-start | bytes 7077888 | tf_op jit(solution)/shard_map/reduce_scatter | solution.py:730
  450.0 47.2 %collective-permute-start.24 = (bf16[768,1152]{1,0:T(8,128)(2,1)}, bf16[768,1152]{1,0:T(8,128)(2,1)}, u32[]{:S(2)}, u32[]{:S(2)}) collective-permute-start(bf16[768,1152]{1,0:T(8,128)(2,1)} %shard_map.205), channel_id=1, source_target_pairs={{1,0},{2,3},{5,4},{6,7},{9,8},{10,11},{13,12},{14,15},{17,16},{18,... | collective-permute-start | bytes 5308424 | tf_op jit(solution)/shard_map/ppermute | solution.py:578
  451.4 42.7 %collective-permute-start.23 = (bf16[768,1152]{1,0:T(8,128)(2,1)}, bf16[768,1152]{1,0:T(8,128)(2,1)}, u32[]{:S(2)}, u32[]{:S(2)}) collective-permute-start(bf16[768,1152]{1,0:T(8,128)(2,1)} %get-tuple-element.242.a_ref), channel_id=1, source_target_pairs={{0,1},{3,2},{4,5},{7,6},{8,9},{11,10},{12,13},{15,14},{16,17},{19,... | collective-permute-start | bytes 5308424 | tf_op jit(solution)/shard_map/ppermute | solution.py:558
  497.2 174.4 %reduce-scatter.12.cloned.1.call-start = ((), (), s32[]{:S(2)}) async-start(), calls=%async_computation.15 | async-start | bytes 7077888 | tf_op jit(solution)/shard_map/reduce_scatter | solution.py:730
  497.3 40.1 %collective-permute-start.26 = (bf16[768,1152]{1,0:T(8,128)(2,1)S(1)}, bf16[768,1152]{1,0:T(8,128)(2,1)}, u32[]{:S(2)}, u32[]{:S(2)}) collective-permute-start(bf16[768,1152]{1,0:T(8,128)(2,1)S(1)} %get-tuple-element.257.a_ref), channel_id=1, source_target_pairs={{0,1},{3,2},{4,5},{7,6},{8,9},{11,10},{12,13},{15,14},{16,17},{19,... | collective-permute-start | bytes 5308424 | tf_op jit(solution)/shard_map/ppermute | solution.py:558
  551.3 42.3 %collective-permute-start.33 = (bf16[768,1152]{1,0:T(8,128)(2,1)}, bf16[768,1152]{1,0:T(8,128)(2,1)}, u32[]{:S(2)}, u32[]{:S(2)}) collective-permute-start(bf16[768,1152]{1,0:T(8,128)(2,1)} %shard_map.210), channel_id=1, source_target_pairs={{1,0},{2,3},{5,4},{6,7},{9,8},{10,11},{13,12},{14,15},{17,16},{18,... | collective-permute-start | bytes 5308424 | tf_op jit(solution)/shard_map/ppermute | solution.py:578
  552.6 41.0 %collective-permute-start.31 = (bf16[768,1152]{1,0:T(8,128)(2,1)}, bf16[768,1152]{1,0:T(8,128)(2,1)}, u32[]{:S(2)}, u32[]{:S(2)}) collective-permute-start(bf16[768,1152]{1,0:T(8,128)(2,1)} %shard_map.207.a_ref), channel_id=1, source_target_pairs={{1,2},{2,1},{5,6},{6,5},{9,10},{10,9},{13,14},{14,13},{17,18},{18,... | collective-permute-start | bytes 5308424 | tf_op jit(solution)/shard_map/ppermute | solution.py:580
  571.0 74.3 %all-to-all-start.3 = ((bf16[8,192,1152]{2,1,0:T(8,128)(2,1)}), bf16[8,192,1152]{2,1,0:T(8,128)(2,1)S(1)}, u32[]{:S(2)}, u32[]{:S(2)}) async-start(bf16[8,192,1152]{2,1,0:T(8,128)(2,1)} %bitcast.56), calls=%async_computation.8 | async-start | bytes 7077888 | tf_op jit(solution)/shard_map/all_to_all | solution.py:629
  (82 other events, 1252.1 us)
Sparse Core Ops, SparseCore 0:
  9.9 53.7 all-gather.5
  65.6 57.7 all-gather.7
  145.1 55.6 all-gather.9
  275.8 67.2 reduce-scatter.5
  371.2 53.6 reduce-scatter.7
  445.9 54.7 reduce-scatter.9
  505.0 61.7 reduce-scatter.13
  570.2 80.8 reduce-scatter.11
